TPU v7x, 32 devices: a whole 2x2x4 slice. The times are simulated.
32 devices in a mesh: pipe: 4 (over z), ctx: 2 (over x), tp: 4 (over y, core).
Axes of the slice: x: 2, y: 2, z: 4, core: 2. Of those that a mesh axis runs over, the one named last changes fastest.
Arguments:
- inputs: bfloat16 [4, 512, 5120], P('pipe', ('ctx', 'tp')), may hold values from -6 to 6
- doc_lengths: int32 [4, 8], P('pipe'), may hold values from 1 to 256, 512 in all within a row
- w_query: bfloat16 [4, 5120, 3072], P('pipe', None, 'tp'), may hold values from -0.078125 to 0.078125
- w_key: bfloat16 [4, 5120, 1024], P('pipe', 'ctx', 'tp'), may hold values from -0.078125 to 0.078125
- w_value: bfloat16 [4, 5120, 1024], P('pipe', 'ctx', 'tp'), may hold values from -0.078125 to 0.078125
- w_out: bfloat16 [4, 3072, 5120], P('pipe', 'tp'), may hold values from -0.625 to 0.625
Outputs:
- next_input: bfloat16 [4, 512, 5120], P('pipe', ('ctx', 'tp'))
Inputs may be any that keep to these rules, and one draw needn't show every extreme that they name: `doc_lengths`: the 8 lengths of a micro-batch sum to 512; the longest is exactly 256.
All inputs are finite; a program needn't handle non-finite values.
Results may differ from a plain program's by a relative error of at most 0.015.
Values may be sent and summed in bfloat16 or wider, within the bound.
No kernel may reach another device: no remote copies, remote signals or barrier semaphores. Data moves between devices by JAX's collectives and lax.ppermute only.
A program may use at most 64 MiB of HBM per device.

v0:
```python
import jax
import jax.numpy as jnp
from jax import lax
from jax.sharding import PartitionSpec as P

HD = 128
SPAN = 1024


ROPE_BASE = 500000.0
NORM_EPS = 1e-06


def from_behind(value, axis, steps):
    count = lax.axis_size(axis)
    pairs = [(source, (source + steps) % count) for source in range(count)]
    return lax.ppermute(value, axis, pairs)


def doc_index(positions, lengths):
    doc_ends = jnp.cumsum(lengths)
    return jnp.sum((positions[:, None] >= doc_ends[None, :]).astype(jnp.int32), axis=1)


def norm_rotate(entries, positions, head_count, head_width):
    row_count = entries.shape[0]
    shaped = entries.reshape(row_count, head_count, head_width)
    shaped = shaped * lax.rsqrt(jnp.mean(shaped * shaped, axis=-1, keepdims=True) + NORM_EPS)
    half_width = head_width // 2
    frequencies = jnp.power(
        ROPE_BASE, -(jnp.arange(half_width, dtype=jnp.float32) * 2.0 / head_width)
    )
    angles = positions.astype(jnp.float32)[:, None] * frequencies[None, :]
    cosine = jnp.cos(angles)[:, None, :]
    sine_part = jnp.sin(angles)[:, None, :]
    first_half = shaped[..., :half_width]
    second = shaped[..., half_width:]
    turned = jnp.concatenate(
        [first_half * cosine - second * sine_part, second * cosine + first_half * sine_part],
        axis=-1,
    )
    return turned.reshape(row_count, head_count * head_width)


def attend(queries, q_pos, q_doc, key_rows, value_rows, k_pos, k_doc):
    score_scale = 1.0 / HD**0.5
    scores = (
        jnp.einsum("tkgd,nkd->kgtn", queries, key_rows, preferred_element_type=jnp.float32)
        * score_scale
    )
    allowed = (
        (k_pos[None, :] <= q_pos[:, None])
        & (k_doc[None, :] == q_doc[:, None])
        & (k_pos[None, :] // SPAN == q_pos[:, None] // SPAN)
    )
    weights = jnp.where(allowed[None, None], jnp.exp(scores), 0.0).astype(jnp.bfloat16)
    numerator = jnp.einsum(
        "kgtn,nkd->tkgd", weights, value_rows, preferred_element_type=jnp.float32
    )
    denominator = jnp.sum(weights.astype(jnp.float32), axis=-1)
    return (numerator, denominator)


def on_device(inputs, doc_lengths, w_query, w_key, w_value, w_out):
    tok_rows = lax.all_gather(inputs[0], "tp", axis=0, tiled=True)
    block_rows = tok_rows.shape[0]
    q_heads = w_query.shape[2] // HD
    kv_heads = w_key.shape[2] // HD
    group_size = q_heads // kv_heads
    ctx_rank = lax.axis_index("ctx")
    positions = ctx_rank * block_rows + jnp.arange(block_rows, dtype=jnp.int32)
    lengths = doc_lengths[0]
    own_docs = doc_index(positions, lengths)
    queries = jnp.dot(tok_rows, w_query[0], preferred_element_type=jnp.float32)
    stacked_weights = jnp.stack([w_key[0], w_value[0]])
    key_value = jnp.einsum(
        "td,sdc->stc",
        tok_rows,
        lax.all_gather(stacked_weights, "ctx", axis=1, tiled=True),
        preferred_element_type=jnp.float32,
    )
    keys_float = key_value[0]
    values_float = key_value[1]
    q_round = (
        norm_rotate(queries, positions, q_heads, HD)
        .astype(jnp.bfloat16)
        .reshape(block_rows, kv_heads, group_size, HD)
    )
    k_round = norm_rotate(keys_float, positions, kv_heads, HD).astype(jnp.bfloat16)
    v_round = values_float.astype(jnp.bfloat16)
    key_value_pair = jnp.stack([k_round, v_round])
    shard_piece = lax.all_gather(key_value_pair, "ctx", axis=1, tiled=True)
    row_count = shard_piece.shape[1]
    k_pos = jnp.arange(row_count, dtype=jnp.int32)
    k_doc = doc_index(k_pos, lengths)
    key_rows = shard_piece[0].reshape(row_count, kv_heads, HD)
    value_rows = shard_piece[1].reshape(row_count, kv_heads, HD)
    numerator, denominator = attend(
        q_round, positions, own_docs, key_rows, value_rows, k_pos, k_doc
    )
    attended = (
        (numerator / jnp.transpose(denominator, (2, 0, 1))[..., None])
        .astype(jnp.bfloat16)
        .reshape(block_rows, q_heads * HD)
    )
    mixed = lax.psum_scatter(
        jnp.dot(attended, w_out[0], preferred_element_type=jnp.float32).astype(jnp.bfloat16),
        "tp",
        scatter_dimension=0,
        tiled=True,
    )
    received = from_behind(mixed, "pipe", 1)
    return received[None]


def solution(mesh):
    in_specs = (
        P("pipe", ("ctx", "tp"), None),
        P("pipe", None),
        P("pipe", None, "tp"),
        P("pipe", "ctx", "tp"),
        P("pipe", "ctx", "tp"),
        P("pipe", "tp", None),
    )
    out_specs = P("pipe", ("ctx", "tp"), None)
    return jax.shard_map(
        on_device, mesh=mesh, in_specs=in_specs, out_specs=out_specs, check_vma=False
    )
```

profile of v0, /device:TPU:0, one launch (start us, length us, event | category | flops | bytes accessed | tf_op | source)
XLA Modules:
  0.0 186.5 jit_solution(15654423579638632060)
XLA Ops:
  6.5 0.0 all-gather.6.cloned.1.call-start
  6.5 0.7 all-gather.6.cloned.1.call-update
  7.3 0.0 all-gather.4.cloned.1.call-start
  7.3 1.6 copy.20
  8.9 1.6 copy.19
  10.5 1.7 pad_maximum_fusion
  12.2 0.0 all-gather.4.cloned.1.call-update
  12.3 0.0 reduce-scatter.2.cloned.1.call-start
  12.3 0.0 copy-start.1
  12.3 10.7 %copy.21 = bf16[1,5120,768]{1,2,0:T(8,128)(2,1)} copy(bf16[1,5120,768]{2,1,0:T(8,128)(2,1)} %param.8) | data formatting | bytes 15728640 | tf_op args[2]
  23.0 0.0 copy-done.1
  23.0 0.2 reduce-window.8
  23.3 0.1 convert_reduce_fusion.1
  23.4 0.1 convert_reduce_fusion.2
  23.4 0.3 multiply_cosine_fusion
  23.8 0.2 fusion.16
  24.0 13.2 %all-gather.6.cloned.1.call-done = bf16[1,256,5120]{2,1,0:T(8,128)(2,1)} async-done(((bf16[1,64,5120]{2,1,0:T(8,128)(2,1)}), bf16[1,256,5120]{2,1,0:T(8,128)(2,1)}) %all-gather.6.cloned.1.call-update) | async-done | bytes 2621456 | tf_op jit(solution)/shard_map/all_gather | solution.py:65
  37.2 6.3 %multiply_reduce_fusion = (f32[256,6]{0,1:T(8,128)S(1)}, f32[256,6,128]{0,2,1:T(8,128)S(1)}) fusion(bf16[6,128,5120]{2,1,0:T(8,128)(2,1)} %bitcast.59, bf16[1,256,5120]{2,1,0:T(8,128)(2,1)} %all-gather.6.cloned.1.call-done), kind=kOutput, calls=%fused_computation.15 | convolution fusion | flops 2013657600 | bytes 11278336 | tf_op jit(solution)/shard_map/dot_general | solution.py:74
  43.5 0.0 copy-start
  43.5 0.1 broadcast_multiply_fusion
  43.6 0.1 subtract_convert_fusion
  43.7 63.6 %all-gather.4.cloned.1.call-done = bf16[2,5120,256]{1,2,0:T(8,128)(2,1)} async-done(((bf16[2,2560,256]{1,2,0:T(8,128)(2,1)}), bf16[2,5120,256]{1,2,0:T(8,128)(2,1)}) %all-gather.4.cloned.1.call-update) | async-done | bytes 5242896 | tf_op jit(solution)/shard_map/all_gather | solution.py:79
  107.3 0.0 copy-done
  107.3 0.0 slice-start
  107.3 4.2 %fusion.12 = f32[2,256,256]{1,2,0:T(8,128)S(1)} fusion(bf16[2,5120,256]{1,2,0:T(8,128)(2,1)} %all-gather.4.cloned.1.call-done, bf16[1,256,5120]{2,1,0:T(8,128)(2,1)S(1)} %copy-done), kind=kOutput, calls=%fused_computation.14 | convolution fusion | flops 1342177280 | bytes 8388608 | tf_op jit(solution)/shard_map/td,sdc->stc/dot_general | solution.py:76
  111.7 0.0 slice-start.1
  111.8 8.8 %all_gather.11 = bf16[2,512,256]{1,2,0:T(8,128)(2,1)S(1)} all-gather(bf16[2,256,256]{1,2,0:T(8,128)(2,1)S(1)} %pad_maximum_fusion.2), channel_id=1, replica_groups=mesh['pipe'=4,'ctx'=2,'tp'=4] {'ctx'}, dimensions={1}, use_global_device_ids=true | all-gather | bytes 786432 | tf_op jit(solution)/shard_map/all_gather | solution.py:92
  120.7 0.9 convert_reduce_fusion
  121.6 0.4 fusion.11
  122.0 0.0 slice-done
  122.0 0.0 slice-done.1
  122.0 3.7 %fusion.2 = bf16[256,5120]{1,0:T(8,128)(2,1)} fusion(bf16[256,768]{0,1:T(8,128)(2,1)S(1)} %bitcast.62, bf16[1,768,5120]{2,1,0:T(8,128)(2,1)S(1)} %bitcast.58), kind=kOutput, calls=%fused_computation.2 | convolution fusion | flops 2014576640 | bytes 10878976 | tf_op jit(solution)/shard_map/dot_general | solution.py:107
  125.8 0.0 reduce-scatter.2.cloned.1.call-update
  125.8 34.8 %reduce-scatter.2.cloned.1.call-done = bf16[64,5120]{1,0:T(8,128)(2,1)} async-done(((bf16[256,5120]{1,0:T(8,128)(2,1)}), bf16[64,5120]{1,0:T(8,128)(2,1)}) %reduce-scatter.2.cloned.1.call-update) | async-done | bytes 655376 | tf_op jit(solution)/shard_map/reduce_scatter | solution.py:106
  160.6 1.5 collective-permute-start
  162.1 17.0 %collective-permute-done = bf16[64,5120]{1,0:T(8,128)(2,1)S(1)} collective-permute-done((bf16[64,5120]{1,0:T(8,128)(2,1)}, bf16[64,5120]{1,0:T(8,128)(2,1)S(1)}, u32[]{:S(2)}, u32[]{:S(2)}) %collective-permute-start) | collective-permute-done | bytes 655392 | tf_op jit(solution)/shard_map/ppermute | solution.py:17
  179.1 0.8 copy.32
  (16 shorter events, 0.3 us)
Async XLA Ops:
  6.5 30.7 %all-gather.6.cloned.1.call-start = ((), (), s32[]{:S(2)}) async-start(), calls=%async_computation.3 | async-start | bytes 3276800 | tf_op jit(solution)/shard_map/all_gather | solution.py:65
  7.3 100.1 %all-gather.4.cloned.1.call-start = ((), (), s32[]{:S(2)}) async-start(), calls=%async_computation.1 | async-start | bytes 7864320 | tf_op jit(solution)/shard_map/all_gather | solution.py:79
  12.3 148.4 %reduce-scatter.2.cloned.1.call-start = ((), (), s32[]{:S(2)}) async-start(), calls=%async_computation.2 | async-start | bytes 3276800 | tf_op jit(solution)/shard_map/reduce_scatter | solution.py:106
  12.3 10.7 %copy-start.1 = (s32[1,8]{1,0:T(1,128)S(1)}, s32[1,8]{1,0:T(1,128)}, u32[]{:S(2)}) copy-start(s32[1,8]{1,0:T(1,128)} %param.7) | copy-start | bytes 100
  43.5 63.9 %copy-start = (bf16[1,256,5120]{2,1,0:T(8,128)(2,1)S(1)}, bf16[1,256,5120]{2,1,0:T(8,128)(2,1)}, u32[]{:S(2)}) copy-start(bf16[1,256,5120]{2,1,0:T(8,128)(2,1)} %all-gather.6.cloned.1.call-done) | copy-start | bytes 7864324
  107.3 14.7 %slice-start = ((s8[7864320]{0:T(1024)(128)(4,1)}), s8[4194304]{0:T(1024)(128)(4,1)S(1)}, s32[]{:S(2)}) async-start(s8[7864320]{0:T(1024)(128)(4,1)} %bitcast.57), calls=%async_computation.4 | async-start | bytes 8388608
  111.7 10.3 %slice-start.1 = ((s8[7864320]{0:T(1024)(128)(4,1)}), s8[3670016]{0:T(1024)(128)(4,1)S(1)}, s32[]{:S(2)}) async-start(s8[7864320]{0:T(1024)(128)(4,1)} %bitcast.57), calls=%async_computation.5 | async-start | bytes 7340032
  160.6 18.5 %collective-permute-start = (bf16[64,5120]{1,0:T(8,128)(2,1)}, bf16[64,5120]{1,0:T(8,128)(2,1)S(1)}, u32[]{:S(2)}, u32[]{:S(2)}) collective-permute-start(bf16[64,5120]{1,0:T(8,128)(2,1)} %reduce-scatter.2.cloned.1.call-done), channel_id=1, source_target_pairs={{0,8},{8,16},{16,24},{24,0},{1,9},{9,17},{17,25},{25,1},{2,10},{10... | collective-permute-start | bytes 1966088 | tf_op jit(solution)/shard_map/ppermute | solution.py:17
Sparse Core Ops, SparseCore 0:
  8.9 28.2 all-gather.5
  38.7 68.5 all-gather.3
  125.9 34.6 reduce-scatter.1
where the time goes:
time: 187 us; the launch traced here: 186 us
  waiting for transfers between devices  129 us (69%)
  matrix products  15.5 us (8%)
  local copies, waits for them, and re-layouts  14.8 us (8%)
  between operations  13.3 us (7%)
  blocking collectives  8.85 us (5%)
  other arithmetic  2.97 us (2%)
    all_gather x1, waiting for transfers between devices, on_device(): lax.all_gather(stacked_weights, 'ctx', axis=1, tiled=True)  63.6 us
    reduce_scatter x1, waiting for transfers between devices, on_device(): lax.psum_scatter(jnp.dot(attended, w_out[0], preferred_element_type=jnp.f...  34.8 us
    ppermute x1, waiting for transfers between devices, from_behind(): return lax.ppermute(value, axis, pairs)  17 us
    unnamed x12, local copies, waits for them, and re-layouts  14.8 us
    all_gather x1, waiting for transfers between devices, on_device(): tok_rows = lax.all_gather(inputs[0], 'tp', axis=0, tiled=True)  13.2 us
    all_gather x1, blocking collectives, on_device(): shard_piece = lax.all_gather(key_value_pair, 'ctx', axis=1, tiled=True)  8.85 us
    dot_general x1, matrix products, on_device(): queries = jnp.dot(tok_rows, w_query[0], preferred_element_type=jnp.float32)  6.27 us
    dot_general x1, matrix products, on_device(): jnp.einsum('td,sdc->stc', tok_rows, lax.all_gather(stacked_weights, 'ctx'...  4.19 us
  transfers between devices with their start and end apart: 4, of which 4 were waited for; matrix products, arithmetic and copies ran while one was open for 12% of the time, Pallas kernels for 0%

commit v1 on v0

--- a/solution.py
+++ b/solution.py
@@ -1,20 +1,314 @@
+import functools
+
 import jax
 import jax.numpy as jnp
 from jax import lax
+from jax.experimental import pallas as pl
+from jax.experimental.pallas import tpu as pltpu
 from jax.sharding import PartitionSpec as P
 
 HD = 128
 SPAN = 1024
-
-
 ROPE_BASE = 500000.0
 NORM_EPS = 1e-06
+OUT_CHUNKS = 4
+MIB = 1 << 20
 
 
 def from_behind(value, axis, steps):
     count = lax.axis_size(axis)
     pairs = [(source, (source + steps) % count) for source in range(count)]
     return lax.ppermute(value, axis, pairs)
+
+
+def swap(value, axis, bit):
+    count = lax.axis_size(axis)
+    return lax.ppermute(value, axis, [(source, source ^ bit) for source in range(count)])
+
+
+def rope_tables(positions):
+    half_width = HD // 2
+    frequencies = jnp.power(ROPE_BASE, -(jnp.arange(half_width, dtype=jnp.float32) * 2.0 / HD))
+    angles = positions.astype(jnp.float32)[:, None] * frequencies[None, :]
+    cosine, sine = jnp.cos(angles), jnp.sin(angles)
+    return jnp.concatenate([cosine, cosine], 1), jnp.concatenate([-sine, sine], 1)
+
+
+def norm_rotate_head(head, cosine, sine):
+    head = head * lax.rsqrt(jnp.mean(head * head, axis=-1, keepdims=True) + NORM_EPS)
+    return head * cosine + pltpu.roll(head, HD // 2, 1) * sine
+
+
+def call(kernel, out_shape, mib, flops, moved, **given):
+    return pl.pallas_call(
+        kernel,
+        out_shape=out_shape,
+        compiler_params=pltpu.CompilerParams(vmem_limit_bytes=mib * MIB),
+        cost_estimate=pl.CostEstimate(flops=flops, bytes_accessed=moved, transcendentals=0),
+        **given,
+    )
+
+
+def shape(rows, columns, dtype):
+    return jax.ShapeDtypeStruct((rows, columns), dtype)
+
+
+def project_kernel(x_count, w_count, widths, *refs):
+    xs, ws = refs[:x_count], refs[x_count : x_count + w_count]
+    outs, acc = refs[x_count + w_count : -1], refs[-1]
+    step = pl.program_id(0)
+
+    @pl.when(step == 0)
+    def _():
+        acc[...] = jnp.zeros_like(acc)
+
+    rows = jnp.concatenate([x[...] for x in xs], axis=0) if x_count > 1 else xs[0][...]
+    at = 0
+    for w in ws:
+        wide = w.shape[1]
+        acc[:, at : at + wide] += jnp.dot(rows, w[...], preferred_element_type=jnp.float32)
+        at += wide
+
+    @pl.when(step == pl.num_programs(0) - 1)
+    def _():
+        for out, (first, last) in zip(outs, widths):
+            out[...] = acc[first:last, :].astype(out.dtype)
+
+
+def project_kv(xs, ws, outs):
+    rows, depth = xs[0].shape
+    block = 512
+    wide = sum(w.shape[1] for w in ws)
+    count = len(xs)
+    return call(
+        functools.partial(project_kernel, count, len(ws), [(a, b) for a, b, _ in outs]),
+        [shape(b - a, wide, dtype) for a, b, dtype in outs],
+        16,
+        2 * count * rows * depth * wide,
+        2 * depth * wide + 2 * count * rows * depth,
+        grid=(depth // block,),
+        in_specs=[pl.BlockSpec((rows, block), lambda i: (0, i))] * count
+        + [pl.BlockSpec((block, w.shape[1]), lambda i: (i, 0)) for w in ws],
+        out_specs=[pl.BlockSpec((b - a, wide), lambda i: (0, 0)) for a, b, _ in outs],
+        scratch_shapes=[pltpu.VMEM((count * rows, wide), jnp.float32)],
+    )(*xs, *ws)
+
+
+def query_first_kernel(half_ref, x0, x1, w0, w1, out):
+    @pl.when(pl.program_id(0) == 0)
+    def _():
+        out[...] = jnp.zeros_like(out)
+
+    rows = jnp.concatenate([x0[...], x1[...]], axis=0)
+    wide = w0.shape[1]
+    out[:, :wide] += jnp.dot(rows, w0[...], preferred_element_type=jnp.float32)
+    out[:, wide:] += jnp.dot(rows, w1[...], preferred_element_type=jnp.float32)
+
+
+def query_last_kernel(half_ref, x0, x1, w0, w1, before, cosine, sine, out, acc):
+    @pl.when(pl.program_id(0) == 0)
+    def _():
+        acc[...] = before[...]
+
+    rows = jnp.concatenate([x0[...], x1[...]], axis=0)
+    wide = w0.shape[1]
+    acc[:, :wide] += jnp.dot(rows, w0[...], preferred_element_type=jnp.float32)
+    acc[:, wide:] += jnp.dot(rows, w1[...], preferred_element_type=jnp.float32)
+
+    @pl.when(pl.program_id(0) == pl.num_programs(0) - 1)
+    def _():
+        for at in range(0, acc.shape[1], HD):
+            turned = norm_rotate_head(acc[:, at : at + HD], cosine[...], sine[...])
+            out[:, at : at + HD] = turned.astype(out.dtype)
+
+
+def project_query(half, x0, x1, w0, w1, before=None, tables=None):
+    rows, depth = x0.shape
+    wide = w0.shape[1]
+    block = 512
+    steps = depth // block
+    in_specs = [
+        pl.BlockSpec((rows, block), lambda i, h: (0, i)),
+        pl.BlockSpec((rows, block), lambda i, h: (0, i)),
+        pl.BlockSpec((block, wide), lambda i, h: (h[0] * steps + i, 0)),
+        pl.BlockSpec((block, wide), lambda i, h: (h[0] * steps + i, 0)),
+    ]
+    arguments = [half, x0, x1, w0, w1]
+    whole = lambda *dims: pl.BlockSpec(dims, lambda i, h: (0, 0))
+    if before is None:
+        kernel, dtype, scratch = query_first_kernel, jnp.float32, []
+    else:
+        kernel, dtype = query_last_kernel, jnp.bfloat16
+        scratch = [pltpu.VMEM((2 * rows, 2 * wide), jnp.float32)]
+        in_specs += [whole(2 * rows, 2 * wide), whole(2 * rows, HD), whole(2 * rows, HD)]
+        arguments += [before, *tables]
+    return call(
+        kernel,
+        shape(2 * rows, 2 * wide, dtype),
+        20,
+        8 * rows * depth * wide,
+        4 * depth * wide + 4 * rows * depth,
+        grid_spec=pltpu.PrefetchScalarGridSpec(
+            num_scalar_prefetch=1,
+            grid=(steps,),
+            in_specs=in_specs,
+            out_specs=whole(2 * rows, 2 * wide),
+            scratch_shapes=scratch,
+        ),
+    )(*arguments)
+
+
+def finish_kernel(own, own_a, own_b, far_a, far_b, early, cosine, sine, out):
+    piece = own_a.shape[0]
+    rows = 2 * piece
+    keys = own.shape[1] // 2
+    for at in range(0, 4 * piece, piece):
+        part = pl.ds(at % rows, piece)
+        if at < rows:
+            total = early[part, :].astype(jnp.float32)
+            total = total + (far_a, far_b)[at // piece][...].astype(jnp.float32)
+        else:
+            total = own[part, :] + (own_a, own_b)[at // piece - 2][...].astype(jnp.float32)
+        turn = pl.ds(at, piece)
+        for head in range(0, keys, HD):
+            key = norm_rotate_head(total[:, head : head + HD], cosine[turn, :], sine[turn, :])
+            out[turn, head : head + HD] = key.astype(out.dtype)
+        out[turn, keys:] = total[:, keys:].astype(out.dtype)
+
+
+def attend_kernel(group, q, mine, other, first, last, k_pos, out):
+    rows = q.shape[0]
+    keys = mine.shape[1] // 2
+    heads = keys // HD
+    allowed = (k_pos[...] >= first[...]) & (k_pos[...] <= last[...])
+    allowed = jnp.concatenate([allowed.astype(jnp.float32)] * group, axis=0) > 0.5
+    for head in range(heads):
+        here, there = head * HD, (head + heads // 2) % heads * HD
+        key = jnp.concatenate([mine[:, here : here + HD], other[:, there : there + HD]], 0)
+        here, there = here + keys, there + keys
+        value = jnp.concatenate([mine[:, here : here + HD], other[:, there : there + HD]], 0)
+        at = head * group * HD
+        query = jnp.concatenate([q[:, at + g * HD : at + (g + 1) * HD] for g in range(group)], 0)
+        scores = lax.dot_general(
+            query, key, (((1,), (1,)), ((), ())), preferred_element_type=jnp.float32
+        )
+        weights = jnp.where(allowed, jnp.exp(scores * (1.0 / HD**0.5)), 0.0)
+        weights = weights.astype(jnp.bfloat16)
+        total = jnp.sum(weights.astype(jnp.float32), axis=-1, keepdims=True)
+        mixed = jnp.dot(weights, value, preferred_element_type=jnp.float32) / total
+        mixed = mixed.astype(out.dtype)
+        for g in range(group):
+            out[:, at + g * HD : at + (g + 1) * HD] = mixed[g * rows : (g + 1) * rows, :]
+
+
+def out_kernel(attended, w0, w1, stay, leave):
+    depth = w0.shape[0]
+    total = jnp.dot(attended[:, :depth], w0[...], preferred_element_type=jnp.float32)
+    total += jnp.dot(attended[:, depth:], w1[...], preferred_element_type=jnp.float32)
+    half = stay.shape[0]
+    stay[...] = total[:half]
+    leave[...] = total[half:].astype(leave.dtype)
+
+
+def project_out(attended, w0, w1, chunk):
+    rows = attended.shape[0]
+    depth, wide = w0.shape
+    block = 256
+    steps = wide // OUT_CHUNKS // block
+    first = chunk * steps
+    return call(
+        out_kernel,
+        [
+            shape(rows // 2, steps * block, jnp.float32),
+            shape(rows // 2, steps * block, jnp.bfloat16),
+        ],
+        8,
+        4 * rows * depth * steps * block,
+        4 * depth * steps * block,
+        grid=(steps,),
+        in_specs=[
+            pl.BlockSpec((rows, 2 * depth), lambda i: (0, 0)),
+            pl.BlockSpec((depth, block), lambda i: (0, first + i)),
+            pl.BlockSpec((depth, block), lambda i: (0, first + i)),
+        ],
+        out_specs=[
+            pl.BlockSpec((rows // 2, block), lambda i: (0, i)),
+            pl.BlockSpec((rows // 2, block), lambda i: (0, i)),
+        ],
+    )(attended, w0, w1)
+
+
+def on_four_by_two(inputs, doc_lengths, w_query, w_key, w_value, w_out):
+    own = inputs[0]
+    w_query, w_key, w_value, w_out = w_query[0], w_key[0], w_value[0], w_out[0]
+    rows = own.shape[0]
+    half = w_key.shape[0]
+    group = w_query.shape[1] // w_key.shape[1]
+    ctx, tp = lax.axis_index("ctx"), lax.axis_index("tp")
+    block_rows = rows * lax.axis_size("tp")
+
+    x_far = lax.dynamic_slice_in_dim(own, (1 - ctx) * half, half, 1)
+    x_near = lax.dynamic_slice_in_dim(own, ctx * half, half, 1)
+    far_a = swap(x_far, "ctx", 1)
+    near_b = swap(x_near, "tp", 2)
+    key_s = swap(w_key, "tp", 1)
+    value_s = swap(w_value, "tp", 1)
+    query_s = swap(w_query, "tp", 1)
+    out_s = swap(w_out, "tp", 1)
+    far_b = swap(far_a, "tp", 2)
+
+    piece = jnp.arange(rows, dtype=jnp.int32)
+    base = ctx * block_rows
+    here = jnp.concatenate([piece + rows * tp, piece + rows * (tp ^ 2)]) + base
+    there = jnp.concatenate([piece + rows * (tp ^ 1), piece + rows * (tp ^ 3)]) + base
+    k_pos = jnp.concatenate([here - block_rows, here, there - block_rows, there])[None, :]
+    ends = jnp.cumsum(doc_lengths[0])
+    doc_start = jnp.max(jnp.where(ends[None, :] <= here[:, None], ends[None, :], 0), axis=1)
+    first = jnp.maximum(doc_start, here // SPAN * SPAN)[:, None]
+    cosine, sine = rope_tables(jnp.concatenate([here - block_rows, here]))
+
+    weights = [w_key, key_s, w_value, value_s]
+    own_sum, own_send, far_sum_a = project_kv(
+        [x_near, near_b, far_a],
+        weights,
+        [
+            (0, 2 * rows, jnp.float32),
+            (0, 2 * rows, jnp.bfloat16),
+            (2 * rows, 3 * rows, jnp.bfloat16),
+        ],
+    )
+    early = lax.ppermute(own_send, "ctx", [(0, 1)])
+    own_a = swap(far_sum_a, "ctx", 1)
+    far_sum_b = project_kv([far_b], weights, [(0, rows, jnp.bfloat16)])[0]
+    own_b = swap(far_sum_b, "ctx", 1)
+    far_c = swap(x_far, "tp", 2)
+
+    near = jnp.reshape(ctx, (1,))
+    queries = project_query(near, x_near, near_b, w_query, query_s)
+    queries = project_query(
+        1 - near, x_far, far_c, w_query, query_s, queries, (cosine[2 * rows :], sine[2 * rows :])
+    )
+
+    kv_shape = shape(4 * rows, own_sum.shape[1], jnp.bfloat16)
+    kv_mine = call(finish_kernel, kv_shape, 8, 0, 1 << 20)(
+        own_sum, own_a, own_b, far_sum_a, far_sum_b, early, cosine, sine
+    )
+    kv_other = swap(kv_mine, "tp", 1)
+    attended = call(
+        functools.partial(attend_kernel, group),
+        shape(2 * rows, queries.shape[1], jnp.bfloat16),
+        16,
+        8 * rows * 8 * rows * queries.shape[1],
+        1 << 20,
+    )(queries, kv_mine, kv_other, first, here[:, None], k_pos)
+
+    parts = []
+    for chunk in range(OUT_CHUNKS):
+        stay, leave = project_out(attended, w_out, out_s, chunk)
+        arrived = swap(leave, "tp", 2)
+        mixed = (stay + arrived.astype(jnp.float32)).astype(jnp.bfloat16)
+        parts.append(from_behind(mixed, "pipe", 1))
+    return jnp.concatenate(parts, axis=1)[None]
 
 
 def doc_index(positions, lengths):
@@ -61,7 +355,7 @@
     return (numerator, denominator)
 
 
-def on_device(inputs, doc_lengths, w_query, w_key, w_value, w_out):
+def on_any(inputs, doc_lengths, w_query, w_key, w_value, w_out):
     tok_rows = lax.all_gather(inputs[0], "tp", axis=0, tiled=True)
     block_rows = tok_rows.shape[0]
     q_heads = w_query.shape[2] // HD
@@ -109,8 +403,7 @@
         scatter_dimension=0,
         tiled=True,
     )
-    received = from_behind(mixed, "pipe", 1)
-    return received[None]
+    return from_behind(mixed, "pipe", 1)[None]
 
 
 def solution(mesh):
@@ -123,6 +416,11 @@
         P("pipe", "tp", None),
     )
     out_specs = P("pipe", ("ctx", "tp"), None)
+    paired = mesh.shape["ctx"] == 2 and mesh.shape["tp"] == 4
     return jax.shard_map(
-        on_device, mesh=mesh, in_specs=in_specs, out_specs=out_specs, check_vma=False
-    )
+        on_four_by_two if paired else on_any,
+        mesh=mesh,
+        in_specs=in_specs,
+        out_specs=out_specs,
+        check_vma=False,
+    )

time: 187 us -> 107 us (0.57)
  waiting for transfers between devices: 129 us -> 27.3 us
  Pallas kernels: 0 us -> 39.5 us
  starting transfers between devices: 1.56 us -> 26.5 us
  matrix products: 15.5 us -> 0 us
  between operations: 13.3 us -> 0.31 us
  local copies, waits for them, and re-layouts: 14.8 us -> 5.43 us
  blocking collectives: 8.85 us -> 0 us
  other arithmetic: 2.97 us -> 7.48 us
    all_gather x2 -> x0, waiting for transfers between devices: 76.9 us -> none  [the longest x1 63.6 us: on_device(): lax.all_gather(stacked_weights, 'ctx', axis=1, tiled=True)]
    pallas_call x0 -> x10, Pallas kernels: none -> 39.5 us  [the longest x4 16.1 us: project_out(): call(out_kernel, [shape(rows // 2, steps * block, jnp.float32), shape(row...]
    reduce_scatter x1 -> x0, waiting for transfers between devices: 34.8 us -> none  [on_device(): lax.psum_scatter(jnp.dot(attended, w_out[0], preferred_element_type=jnp.f...]
    ppermute x0 -> x16, starting transfers between devices: none -> 19.9 us  [the longest x15 15.2 us: swap(): lax.ppermute(value, axis, [(source, source ^ bit) for source in range(cou...]
    ppermute x0 -> x16, waiting for transfers between devices: none -> 16.2 us  [the longest x15 16.2 us: swap(): lax.ppermute(value, axis, [(source, source ^ bit) for source in range(cou...]
    dot_general x5 -> x0, matrix products: 15.5 us -> none  [the longest x1 6.27 us: on_device(): queries = jnp.dot(tok_rows, w_query[0], preferred_element_type=jnp.float32)]
    unnamed x12 -> x18, local copies, waits for them, and re-layouts: 14.8 us -> 3.26 us
    all_gather x1 -> x0, blocking collectives: 8.85 us -> none  [on_device(): shard_piece = lax.all_gather(key_value_pair, 'ctx', axis=1, tiled=True)]
  transfers between devices with their start and end apart: 4 -> 20, of which waited for: 4 -> 10; matrix products, arithmetic and copies ran while one was open for 12% -> 8% of each run, Pallas kernels for 0% -> 33%
where the time goes in v1:
time: 107 us
  Pallas kernels  39.5 us (37%)
  waiting for transfers between devices  27.3 us (26%)
  starting transfers between devices  26.5 us (25%)
  other arithmetic  7.48 us (7%)
  local copies, waits for them, and re-layouts  5.43 us (5%)
    ppermute x15, waiting for transfers between devices, swap(): lax.ppermute(value, axis, [(source, source ^ bit) for source in range(cou...  16.2 us
    pallas_call x4, Pallas kernels, project_out(): call(out_kernel, [shape(rows // 2, steps * block, jnp.float32), shape(row...  16.1 us
    ppermute x15, starting transfers between devices, swap(): lax.ppermute(value, axis, [(source, source ^ bit) for source in range(cou...  15.2 us
    pallas_call x2, Pallas kernels, project_query(): call(kernel, shape(2 * rows, 2 * wide, dtype), 20, 8 * rows * depth * wid...  12.1 us
    ppermute x4, waiting for transfers between devices, from_behind(): return lax.ppermute(value, axis, pairs)  11 us
    pallas_call x2, Pallas kernels, project_kv(): call(functools.partial(project_kernel, count, len(ws), [(a, b) for a, b,...  8.62 us
    ppermute x4, starting transfers between devices, from_behind(): return lax.ppermute(value, axis, pairs)  6.53 us
    ppermute x1, starting transfers between devices, on_four_by_two(): early = lax.ppermute(own_send, 'ctx', [(0, 1)])  4.78 us
  transfers between devices with their start and end apart: 20, of which 10 were waited for; matrix products, arithmetic and copies ran while one was open for 8% of the time, Pallas kernels for 33%

profile of v1, /device:TPU:0, one launch (start us, length us, event | category | flops | bytes accessed | tf_op | source)
XLA Modules:
  0.0 106.5 jit_solution(4018791318229966046)
XLA Ops:
  0.0 0.5 collective-permute-start.1
  0.5 0.1 collective-permute-start.11
  0.5 1.9 %dynamic-slice_bitcast_fusion = (bf16[64,2560]{1,0:T(8,128)(2,1)S(1)}, bf16[64,2560]{1,0:T(8,128)(2,1)}) fusion(bf16[1,64,5120]{2,1,0:T(8,128)(2,1)} %param.6, s32[]{:T(128)S(6)} %select_n.23, s32[]{:T(128)S(6)} %select_n.22), kind=kLoop, calls=%fused_computation.5 | loop fusion | bytes 1310728 | tf_op jit(solution)/shard_map/dynamic_slice | solution.py:251
  2.5 2.9 %collective-permute-start.2 = (bf16[64,2560]{1,0:T(8,128)(2,1)S(1)}, bf16[64,2560]{1,0:T(8,128)(2,1)S(1)}, u32[]{:S(2)}, u32[]{:S(2)}) collective-permute-start(bf16[64,2560]{1,0:T(8,128)(2,1)S(1)} %get-tuple-element.33.x0.refs_0_), channel_id=1, source_target_pairs={{0,2},{1,3},{2,0},{3,1},{4,6},{5,7},{6,4},{7,5},{8,10},{9,11},{10,... | collective-permute-start | bytes 983048 | tf_op jit(solution)/shard_map/ppermute | solution.py:26
  5.4 0.0 collective-permute-start.4
  5.4 0.5 collective-permute-start.5
  6.0 0.1 broadcast_add_fusion.1
  6.1 7.3 %collective-permute-done.2.x1.refs_1_ = bf16[64,2560]{1,0:T(8,128)(2,1)S(1)} collective-permute-done((bf16[64,2560]{1,0:T(8,128)(2,1)S(1)}, bf16[64,2560]{1,0:T(8,128)(2,1)S(1)}, u32[]{:S(2)}, u32[]{:S(2)}) %collective-permute-start.2) | collective-permute-done | bytes 327712 | tf_op jit(solution)/shard_map/ppermute | solution.py:26
  13.4 1.7 %collective-permute-start.3 = (bf16[64,2560]{1,0:T(8,128)(2,1)}, bf16[64,2560]{1,0:T(8,128)(2,1)}, u32[]{:S(2)}, u32[]{:S(2)}) collective-permute-start(bf16[64,2560]{1,0:T(8,128)(2,1)} %get-tuple-element.34.x0), channel_id=1, source_target_pairs={{0,4},{4,0},{1,5},{5,1},{2,6},{6,2},{3,7},{7,3},{8,12},{12,8},{9,1... | collective-permute-start | bytes 983048 | tf_op jit(solution)/shard_map/ppermute | solution.py:26
  15.1 1.2 %multiply_sine_fusion = (f32[256,64]{1,0:T(8,128)S(1)}, f32[256,64]{1,0:T(8,128)}, f32[256,64]{1,0:T(8,128)}) fusion(f32[64]{0:T(128)S(1)} %negate_power_fusion, f32[256]{0:T(256)S(1)} %add_convert_fusion.4), kind=kLoop, calls=%fused_computation.7 | loop fusion | flops 32768 | bytes 197888 | tf_op jit(solution)/shard_map/sin | solution.py:33
  16.3 0.7 reduce-window.8
  17.0 1.0 fusion.4.cosine
  18.0 0.9 fusion.3.sine
  19.0 3.9 %collective-permute-done.3.refs_2_ = bf16[64,2560]{1,0:T(8,128)(2,1)} collective-permute-done((bf16[64,2560]{1,0:T(8,128)(2,1)}, bf16[64,2560]{1,0:T(8,128)(2,1)}, u32[]{:S(2)}, u32[]{:S(2)}) %collective-permute-start.3) | collective-permute-done | bytes 327712 | tf_op jit(solution)/shard_map/ppermute | solution.py:26
  22.9 1.4 %collective-permute-start.7 = (bf16[64,2560]{1,0:T(8,128)(2,1)}, bf16[64,2560]{1,0:T(8,128)(2,1)S(1)}, u32[]{:S(2)}, u32[]{:S(2)}) collective-permute-start(bf16[64,2560]{1,0:T(8,128)(2,1)} %collective-permute-done.3.refs_2_), channel_id=1, source_target_pairs={{0,2},{1,3},{2,0},{3,1},{4,6},{5,7},{6,4},{7,5},{8,10},{9,11},{10,... | collective-permute-start | bytes 983048 | tf_op jit(solution)/shard_map/ppermute | solution.py:26
  24.3 1.3 %select_reduce_fusion = s32[128]{0:T(128)} fusion(s32[128]{0:T(128)S(1)} %get-tuple-element.39, s32[8]{0:T(128)} %bitcast.38), kind=kLoop, calls=%fused_computation.28 | loop fusion | flops 2944 | bytes 1056 | tf_op jit(solution)/shard_map/reduce_max | solution.py:266
  25.6 1.0 pad_maximum_fusion.1.sine
  26.6 0.0 collective-permute-done.4.refs_4_.refs_2_
  26.6 1.3 %collective-permute-done.5.refs_6_.refs_4_ = bf16[2560,256]{1,0:T(8,128)(2,1)} collective-permute-done((bf16[2560,256]{1,0:T(8,128)(2,1)}, bf16[2560,256]{1,0:T(8,128)(2,1)}, u32[]{:S(2)}, u32[]{:S(2)}) %collective-permute-start.5) | collective-permute-done | bytes 1310752 | tf_op jit(solution)/shard_map/ppermute | solution.py:26
  27.8 4.5 %shard_map.66 = (f32[128,1024]{1,0:T(8,128)S(1)}, bf16[128,1024]{1,0:T(8,128)(2,1)S(1)}, bf16[64,1024]{1,0:T(8,128)(2,1)S(1)}) custom-call(bf16[64,2560]{1,0:T(8,128)(2,1)S(1)} %get-tuple-element.33.x0.refs_0_, bf16[64,2560]{1,0:T(8,128)(2,1)S(1)} %collective-permute-done.2.x1.refs_1_, bf16[64,2560]{1,0:T(8,128)(2,1)} %collective-permute-done.3.refs_2_, ...), custom_call_target="tpu_custom_call" | custom-call | flops 1006632960 | bytes 6225920 | tf_op jit(solution)/shard_map/pallas_call | solution.py:83
  32.4 4.8 %collective-permute-start.9 = (bf16[128,1024]{1,0:T(8,128)(2,1)S(1)}, bf16[128,1024]{1,0:T(8,128)(2,1)S(1)}, u32[]{:S(2)}, u32[]{:S(2)}) collective-permute-start(bf16[128,1024]{1,0:T(8,128)(2,1)S(1)} %get-tuple-element.18), channel_id=1, source_target_pairs={{0,4},{1,5},{2,6},{3,7},{8,12},{9,13},{10,14},{11,15},{16,20},{17,... | collective-permute-start | bytes 786440 | tf_op jit(solution)/shard_map/ppermute | solution.py:280
  37.2 0.1 collective-permute-start.6
  37.3 0.0 collective-permute-done.7.refs_0_
  37.3 4.1 %shard_map.67.far_b = bf16[64,1024]{1,0:T(8,128)(2,1)S(1)} custom-call(bf16[64,2560]{1,0:T(8,128)(2,1)S(1)} %collective-permute-done.7.refs_0_, bf16[2560,256]{1,0:T(8,128)(2,1)S(1)} %bitcast.31, bf16[2560,256]{1,0:T(8,128)(2,1)} %collective-permute-done.4.refs_4_.refs_2_, bf16[2560,256]{1,0:T(8,128)(2,1)S(1)} %bitcast.34, ...), custom_call_target="tpu_custom_call" | custom-call | flops 335544320 | bytes 5570560 | tf_op jit(solution)/shard_map/pallas_call | solution.py:83
  41.4 2.1 %collective-permute-start.8 = (bf16[64,1024]{1,0:T(8,128)(2,1)S(1)}, bf16[64,1024]{1,0:T(8,128)(2,1)S(1)}, u32[]{:S(2)}, u32[]{:S(2)}) collective-permute-start(bf16[64,1024]{1,0:T(8,128)(2,1)S(1)} %shard_map.67.far_b), channel_id=1, source_target_pairs={{0,4},{4,0},{1,5},{5,1},{2,6},{6,2},{3,7},{7,3},{8,12},{12,8},{9,1... | collective-permute-start | bytes 393224 | tf_op jit(solution)/shard_map/ppermute | solution.py:26
  43.4 0.1 pad_maximum_fusion.cosine
  43.5 3.1 %collective-permute-done.6.own_a = bf16[64,1024]{1,0:T(8,128)(2,1)S(1)} collective-permute-done((bf16[64,1024]{1,0:T(8,128)(2,1)S(1)}, bf16[64,1024]{1,0:T(8,128)(2,1)S(1)}, u32[]{:S(2)}, u32[]{:S(2)}) %collective-permute-start.6) | collective-permute-done | bytes 131104 | tf_op jit(solution)/shard_map/ppermute | solution.py:26
  46.6 1.5 %collective-permute-start = (bf16[64,2560]{1,0:T(8,128)(2,1)}, bf16[64,2560]{1,0:T(8,128)(2,1)S(1)}, u32[]{:S(2)}, u32[]{:S(2)}) collective-permute-start(bf16[64,2560]{1,0:T(8,128)(2,1)} %get-tuple-element.34.x0), channel_id=1, source_target_pairs={{0,2},{1,3},{2,0},{3,1},{4,6},{5,7},{6,4},{7,5},{8,10},{9,11},{10,... | collective-permute-start | bytes 983048 | tf_op jit(solution)/shard_map/ppermute | solution.py:26
  48.1 0.5 collective-permute-done.8.own_b
  48.6 0.0 collective-permute-done.9.early
  48.6 1.4 %shard_map.68.mine = bf16[256,1024]{1,0:T(8,128)(2,1)S(1)} custom-call(f32[128,1024]{1,0:T(8,128)S(1)} %get-tuple-element.16.own, bf16[64,1024]{1,0:T(8,128)(2,1)S(1)} %collective-permute-done.6.own_a, bf16[64,1024]{1,0:T(8,128)(2,1)S(1)} %collective-permute-done.8.own_b, bf16[64,1024]{1,0:T(8,128)(2,1)S(1)} %get-tuple-element.17.far_a, ...), custom_call_target="tpu_custom_call" | custom-call | bytes 1048576 | tf_op jit(solution)/shard_map/pallas_call | solution.py:293
  50.1 0.1 collective-permute-start.10
  50.1 0.1 pad_add_fusion.1
  50.2 0.1 copy.16
  50.3 0.1 copy.14
  50.4 0.1 fusion.2
  50.5 0.0 collective-permute-done.1.w1
  50.5 0.0 copy-start
  50.5 3.2 %copy-done = bf16[1,5120,768]{2,1,0:T(8,128)(2,1)S(1)} copy-done((bf16[1,5120,768]{2,1,0:T(8,128)(2,1)S(1)}, bf16[1,5120,768]{2,1,0:T(8,128)(2,1)}, u32[]{:S(2)}) %copy-start) | copy-done | bytes 7864344
  53.7 5.9 %shard_map.64.before = f32[128,1536]{1,0:T(8,128)S(1)} custom-call(s32[1]{0:T(128)} %bitcast.half_ref, bf16[64,2560]{1,0:T(8,128)(2,1)S(1)} %get-tuple-element.33.x0.refs_0_, bf16[64,2560]{1,0:T(8,128)(2,1)S(1)} %collective-permute-done.2.x1.refs_1_, bf16[5120,768]{1,0:T(8,128)(2,1)S(1)} %bitcast.27, bf16[5120,768]{1,0:T(8,128)(2,1)} %collective-permute-done.1.w1), custom_call_target="tpu_custom_call" | custom-call | flops 1006632960 | bytes 8519680 | tf_op jit(solution)/shard_map/pallas_call | solution.py:145
  59.7 0.0 slice-start.1
  59.7 6.2 %shard_map.65.q = bf16[128,1536]{1,0:T(8,128)(2,1)S(1)} custom-call(s32[1]{0:T(128)S(6)} %sub.19.half_ref, bf16[64,2560]{1,0:T(8,128)(2,1)} %get-tuple-element.34.x0, bf16[64,2560]{1,0:T(8,128)(2,1)S(1)} %collective-permute-done.x1, bf16[5120,768]{1,0:T(8,128)(2,1)S(1)} %bitcast.28, bf16[5120,768]{1,0:T(8,128)(2,1)} %collective-permute-done.1.w1, ...), custom_call_target="tpu_custom_call" | custom-call | flops 1006632960 | bytes 8519680 | tf_op jit(solution)/shard_map/pallas_call | solution.py:145
  65.9 1.2 %shard_map.69.attended = bf16[128,1536]{1,0:T(8,128)(2,1)S(1)} custom-call(bf16[128,1536]{1,0:T(8,128)(2,1)S(1)} %shard_map.65.q, bf16[256,1024]{1,0:T(8,128)(2,1)S(1)} %shard_map.68.mine, bf16[256,1024]{1,0:T(8,128)(2,1)S(1)} %collective-permute-done.10.other, s32[128,1]{1,0:T(8,128)S(1)} %get-tuple-element.29.first, s32[128,1]{1,0:T(8,128)S(1)} %get-tuple-element.30.last, ...), custom_call_target="tpu_custom_call" | custom-call | flops 402653184 | bytes 1048576 | tf_op jit(solution)/shard_map/pallas_call | solution.py:297
  67.1 0.0 collective-permute-done.11.w1
  67.2 4.0 %shard_map.70 = (f32[64,1280]{1,0:T(8,128)S(1)}, bf16[64,1280]{1,0:T(8,128)(2,1)S(1)}) custom-call(bf16[128,1536]{1,0:T(8,128)(2,1)S(1)} %shard_map.69.attended, bf16[768,5120]{1,0:T(8,128)(2,1)S(1)} %bitcast.22, bf16[768,5120]{1,0:T(8,128)(2,1)} %collective-permute-done.11.w1), custom_call_target="tpu_custom_call" | custom-call | flops 503316480 | bytes 3932160 | tf_op jit(solution)/shard_map/pallas_call | solution.py:219
  71.2 1.6 %collective-permute-start.12 = (bf16[64,1280]{1,0:T(8,128)(2,1)S(1)}, bf16[64,1280]{1,0:T(8,128)(2,1)S(1)}, u32[]{:S(2)}, u32[]{:S(2)}) collective-permute-start(bf16[64,1280]{1,0:T(8,128)(2,1)S(1)} %get-tuple-element.20), channel_id=1, source_target_pairs={{0,2},{1,3},{2,0},{3,1},{4,6},{5,7},{6,4},{7,5},{8,10},{9,11},{10,... | collective-permute-start | bytes 491528 | tf_op jit(solution)/shard_map/ppermute | solution.py:26
  72.8 4.0 %shard_map.71 = (f32[64,1280]{1,0:T(8,128)S(1)}, bf16[64,1280]{1,0:T(8,128)(2,1)S(1)}) custom-call(bf16[128,1536]{1,0:T(8,128)(2,1)S(1)} %shard_map.69.attended, bf16[768,5120]{1,0:T(8,128)(2,1)S(1)} %bitcast.23, bf16[768,5120]{1,0:T(8,128)(2,1)} %collective-permute-done.11.w1), custom_call_target="tpu_custom_call" | custom-call | flops 503316480 | bytes 3932160 | tf_op jit(solution)/shard_map/pallas_call | solution.py:219
  76.8 0.6 collective-permute-start.14
  77.4 4.0 %shard_map.72 = (f32[64,1280]{1,0:T(8,128)S(1)}, bf16[64,1280]{1,0:T(8,128)(2,1)S(1)}) custom-call(bf16[128,1536]{1,0:T(8,128)(2,1)S(1)} %shard_map.69.attended, bf16[768,5120]{1,0:T(8,128)(2,1)S(1)} %bitcast.24, bf16[768,5120]{1,0:T(8,128)(2,1)} %collective-permute-done.11.w1), custom_call_target="tpu_custom_call" | custom-call | flops 503316480 | bytes 3932160 | tf_op jit(solution)/shard_map/pallas_call | solution.py:219
  81.5 1.6 %collective-permute-start.16 = (bf16[64,1280]{1,0:T(8,128)(2,1)S(1)}, bf16[64,1280]{1,0:T(8,128)(2,1)S(1)}, u32[]{:S(2)}, u32[]{:S(2)}) collective-permute-start(bf16[64,1280]{1,0:T(8,128)(2,1)S(1)} %get-tuple-element.24), channel_id=1, source_target_pairs={{0,2},{1,3},{2,0},{3,1},{4,6},{5,7},{6,4},{7,5},{8,10},{9,11},{10,... | collective-permute-start | bytes 491528 | tf_op jit(solution)/shard_map/ppermute | solution.py:26
  83.0 4.0 %shard_map.73 = (f32[64,1280]{1,0:T(8,128)S(1)}, bf16[64,1280]{1,0:T(8,128)(2,1)S(1)}) custom-call(bf16[128,1536]{1,0:T(8,128)(2,1)S(1)} %shard_map.69.attended, bf16[768,5120]{1,0:T(8,128)(2,1)S(1)} %bitcast.25, bf16[768,5120]{1,0:T(8,128)(2,1)} %collective-permute-done.11.w1), custom_call_target="tpu_custom_call" | custom-call | flops 503316480 | bytes 3932160 | tf_op jit(solution)/shard_map/pallas_call | solution.py:219
  87.1 0.6 collective-permute-start.18
  87.7 0.0 collective-permute-done.12
  87.7 1.6 %collective-permute-start.13 = (bf16[64,1280]{1,0:T(8,128)(2,1)S(1)}, bf16[64,1280]{1,0:T(8,128)(2,1)S(1)}, u32[]{:S(2)}, u32[]{:S(2)}) collective-permute-start(bf16[64,1280]{1,0:T(8,128)(2,1)S(1)} %add_convert_fusion.3), channel_id=1, source_target_pairs={{0,8},{8,16},{16,24},{24,0},{1,9},{9,17},{17,25},{25,1},{2,10},{10... | collective-permute-start | bytes 491528 | tf_op jit(solution)/shard_map/ppermute | solution.py:21
  89.4 1.6 %collective-permute-start.15 = (bf16[64,1280]{1,0:T(8,128)(2,1)S(1)}, bf16[64,1280]{1,0:T(8,128)(2,1)S(1)}, u32[]{:S(2)}, u32[]{:S(2)}) collective-permute-start(bf16[64,1280]{1,0:T(8,128)(2,1)S(1)} %add_convert_fusion.2), channel_id=1, source_target_pairs={{0,8},{8,16},{16,24},{24,0},{1,9},{9,17},{17,25},{25,1},{2,10},{10... | collective-permute-start | bytes 491528 | tf_op jit(solution)/shard_map/ppermute | solution.py:21
  91.0 0.0 collective-permute-done.16
  91.0 1.6 %collective-permute-start.17 = (bf16[64,1280]{1,0:T(8,128)(2,1)S(1)}, bf16[64,1280]{1,0:T(8,128)(2,1)S(1)}, u32[]{:S(2)}, u32[]{:S(2)}) collective-permute-start(bf16[64,1280]{1,0:T(8,128)(2,1)S(1)} %add_convert_fusion.1), channel_id=1, source_target_pairs={{0,8},{8,16},{16,24},{24,0},{1,9},{9,17},{17,25},{25,1},{2,10},{10... | collective-permute-start | bytes 491528 | tf_op jit(solution)/shard_map/ppermute | solution.py:21
  92.7 0.2 collective-permute-done.18
  92.9 1.6 %collective-permute-start.19 = (bf16[64,1280]{1,0:T(8,128)(2,1)S(1)}, bf16[64,1280]{1,0:T(8,128)(2,1)S(1)}, u32[]{:S(2)}, u32[]{:S(2)}) collective-permute-start(bf16[64,1280]{1,0:T(8,128)(2,1)S(1)} %add_convert_fusion), channel_id=1, source_target_pairs={{0,8},{8,16},{16,24},{24,0},{1,9},{9,17},{17,25},{25,1},{2,10},{10... | collective-permute-start | bytes 491528 | tf_op jit(solution)/shard_map/ppermute | solution.py:21
  94.6 2.1 %collective-permute-done.13 = bf16[64,1280]{1,0:T(8,128)(2,1)S(1)} collective-permute-done((bf16[64,1280]{1,0:T(8,128)(2,1)S(1)}, bf16[64,1280]{1,0:T(8,128)(2,1)S(1)}, u32[]{:S(2)}, u32[]{:S(2)}) %collective-permute-start.13) | collective-permute-done | bytes 163872 | tf_op jit(solution)/shard_map/ppermute | solution.py:21
  96.7 3.5 %collective-permute-done.15 = bf16[64,1280]{1,0:T(8,128)(2,1)S(1)} collective-permute-done((bf16[64,1280]{1,0:T(8,128)(2,1)S(1)}, bf16[64,1280]{1,0:T(8,128)(2,1)S(1)}, u32[]{:S(2)}, u32[]{:S(2)}) %collective-permute-start.15) | collective-permute-done | bytes 163872 | tf_op jit(solution)/shard_map/ppermute | solution.py:21
  100.2 3.5 %collective-permute-done.17 = bf16[64,1280]{1,0:T(8,128)(2,1)S(1)} collective-permute-done((bf16[64,1280]{1,0:T(8,128)(2,1)S(1)}, bf16[64,1280]{1,0:T(8,128)(2,1)S(1)}, u32[]{:S(2)}, u32[]{:S(2)}) %collective-permute-start.17) | collective-permute-done | bytes 163872 | tf_op jit(solution)/shard_map/ppermute | solution.py:21
  103.7 1.9 %collective-permute-done.19 = bf16[64,1280]{1,0:T(8,128)(2,1)S(1)} collective-permute-done((bf16[64,1280]{1,0:T(8,128)(2,1)S(1)}, bf16[64,1280]{1,0:T(8,128)(2,1)S(1)}, u32[]{:S(2)}, u32[]{:S(2)}) %collective-permute-start.19) | collective-permute-done | bytes 163872 | tf_op jit(solution)/shard_map/ppermute | solution.py:21
  105.6 0.9 maximum_bitcast_fusion
  (31 shorter events, 0.2 us)
Async XLA Ops:
  0.0 5.4 %copy-start.2 = (bf16[1,2560,256]{2,1,0:T(8,128)(2,1)S(1)}, bf16[1,2560,256]{2,1,0:T(8,128)(2,1)}, u32[]{:S(2)}) copy-start(bf16[1,2560,256]{2,1,0:T(8,128)(2,1)} %param.9) | copy-start | bytes 3932164
  0.0 16.3 %copy-start.6 = (s32[1,8]{1,0:T(1,128)S(1)}, s32[1,8]{1,0:T(1,128)}, u32[]{:S(2)}) copy-start(s32[1,8]{1,0:T(1,128)} %param.7) | copy-start | bytes 100
  0.0 50.5 %collective-permute-start.1 = (bf16[5120,768]{1,0:T(8,128)(2,1)}, bf16[5120,768]{1,0:T(8,128)(2,1)}, u32[]{:S(2)}, u32[]{:S(2)}) collective-permute-start(bf16[5120,768]{1,0:T(8,128)(2,1)} %bitcast.26), channel_id=1, source_target_pairs={{0,1},{1,0},{2,3},{3,2},{4,5},{5,4},{6,7},{7,6},{8,9},{9,8},{10,11... | collective-permute-start | bytes 23592968 | tf_op jit(solution)/shard_map/ppermute | solution.py:26
  0.5 66.7 %collective-permute-start.11 = (bf16[768,5120]{1,0:T(8,128)(2,1)}, bf16[768,5120]{1,0:T(8,128)(2,1)}, u32[]{:S(2)}, u32[]{:S(2)}) collective-permute-start(bf16[768,5120]{1,0:T(8,128)(2,1)} %bitcast.19), channel_id=1, source_target_pairs={{0,1},{1,0},{2,3},{3,2},{4,5},{5,4},{6,7},{7,6},{8,9},{9,8},{10,11... | collective-permute-start | bytes 23592968 | tf_op jit(solution)/shard_map/ppermute | solution.py:26
  0.5 27.3 %copy-start.3 = (bf16[1,2560,256]{2,1,0:T(8,128)(2,1)S(1)}, bf16[1,2560,256]{2,1,0:T(8,128)(2,1)}, u32[]{:S(2)}) copy-start(bf16[1,2560,256]{2,1,0:T(8,128)(2,1)} %param.10) | copy-start | bytes 3932164
  2.5 10.9 %collective-permute-start.2 = (bf16[64,2560]{1,0:T(8,128)(2,1)S(1)}, bf16[64,2560]{1,0:T(8,128)(2,1)S(1)}, u32[]{:S(2)}, u32[]{:S(2)}) collective-permute-start(bf16[64,2560]{1,0:T(8,128)(2,1)S(1)} %get-tuple-element.33.x0.refs_0_), channel_id=1, source_target_pairs={{0,2},{1,3},{2,0},{3,1},{4,6},{5,7},{6,4},{7,5},{8,10},{9,11},{10,... | collective-permute-start | bytes 983048 | tf_op jit(solution)/shard_map/ppermute | solution.py:26
  5.4 21.1 %collective-permute-start.4 = (bf16[2560,256]{1,0:T(8,128)(2,1)S(1)}, bf16[2560,256]{1,0:T(8,128)(2,1)}, u32[]{:S(2)}, u32[]{:S(2)}) collective-permute-start(bf16[2560,256]{1,0:T(8,128)(2,1)S(1)} %bitcast.29), channel_id=1, source_target_pairs={{0,1},{1,0},{2,3},{3,2},{4,5},{5,4},{6,7},{7,6},{8,9},{9,8},{10,11... | collective-permute-start | bytes 3932168 | tf_op jit(solution)/shard_map/ppermute | solution.py:26
  5.4 22.4 %collective-permute-start.5 = (bf16[2560,256]{1,0:T(8,128)(2,1)}, bf16[2560,256]{1,0:T(8,128)(2,1)}, u32[]{:S(2)}, u32[]{:S(2)}) collective-permute-start(bf16[2560,256]{1,0:T(8,128)(2,1)} %bitcast.32), channel_id=1, source_target_pairs={{0,1},{1,0},{2,3},{3,2},{4,5},{5,4},{6,7},{7,6},{8,9},{9,8},{10,11... | collective-permute-start | bytes 3932168 | tf_op jit(solution)/shard_map/ppermute | solution.py:26
  13.4 9.5 %collective-permute-start.3 = (bf16[64,2560]{1,0:T(8,128)(2,1)}, bf16[64,2560]{1,0:T(8,128)(2,1)}, u32[]{:S(2)}, u32[]{:S(2)}) collective-permute-start(bf16[64,2560]{1,0:T(8,128)(2,1)} %get-tuple-element.34.x0), channel_id=1, source_target_pairs={{0,4},{4,0},{1,5},{5,1},{2,6},{6,2},{3,7},{7,3},{8,12},{12,8},{9,1... | collective-permute-start | bytes 983048 | tf_op jit(solution)/shard_map/ppermute | solution.py:26
  22.9 14.4 %collective-permute-start.7 = (bf16[64,2560]{1,0:T(8,128)(2,1)}, bf16[64,2560]{1,0:T(8,128)(2,1)S(1)}, u32[]{:S(2)}, u32[]{:S(2)}) collective-permute-start(bf16[64,2560]{1,0:T(8,128)(2,1)} %collective-permute-done.3.refs_2_), channel_id=1, source_target_pairs={{0,2},{1,3},{2,0},{3,1},{4,6},{5,7},{6,4},{7,5},{8,10},{9,11},{10,... | collective-permute-start | bytes 983048 | tf_op jit(solution)/shard_map/ppermute | solution.py:26
  32.4 16.2 %collective-permute-start.9 = (bf16[128,1024]{1,0:T(8,128)(2,1)S(1)}, bf16[128,1024]{1,0:T(8,128)(2,1)S(1)}, u32[]{:S(2)}, u32[]{:S(2)}) collective-permute-start(bf16[128,1024]{1,0:T(8,128)(2,1)S(1)} %get-tuple-element.18), channel_id=1, source_target_pairs={{0,4},{1,5},{2,6},{3,7},{8,12},{9,13},{10,14},{11,15},{16,20},{17,... | collective-permute-start | bytes 786440 | tf_op jit(solution)/shard_map/ppermute | solution.py:280
  37.2 6.3 %copy-start.4 = (f32[256,64]{1,0:T(8,128)S(1)}, f32[256,64]{1,0:T(8,128)}, u32[]{:S(2)}) copy-start(f32[256,64]{1,0:T(8,128)} %get-tuple-element.37) | copy-start | bytes 196612
  37.2 9.4 %collective-permute-start.6 = (bf16[64,1024]{1,0:T(8,128)(2,1)S(1)}, bf16[64,1024]{1,0:T(8,128)(2,1)S(1)}, u32[]{:S(2)}, u32[]{:S(2)}) collective-permute-start(bf16[64,1024]{1,0:T(8,128)(2,1)S(1)} %get-tuple-element.17.far_a), channel_id=1, source_target_pairs={{0,4},{4,0},{1,5},{5,1},{2,6},{6,2},{3,7},{7,3},{8,12},{12,8},{9,1... | collective-permute-start | bytes 393224 | tf_op jit(solution)/shard_map/ppermute | solution.py:26
  41.4 8.8 %copy-start.5 = (s32[128]{0:T(128)S(1)}, s32[128]{0:T(128)}, u32[]{:S(2)}) copy-start(s32[128]{0:T(128)} %select_reduce_fusion) | copy-start | bytes 1540
  41.4 7.2 %collective-permute-start.8 = (bf16[64,1024]{1,0:T(8,128)(2,1)S(1)}, bf16[64,1024]{1,0:T(8,128)(2,1)S(1)}, u32[]{:S(2)}, u32[]{:S(2)}) collective-permute-start(bf16[64,1024]{1,0:T(8,128)(2,1)S(1)} %shard_map.67.far_b), channel_id=1, source_target_pairs={{0,4},{4,0},{1,5},{5,1},{2,6},{6,2},{3,7},{7,3},{8,12},{12,8},{9,1... | collective-permute-start | bytes 393224 | tf_op jit(solution)/shard_map/ppermute | solution.py:26
  46.6 13.1 %collective-permute-start = (bf16[64,2560]{1,0:T(8,128)(2,1)}, bf16[64,2560]{1,0:T(8,128)(2,1)S(1)}, u32[]{:S(2)}, u32[]{:S(2)}) collective-permute-start(bf16[64,2560]{1,0:T(8,128)(2,1)} %get-tuple-element.34.x0), channel_id=1, source_target_pairs={{0,2},{1,3},{2,0},{3,1},{4,6},{5,7},{6,4},{7,5},{8,10},{9,11},{10,... | collective-permute-start | bytes 983048 | tf_op jit(solution)/shard_map/ppermute | solution.py:26
  50.1 15.9 %collective-permute-start.10 = (bf16[256,1024]{1,0:T(8,128)(2,1)S(1)}, bf16[256,1024]{1,0:T(8,128)(2,1)S(1)}, u32[]{:S(2)}, u32[]{:S(2)}) collective-permute-start(bf16[256,1024]{1,0:T(8,128)(2,1)S(1)} %shard_map.68.mine), channel_id=1, source_target_pairs={{0,1},{1,0},{2,3},{3,2},{4,5},{5,4},{6,7},{7,6},{8,9},{9,8},{10,11... | collective-permute-start | bytes 1572872 | tf_op jit(solution)/shard_map/ppermute | solution.py:26
  50.5 3.2 %copy-start = (bf16[1,5120,768]{2,1,0:T(8,128)(2,1)S(1)}, bf16[1,5120,768]{2,1,0:T(8,128)(2,1)}, u32[]{:S(2)}) copy-start(bf16[1,5120,768]{2,1,0:T(8,128)(2,1)} %param.8) | copy-start | bytes 23592964
  53.7 6.0 %copy-start.1 = (bf16[1,5120,768]{2,1,0:T(8,128)(2,1)S(1)}, bf16[1,5120,768]{2,1,0:T(8,128)(2,1)}, u32[]{:S(2)}) copy-start(bf16[1,5120,768]{2,1,0:T(8,128)(2,1)} %param.8) | copy-start | bytes 23592964
  53.7 13.4 %slice-start = ((s8[7864320]{0:T(1024)(128)(4,1)}), s8[4194304]{0:T(1024)(128)(4,1)S(1)}, s32[]{:S(2)}) async-start(s8[7864320]{0:T(1024)(128)(4,1)} %bitcast.20), calls=%async_computation | async-start | bytes 8388608
  59.7 7.5 %slice-start.1 = ((s8[7864320]{0:T(1024)(128)(4,1)}), s8[3670016]{0:T(1024)(128)(4,1)S(1)}, s32[]{:S(2)}) async-start(s8[7864320]{0:T(1024)(128)(4,1)} %bitcast.20), calls=%async_computation.1 | async-start | bytes 7340032
  71.2 16.4 %collective-permute-start.12 = (bf16[64,1280]{1,0:T(8,128)(2,1)S(1)}, bf16[64,1280]{1,0:T(8,128)(2,1)S(1)}, u32[]{:S(2)}, u32[]{:S(2)}) collective-permute-start(bf16[64,1280]{1,0:T(8,128)(2,1)S(1)} %get-tuple-element.20), channel_id=1, source_target_pairs={{0,2},{1,3},{2,0},{3,1},{4,6},{5,7},{6,4},{7,5},{8,10},{9,11},{10,... | collective-permute-start | bytes 491528 | tf_op jit(solution)/shard_map/ppermute | solution.py:26
  76.8 12.5 %collective-permute-start.14 = (bf16[64,1280]{1,0:T(8,128)(2,1)S(1)}, bf16[64,1280]{1,0:T(8,128)(2,1)S(1)}, u32[]{:S(2)}, u32[]{:S(2)}) collective-permute-start(bf16[64,1280]{1,0:T(8,128)(2,1)S(1)} %get-tuple-element.22), channel_id=1, source_target_pairs={{0,2},{1,3},{2,0},{3,1},{4,6},{5,7},{6,4},{7,5},{8,10},{9,11},{10,... | collective-permute-start | bytes 491528 | tf_op jit(solution)/shard_map/ppermute | solution.py:26
  81.5 9.5 %collective-permute-start.16 = (bf16[64,1280]{1,0:T(8,128)(2,1)S(1)}, bf16[64,1280]{1,0:T(8,128)(2,1)S(1)}, u32[]{:S(2)}, u32[]{:S(2)}) collective-permute-start(bf16[64,1280]{1,0:T(8,128)(2,1)S(1)} %get-tuple-element.24), channel_id=1, source_target_pairs={{0,2},{1,3},{2,0},{3,1},{4,6},{5,7},{6,4},{7,5},{8,10},{9,11},{10,... | collective-permute-start | bytes 491528 | tf_op jit(solution)/shard_map/ppermute | solution.py:26
  87.1 5.8 %collective-permute-start.18 = (bf16[64,1280]{1,0:T(8,128)(2,1)S(1)}, bf16[64,1280]{1,0:T(8,128)(2,1)S(1)}, u32[]{:S(2)}, u32[]{:S(2)}) collective-permute-start(bf16[64,1280]{1,0:T(8,128)(2,1)S(1)} %get-tuple-element.26), channel_id=1, source_target_pairs={{0,2},{1,3},{2,0},{3,1},{4,6},{5,7},{6,4},{7,5},{8,10},{9,11},{10,... | collective-permute-start | bytes 491528 | tf_op jit(solution)/shard_map/ppermute | solution.py:26
  87.7 9.0 %collective-permute-start.13 = (bf16[64,1280]{1,0:T(8,128)(2,1)S(1)}, bf16[64,1280]{1,0:T(8,128)(2,1)S(1)}, u32[]{:S(2)}, u32[]{:S(2)}) collective-permute-start(bf16[64,1280]{1,0:T(8,128)(2,1)S(1)} %add_convert_fusion.3), channel_id=1, source_target_pairs={{0,8},{8,16},{16,24},{24,0},{1,9},{9,17},{17,25},{25,1},{2,10},{10... | collective-permute-start | bytes 491528 | tf_op jit(solution)/shard_map/ppermute | solution.py:21
  89.4 10.8 %collective-permute-start.15 = (bf16[64,1280]{1,0:T(8,128)(2,1)S(1)}, bf16[64,1280]{1,0:T(8,128)(2,1)S(1)}, u32[]{:S(2)}, u32[]{:S(2)}) collective-permute-start(bf16[64,1280]{1,0:T(8,128)(2,1)S(1)} %add_convert_fusion.2), channel_id=1, source_target_pairs={{0,8},{8,16},{16,24},{24,0},{1,9},{9,17},{17,25},{25,1},{2,10},{10... | collective-permute-start | bytes 491528 | tf_op jit(solution)/shard_map/ppermute | solution.py:21
  91.0 12.7 %collective-permute-start.17 = (bf16[64,1280]{1,0:T(8,128)(2,1)S(1)}, bf16[64,1280]{1,0:T(8,128)(2,1)S(1)}, u32[]{:S(2)}, u32[]{:S(2)}) collective-permute-start(bf16[64,1280]{1,0:T(8,128)(2,1)S(1)} %add_convert_fusion.1), channel_id=1, source_target_pairs={{0,8},{8,16},{16,24},{24,0},{1,9},{9,17},{17,25},{25,1},{2,10},{10... | collective-permute-start | bytes 491528 | tf_op jit(solution)/shard_map/ppermute | solution.py:21
  92.9 12.7 %collective-permute-start.19 = (bf16[64,1280]{1,0:T(8,128)(2,1)S(1)}, bf16[64,1280]{1,0:T(8,128)(2,1)S(1)}, u32[]{:S(2)}, u32[]{:S(2)}) collective-permute-start(bf16[64,1280]{1,0:T(8,128)(2,1)S(1)} %add_convert_fusion), channel_id=1, source_target_pairs={{0,8},{8,16},{16,24},{24,0},{1,9},{9,17},{17,25},{25,1},{2,10},{10... | collective-permute-start | bytes 491528 | tf_op jit(solution)/shard_map/ppermute | solution.py:21

commit v2 on v0

--- a/solution.py
+++ b/solution.py
@@ -1,20 +1,304 @@
+import functools
+import math
+
 import jax
 import jax.numpy as jnp
 from jax import lax
+from jax.experimental import pallas as pl
+from jax.experimental.pallas import tpu as pltpu
 from jax.sharding import PartitionSpec as P
 
 HD = 128
 SPAN = 1024
-
-
 ROPE_BASE = 500000.0
 NORM_EPS = 1e-06
+OUT_CHUNKS = 4
+MIB = 1 << 20
 
 
 def from_behind(value, axis, steps):
     count = lax.axis_size(axis)
     pairs = [(source, (source + steps) % count) for source in range(count)]
     return lax.ppermute(value, axis, pairs)
+
+
+def swap(value, axis, bit):
+    count = lax.axis_size(axis)
+    return lax.ppermute(value, axis, [(source, source ^ bit) for source in range(count)])
+
+
+def norm_rotate_head(head, cosine, sine):
+    head = head * lax.rsqrt(jnp.mean(head * head, axis=-1, keepdims=True) + NORM_EPS)
+    return head * cosine + pltpu.roll(head, HD // 2, 1) * sine
+
+
+def shape(rows, columns, dtype):
+    return jax.ShapeDtypeStruct((rows, columns), dtype)
+
+
+def in_vmem(value):
+    return pltpu.with_memory_space_constraint(value, pltpu.VMEM)
+
+
+def call(kernel, out_shape, mib, flops, moved, **given):
+    return pl.pallas_call(
+        kernel,
+        out_shape=out_shape,
+        compiler_params=pltpu.CompilerParams(vmem_limit_bytes=mib * MIB),
+        cost_estimate=pl.CostEstimate(flops=flops, bytes_accessed=moved, transcendentals=0),
+        **given,
+    )
+
+
+def after(value, *others):
+    return lax.optimization_barrier((value, *others))[0]
+
+
+def piece_positions(start, index, rows, pieces, dims, axis):
+    at = lax.broadcasted_iota(jnp.int32, dims, axis)
+    positions = at % rows + start
+    for order, (shift, flip) in enumerate(pieces):
+        offset = shift + rows * (index ^ flip)
+        positions = positions + jnp.where(at // rows == order, offset, 0)
+    return positions
+
+
+def tables_kernel(rows, block_rows, place, lengths, cosine, sine, allowed):
+    start, index = place[0] * block_rows, place[1]
+    keys = [(shift, flip) for shift in (-block_rows, 0) for flip in range(4)]
+    dims = cosine.shape
+    positions = piece_positions(start, index, rows, keys, dims, 0).astype(jnp.float32)
+    lane = lax.broadcasted_iota(jnp.int32, dims, 1)
+    power = (lane % (HD // 2)).astype(jnp.float32) * (2.0 / HD)
+    angles = positions * jnp.exp(power * -math.log(ROPE_BASE))
+    cosine[...] = jnp.cos(angles)
+    sine[...] = jnp.sin(angles) * jnp.where(lane < HD // 2, -1.0, 1.0)
+    dims = allowed.shape
+    q_pos = piece_positions(start, index, rows, [(0, flip) for flip in (0, 2, 1, 3)], dims, 0)
+    k_pos = piece_positions(start, index, rows, keys, dims, 1)
+    first = q_pos // SPAN * SPAN
+    end = 0
+    for doc in range(lengths.shape[1]):
+        end = end + lengths[0, doc]
+        first = jnp.where(end <= q_pos, jnp.maximum(first, end), first)
+    allowed[...] = jnp.where((k_pos >= first) & (k_pos <= q_pos), 1.0, 0.0)
+
+
+def stacked(pieces):
+    return jnp.concatenate([piece[...] for piece in pieces], axis=0)
+
+
+def project_kernel(x_count, w_count, ranges, *refs):
+    xs, ws, outs = refs[:x_count], refs[x_count : x_count + w_count], refs[x_count + w_count :]
+    rows = stacked(xs)
+    at = 0
+    for w in ws:
+        wide = w.shape[1]
+        total = jnp.dot(rows, w[...], preferred_element_type=jnp.float32)
+        for out, (first, last) in zip(outs, ranges):
+            out[:, at : at + wide] = total[first:last, :].astype(out.dtype)
+        at += wide
+
+
+def project_kv(xs, ws, outs):
+    rows, depth = xs[0].shape
+    wide = sum(w.shape[1] for w in ws)
+    count = len(xs)
+    return call(
+        functools.partial(project_kernel, count, len(ws), [(a, b) for a, b, _ in outs]),
+        [shape(b - a, wide, dtype) for a, b, dtype in outs],
+        8,
+        2 * count * rows * depth * wide,
+        2 * count * rows * depth,
+    )(*xs, *ws)
+
+
+def query_kernel(x_count, last, half, *refs):
+    xs, w = refs[:x_count], refs[x_count]
+    rows = stacked(xs)
+    depth = rows.shape[1]
+    block = 2 * HD
+    part = pl.ds(pl.multiple_of(half[0] * depth, depth), depth)
+    if last:
+        before, cosine, sine, out = refs[x_count + 1 :]
+        piece, whole = xs[0].shape[0], rows.shape[0]
+        order = [pl.ds(whole + piece * flip, piece) for flip in (0, 2, 1, 3)]
+        cosine = jnp.concatenate([cosine[at, :] for at in order], axis=0)
+        sine = jnp.concatenate([sine[at, :] for at in order], axis=0)
+    else:
+        out = refs[x_count + 1]
+    for at in range(0, w.shape[1], block):
+        total = jnp.dot(rows, w[part, at : at + block], preferred_element_type=jnp.float32)
+        if last:
+            total = total + before[:, at : at + block]
+            for head in range(0, block, HD):
+                query = norm_rotate_head(total[:, head : head + HD], cosine, sine)
+                out[:, at + head : at + head + HD] = query.astype(out.dtype)
+        else:
+            out[:, at : at + block] = total
+
+
+def project_query(half, xs, w, *rest):
+    rows, depth = xs[0].shape
+    rows = rows * len(xs)
+    wide = w.shape[1]
+    return call(
+        functools.partial(query_kernel, len(xs), bool(rest)),
+        shape(rows, wide, jnp.bfloat16 if rest else jnp.float32),
+        16,
+        2 * rows * depth * wide,
+        4 * rows * depth,
+        in_specs=[pl.BlockSpec(memory_space=pltpu.SMEM)]
+        + [pl.BlockSpec(memory_space=pltpu.VMEM)] * (len(xs) + 1 + len(rest)),
+    )(half, *xs, w, *rest)
+
+
+def finish(total, cosine, sine, out, at):
+    rows, wide = total.shape
+    keys = wide // 2
+    part = pl.ds(at, rows)
+    for head in range(0, keys, HD):
+        key = norm_rotate_head(total[:, head : head + HD], cosine[part, :], sine[part, :])
+        out[part, head : head + HD] = key.astype(out.dtype)
+    out[part, keys:] = total[:, keys:].astype(out.dtype)
+
+
+def finish_kernel(own_sum_a, own_a, far_a, far_b, early, cosine, sine, out):
+    rows = own_a.shape[0]
+    for index, far in enumerate((far_a, far_b)):
+        at = index * rows
+        total = early[at : at + rows, :].astype(jnp.float32) + far[...].astype(jnp.float32)
+        finish(total, cosine, sine, out, at)
+    finish(own_sum_a[...] + own_a[...].astype(jnp.float32), cosine, sine, out, 2 * rows)
+
+
+def attend_kernel(group, q, done, own_sum_b, own_b, cosine, sine, allowed, out, kv):
+    rows = q.shape[0]
+    ready = done.shape[0]
+    kv[:ready, :] = done[...]
+    finish(own_sum_b[...] + own_b[...].astype(jnp.float32), cosine, sine, kv, ready)
+    keys = kv.shape[1] // 2
+    allow = jnp.concatenate([allowed[...]] * group, axis=0) > 0.5
+    for head in range(0, keys, HD):
+        key = kv[:, head : head + HD]
+        value = kv[:, keys + head : keys + head + HD]
+        at = head * group
+        query = jnp.concatenate([q[:, at + g * HD : at + (g + 1) * HD] for g in range(group)], 0)
+        scores = lax.dot_general(
+            query, key, (((1,), (1,)), ((), ())), preferred_element_type=jnp.float32
+        )
+        weights = jnp.where(allow, jnp.exp(scores * (1.0 / HD**0.5)), 0.0)
+        weights = weights.astype(jnp.bfloat16)
+        total = jnp.sum(weights.astype(jnp.float32), axis=-1, keepdims=True)
+        mixed = jnp.dot(weights, value, preferred_element_type=jnp.float32) / total
+        mixed = mixed.astype(out.dtype)
+        for g in range(group):
+            out[:, at + g * HD : at + (g + 1) * HD] = mixed[g * rows : (g + 1) * rows, :]
+
+
+def out_kernel(first, attended, w, stay, leave):
+    half, wide = stay.shape
+    block = 2 * HD
+    for at in range(0, wide, block):
+        part = pl.ds(first + at, block)
+        total = jnp.dot(attended[...], w[:, part], preferred_element_type=jnp.float32)
+        stay[:, at : at + block] = total[:half]
+        leave[:, at : at + block] = total[half:].astype(leave.dtype)
+
+
+def project_out(attended, w, first, wide):
+    rows, depth = attended.shape
+    return call(
+        functools.partial(out_kernel, first),
+        [shape(rows // 2, wide, jnp.float32), shape(rows // 2, wide, jnp.bfloat16)],
+        16,
+        2 * rows * depth * wide,
+        2 * rows * depth,
+    )(attended, w)
+
+
+def on_four_by_two(inputs, doc_lengths, w_query, w_key, w_value, w_out):
+    own = inputs[0]
+    w_query, w_key, w_value, w_out = w_query[0], w_key[0], w_value[0], w_out[0]
+    rows = own.shape[0]
+    half = w_key.shape[0]
+    group = w_query.shape[1] // w_key.shape[1]
+    ctx, tp = lax.axis_index("ctx"), lax.axis_index("tp")
+    block_rows = rows * lax.axis_size("tp")
+
+    x_far = lax.dynamic_slice_in_dim(own, (1 - ctx) * half, half, 1)
+    far_a = swap(x_far, "ctx", 1)
+    x_near = lax.dynamic_slice_in_dim(after(own, x_far), ctx * half, half, 1)
+    near_b = swap(x_near, "tp", 2)
+    x_near_s = swap(x_near, "tp", 1)
+    x_far_s = swap(x_far, "tp", 1)
+    far_b = swap(far_a, "tp", 2)
+    far_a_s = swap(far_a, "tp", 1)
+    near_b_s = swap(near_b, "tp", 1)
+    far_b_s = swap(far_b, "tp", 1)
+
+    smem = pl.BlockSpec(memory_space=pltpu.SMEM)
+    cosine, sine, allowed = call(
+        functools.partial(tables_kernel, rows, block_rows),
+        [
+            shape(8 * rows, HD, jnp.float32),
+            shape(8 * rows, HD, jnp.float32),
+            shape(4 * rows, 8 * rows, jnp.float32),
+        ],
+        8,
+        1 << 24,
+        1 << 20,
+        in_specs=[smem, smem],
+    )(jnp.stack([ctx, tp]), doc_lengths)
+
+    weights = [in_vmem(w_key), in_vmem(w_value)]
+    own_sum_a, own_sum_b, own_send, far_sum_a = project_kv(
+        [x_near, x_near_s, near_b, near_b_s, far_a, far_a_s],
+        weights,
+        [
+            (0, 2 * rows, jnp.float32),
+            (2 * rows, 4 * rows, jnp.float32),
+            (0, 4 * rows, jnp.bfloat16),
+            (4 * rows, 6 * rows, jnp.bfloat16),
+        ],
+    )
+    early = lax.ppermute(own_send, "ctx", [(0, 1)])
+    own_a = swap(far_sum_a, "ctx", 1)
+    far_sum_b = project_kv([far_b, far_b_s], weights, [(0, 2 * rows, jnp.bfloat16)])[0]
+    own_b = swap(far_sum_b, "ctx", 1)
+    far_c = swap(x_far, "tp", 2)
+    far_c_s = swap(far_c, "tp", 1)
+
+    near = jnp.reshape(ctx, (1,))
+    w_query = in_vmem(w_query)
+    queries = project_query(near, [x_near, near_b, x_near_s, near_b_s], w_query)
+    queries = project_query(
+        1 - near, [x_far, far_c, x_far_s, far_c_s], w_query, queries, cosine, sine
+    )
+
+    kv_shape = shape(6 * rows, own_send.shape[1], jnp.bfloat16)
+    done = call(finish_kernel, kv_shape, 8, 1 << 24, 1 << 20)(
+        own_sum_a, own_a, far_sum_a, far_sum_b, early, cosine, sine
+    )
+    attended = call(
+        functools.partial(attend_kernel, group),
+        shape(4 * rows, queries.shape[1], jnp.bfloat16),
+        16,
+        8 * rows * 8 * rows * queries.shape[1],
+        1 << 20,
+        scratch_shapes=[pltpu.VMEM((8 * rows, own_send.shape[1]), jnp.bfloat16)],
+    )(queries, done, own_sum_b, own_b, cosine, sine, allowed)
+
+    w_out = in_vmem(w_out)
+    wide = w_out.shape[1] // OUT_CHUNKS
+    parts = []
+    for chunk in range(OUT_CHUNKS):
+        stay, leave = project_out(attended, w_out, chunk * wide, wide)
+        stay = stay + swap(leave, "tp", 1).astype(jnp.float32)
+        arrived = swap(stay[rows:].astype(jnp.bfloat16), "tp", 2)
+        mixed = (stay[:rows] + arrived.astype(jnp.float32)).astype(jnp.bfloat16)
+        parts.append(from_behind(mixed, "pipe", 1))
+    return jnp.concatenate(parts, axis=1)[None]
 
 
 def doc_index(positions, lengths):
@@ -61,7 +345,7 @@
     return (numerator, denominator)
 
 
-def on_device(inputs, doc_lengths, w_query, w_key, w_value, w_out):
+def on_any(inputs, doc_lengths, w_query, w_key, w_value, w_out):
     tok_rows = lax.all_gather(inputs[0], "tp", axis=0, tiled=True)
     block_rows = tok_rows.shape[0]
     q_heads = w_query.shape[2] // HD
@@ -109,8 +393,7 @@
         scatter_dimension=0,
         tiled=True,
     )
-    received = from_behind(mixed, "pipe", 1)
-    return received[None]
+    return from_behind(mixed, "pipe", 1)[None]
 
 
 def solution(mesh):
@@ -123,6 +406,11 @@
         P("pipe", "tp", None),
     )
     out_specs = P("pipe", ("ctx", "tp"), None)
+    paired = mesh.shape["ctx"] == 2 and mesh.shape["tp"] == 4
     return jax.shard_map(
-        on_device, mesh=mesh, in_specs=in_specs, out_specs=out_specs, check_vma=False
-    )
+        on_four_by_two if paired else on_any,
+        mesh=mesh,
+        in_specs=in_specs,
+        out_specs=out_specs,
+        check_vma=False,
+    )

time: 187 us -> 79.6 us (0.43)
  waiting for transfers between devices: 129 us -> 33.5 us
  starting transfers between devices: 1.56 us -> 25.3 us
  matrix products: 15.5 us -> 0 us
  Pallas kernels: 0 us -> 14.4 us
  between operations: 13.3 us -> 0.29 us
  local copies, waits for them, and re-layouts: 14.8 us -> 4.58 us
  blocking collectives: 8.85 us -> 0 us
    all_gather x2 -> x0, waiting for transfers between devices: 76.9 us -> none  [the longest x1 63.6 us: on_device(): lax.all_gather(stacked_weights, 'ctx', axis=1, tiled=True)]
    reduce_scatter x1 -> x0, waiting for transfers between devices: 34.8 us -> none  [on_device(): lax.psum_scatter(jnp.dot(attended, w_out[0], preferred_element_type=jnp.f...]
    ppermute x0 -> x21, waiting for transfers between devices: none -> 27 us  [the longest x20 27 us: swap(): lax.ppermute(value, axis, [(source, source ^ bit) for source in range(cou...]
    ppermute x0 -> x21, starting transfers between devices: none -> 18.8 us  [the longest x20 15.3 us: swap(): lax.ppermute(value, axis, [(source, source ^ bit) for source in range(cou...]
    dot_general x5 -> x0, matrix products: 15.5 us -> none  [the longest x1 6.27 us: on_device(): queries = jnp.dot(tok_rows, w_query[0], preferred_element_type=jnp.float32)]
    pallas_call x0 -> x11, Pallas kernels: none -> 14.4 us  [the longest x2 3.97 us: project_kv(): call(functools.partial(project_kernel, count, len(ws), [(a, b) for a, b,...]
    unnamed x12 -> x16, local copies, waits for them, and re-layouts: 14.8 us -> 3.73 us
    ppermute x1 -> x4, waiting for transfers between devices: 17 us -> 6.47 us  [from_behind(): return lax.ppermute(value, axis, pairs)]
  transfers between devices with their start and end apart: 4 -> 25, of which waited for: 4 -> 11; matrix products, arithmetic and copies ran while one was open for 12% -> 1% of each run, Pallas kernels for 0% -> 16%
where the time goes in v2:
time: 79.6 us; the launch traced here: 79.3 us
  waiting for transfers between devices  33.5 us (42%)
  starting transfers between devices  25.3 us (32%)
  Pallas kernels  14.4 us (18%)
  local copies, waits for them, and re-layouts  4.58 us (6%)
  other arithmetic  1.3 us (2%)
    ppermute x20, waiting for transfers between devices, swap(): lax.ppermute(value, axis, [(source, source ^ bit) for source in range(cou...  27 us
    ppermute x20, starting transfers between devices, swap(): lax.ppermute(value, axis, [(source, source ^ bit) for source in range(cou...  15.3 us
    ppermute x4, starting transfers between devices, from_behind(): return lax.ppermute(value, axis, pairs)  6.52 us
    ppermute x4, waiting for transfers between devices, from_behind(): return lax.ppermute(value, axis, pairs)  6.47 us
    pallas_call x2, Pallas kernels, project_kv(): call(functools.partial(project_kernel, count, len(ws), [(a, b) for a, b,...  3.97 us
    pallas_call x2, Pallas kernels, project_query(): call(functools.partial(query_kernel, len(xs), bool(rest)), shape(rows, wi...  3.88 us
    unnamed x16, local copies, waits for them, and re-layouts  3.73 us
    ppermute x1, starting transfers between devices, on_four_by_two(): early = lax.ppermute(own_send, 'ctx', [(0, 1)])  3.48 us
  transfers between devices with their start and end apart: 25, of which 11 were waited for; matrix products, arithmetic and copies ran while one was open for 1% of the time, Pallas kernels for 16%

profile of v2, /device:TPU:0, one launch (start us, length us, event | category | flops | bytes accessed | tf_op | source)
XLA Modules:
  0.0 79.3 jit_solution(11811059659653336247)
XLA Ops:
  0.0 1.1 %copy-done = bf16[1,64,5120]{2,1,0:T(8,128)(2,1)S(1)} copy-done((bf16[1,64,5120]{2,1,0:T(8,128)(2,1)S(1)}, bf16[1,64,5120]{2,1,0:T(8,128)(2,1)}, u32[]{:S(2)}) %copy-start) | copy-done | bytes 655384
  1.1 0.7 dynamic-slice_bitcast_fusion.refs_0_
  1.8 2.9 %collective-permute-start.6 = (bf16[64,2560]{1,0:T(8,128)(2,1)}, bf16[64,2560]{1,0:T(8,128)(2,1)}, u32[]{:S(2)}, u32[]{:S(2)}) collective-permute-start(bf16[64,2560]{1,0:T(8,128)(2,1)} %dynamic-slice_bitcast_fusion.refs_0_), channel_id=1, source_target_pairs={{0,4},{4,0},{1,5},{5,1},{2,6},{6,2},{3,7},{7,3},{8,12},{12,8},{9,1... | collective-permute-start | bytes 983048 | tf_op jit(solution)/shard_map/ppermute | solution.py:27
  4.8 1.6 %collective-permute-start.3 = (bf16[64,2560]{1,0:T(8,128)(2,1)S(1)}, bf16[64,2560]{1,0:T(8,128)(2,1)S(1)}, u32[]{:S(2)}, u32[]{:S(2)}) collective-permute-start(bf16[64,2560]{1,0:T(8,128)(2,1)S(1)} %constant_dynamic-slice_fusion.refs_0_), channel_id=1, source_target_pairs={{0,2},{1,3},{2,0},{3,1},{4,6},{5,7},{6,4},{7,5},{8,10},{9,11},{10,... | collective-permute-start | bytes 983048 | tf_op jit(solution)/shard_map/ppermute | solution.py:27
  6.4 6.4 %collective-permute-done.6.refs_4_ = bf16[64,2560]{1,0:T(8,128)(2,1)} collective-permute-done((bf16[64,2560]{1,0:T(8,128)(2,1)}, bf16[64,2560]{1,0:T(8,128)(2,1)}, u32[]{:S(2)}, u32[]{:S(2)}) %collective-permute-start.6) | collective-permute-done | bytes 327712 | tf_op jit(solution)/shard_map/ppermute | solution.py:27
  12.8 1.8 %collective-permute-start.9 = (bf16[64,2560]{1,0:T(8,128)(2,1)}, bf16[64,2560]{1,0:T(8,128)(2,1)}, u32[]{:S(2)}, u32[]{:S(2)}) collective-permute-start(bf16[64,2560]{1,0:T(8,128)(2,1)} %collective-permute-done.6.refs_4_), channel_id=1, source_target_pairs={{0,2},{1,3},{2,0},{3,1},{4,6},{5,7},{6,4},{7,5},{8,10},{9,11},{10,... | collective-permute-start | bytes 983048 | tf_op jit(solution)/shard_map/ppermute | solution.py:27
  14.6 0.0 collective-permute-start.4
  14.6 0.3 collective-permute-start
  14.8 0.0 collective-permute-done.3.refs_1_.refs_2_
  14.8 0.3 collective-permute-start.5
  15.1 0.3 collective-permute-start.7
  15.3 8.4 %collective-permute-done.9.refs_0_ = bf16[64,2560]{1,0:T(8,128)(2,1)} collective-permute-done((bf16[64,2560]{1,0:T(8,128)(2,1)}, bf16[64,2560]{1,0:T(8,128)(2,1)}, u32[]{:S(2)}, u32[]{:S(2)}) %collective-permute-start.9) | collective-permute-done | bytes 327712 | tf_op jit(solution)/shard_map/ppermute | solution.py:27
  23.8 0.0 collective-permute-start.10
  23.8 0.0 collective-permute-done.4.refs_2_.refs_1_
  23.8 0.5 collective-permute-start.1
  24.3 4.8 %collective-permute-done.refs_1_ = bf16[64,2560]{1,0:T(8,128)(2,1)} collective-permute-done((bf16[64,2560]{1,0:T(8,128)(2,1)}, bf16[64,2560]{1,0:T(8,128)(2,1)}, u32[]{:S(2)}, u32[]{:S(2)}) %collective-permute-start) | collective-permute-done | bytes 327712 | tf_op jit(solution)/shard_map/ppermute | solution.py:27
  29.0 0.0 collective-permute-start.2
  29.0 0.0 collective-permute-done.5.refs_3_
  29.0 0.0 collective-permute-done.7.refs_5_
  29.1 0.0 copy-start.3
  29.1 1.3 %copy-done.3 = bf16[1,2560,256]{2,1,0:T(8,128)(2,1)S(1)} copy-done((bf16[1,2560,256]{2,1,0:T(8,128)(2,1)S(1)}, bf16[1,2560,256]{2,1,0:T(8,128)(2,1)}, u32[]{:S(2)}) %copy-start.3) | copy-done | bytes 1310744
  30.4 2.4 %shard_map.67 = (f32[128,512]{1,0:T(8,128)S(1)}, f32[128,512]{1,0:T(8,128)S(1)}, bf16[256,512]{1,0:T(8,128)(2,1)S(1)}, bf16[128,512]{1,0:T(8,128)(2,1)S(1)}) custom-call(bf16[64,2560]{1,0:T(8,128)(2,1)S(1)} %constant_dynamic-slice_fusion.refs_0_, bf16[64,2560]{1,0:T(8,128)(2,1)S(1)} %collective-permute-done.4.refs_2_.refs_1_, ...), custom_call_target="tpu_custom_call" | custom-call | flops 1006632960 | bytes 1966080 | tf_op jit(solution)/shard_map/pallas_call | solution.py:107
  32.8 3.5 %collective-permute-start.11 = (bf16[256,512]{1,0:T(8,128)(2,1)S(1)}, bf16[256,512]{1,0:T(8,128)(2,1)S(1)}, u32[]{:S(2)}, u32[]{:S(2)}) collective-permute-start(bf16[256,512]{1,0:T(8,128)(2,1)S(1)} %get-tuple-element.26), channel_id=1, source_target_pairs={{0,4},{1,5},{2,6},{3,7},{8,12},{9,13},{10,14},{11,15},{16,20},{17,... | collective-permute-start | bytes 786440 | tf_op jit(solution)/shard_map/ppermute | solution.py:265
  36.3 0.1 pad_add_fusion.place
  36.3 1.8 %shard_map.65 = (f32[512,128]{1,0:T(8,128)S(1)}, f32[512,128]{1,0:T(8,128)S(1)}, f32[256,512]{1,0:T(8,128)S(1)}) custom-call(s32[2]{0:T(128)S(1)} %pad_add_fusion.place, s32[1,8]{1,0:T(1,128)S(1)} %copy-done.5), custom_call_target="tpu_custom_call" | custom-call | flops 16777216 | bytes 1048576 | tf_op jit(solution)/shard_map/pallas_call | solution.py:241
  38.2 0.1 collective-permute-start.8
  38.3 0.0 copy-start.4
  38.3 1.3 %copy-done.4 = bf16[1,2560,256]{2,1,0:T(8,128)(2,1)S(1)} copy-done((bf16[1,2560,256]{2,1,0:T(8,128)(2,1)S(1)}, bf16[1,2560,256]{2,1,0:T(8,128)(2,1)}, u32[]{:S(2)}) %copy-start.4) | copy-done | bytes 1310744
  39.6 1.6 %shard_map.68.far_b = bf16[128,512]{1,0:T(8,128)(2,1)S(1)} custom-call(bf16[64,2560]{1,0:T(8,128)(2,1)} %collective-permute-done.9.refs_0_, bf16[64,2560]{1,0:T(8,128)(2,1)} %collective-permute-done.10.refs_1_, bf16[2560,256]{1,0:T(8,128)(2,1)S(1)} %bitcast.21, bf16[2560,256]{1,0:T(8,128)(2,1)S(1)} %bitcast.23), custom_call_target="tpu_custom_call" | custom-call | flops 335544320 | bytes 655360 | tf_op jit(solution)/shard_map/pallas_call | solution.py:107
  41.2 2.1 %collective-permute-start.12 = (bf16[128,512]{1,0:T(8,128)(2,1)S(1)}, bf16[128,512]{1,0:T(8,128)(2,1)S(1)}, u32[]{:S(2)}, u32[]{:S(2)}) collective-permute-start(bf16[128,512]{1,0:T(8,128)(2,1)S(1)} %shard_map.68.far_b), channel_id=1, source_target_pairs={{0,4},{4,0},{1,5},{5,1},{2,6},{6,2},{3,7},{7,3},{8,12},{12,8},{9,1... | collective-permute-start | bytes 393224 | tf_op jit(solution)/shard_map/ppermute | solution.py:27
  43.3 1.2 %shard_map.64.refs_5_ = f32[256,768]{1,0:T(8,128)S(1)} custom-call(s32[1]{0:T(128)} %bitcast.half, bf16[64,2560]{1,0:T(8,128)(2,1)S(1)} %constant_dynamic-slice_fusion.refs_0_, bf16[64,2560]{1,0:T(8,128)(2,1)S(1)} %collective-permute-done.3.refs_1_.refs_2_, bf16[64,2560]{1,0:T(8,128)(2,1)S(1)} %collective-permute-done.4.refs_2_.refs_1_, ...), custom_call_target="tpu_custom_call" | custom-call | flops 1006632960 | bytes 2621440 | tf_op jit(solution)/shard_map/pallas_call | solution.py:145
  44.5 0.0 slice-start.1
  44.5 2.7 %shard_map.66.q = bf16[256,768]{1,0:T(8,128)(2,1)S(1)} custom-call(s32[1]{0:T(128)S(6)} %sub.6.half, bf16[64,2560]{1,0:T(8,128)(2,1)} %dynamic-slice_bitcast_fusion.refs_0_, bf16[64,2560]{1,0:T(8,128)(2,1)} %collective-permute-done.refs_1_, bf16[64,2560]{1,0:T(8,128)(2,1)S(1)} %collective-permute-done.1.refs_2_, ...), custom_call_target="tpu_custom_call" | custom-call | flops 1006632960 | bytes 2621440 | tf_op jit(solution)/shard_map/pallas_call | solution.py:145
  47.2 0.6 shard_map.69.done
  47.8 0.3 collective-permute-done.12.own_b
  48.1 1.3 %shard_map.70.attended = bf16[256,768]{1,0:T(8,128)(2,1)S(1)} custom-call(bf16[256,768]{1,0:T(8,128)(2,1)S(1)} %shard_map.66.q, bf16[384,512]{1,0:T(8,128)(2,1)S(1)} %shard_map.69.done, f32[128,512]{1,0:T(8,128)S(1)} %get-tuple-element.27.own_sum_b, bf16[128,512]{1,0:T(8,128)(2,1)S(1)} %collective-permute-done.12.own_b, ...), custom_call_target="tpu_custom_call" | custom-call | flops 201326592 | bytes 1048576 | tf_op jit(solution)/shard_map/pallas_call | solution.py:283
  49.4 0.7 shard_map.71
  50.1 0.1 collective-permute-start.13
  50.2 0.7 shard_map.72
  50.9 0.6 collective-permute-start.16
  51.5 0.7 shard_map.73
  52.2 0.1 collective-permute-start.19
  52.2 0.7 shard_map.74
  52.9 0.6 collective-permute-start.22
  53.5 0.1 convert_add_fusion.3
  53.6 1.6 %collective-permute-start.14 = (bf16[64,1280]{1,0:T(8,128)(2,1)S(1)}, bf16[64,1280]{1,0:T(8,128)(2,1)S(1)}, u32[]{:S(2)}, u32[]{:S(2)}) collective-permute-start(bf16[64,1280]{1,0:T(8,128)(2,1)S(1)} %slice.63), channel_id=1, source_target_pairs={{0,2},{1,3},{2,0},{3,1},{4,6},{5,7},{6,4},{7,5},{8,10},{9,11},{10,... | collective-permute-start | bytes 491528 | tf_op jit(solution)/shard_map/ppermute | solution.py:27
  55.2 0.1 convert_add_fusion.2
  55.3 0.6 collective-permute-start.17
  55.8 0.1 convert_add_fusion.1
  55.9 1.6 %collective-permute-start.20 = (bf16[64,1280]{1,0:T(8,128)(2,1)S(1)}, bf16[64,1280]{1,0:T(8,128)(2,1)S(1)}, u32[]{:S(2)}, u32[]{:S(2)}) collective-permute-start(bf16[64,1280]{1,0:T(8,128)(2,1)S(1)} %slice.61), channel_id=1, source_target_pairs={{0,2},{1,3},{2,0},{3,1},{4,6},{5,7},{6,4},{7,5},{8,10},{9,11},{10,... | collective-permute-start | bytes 491528 | tf_op jit(solution)/shard_map/ppermute | solution.py:27
  57.5 0.1 convert_add_fusion
  57.6 0.6 collective-permute-start.23
  58.2 2.5 %collective-permute-done.14 = bf16[64,1280]{1,0:T(8,128)(2,1)S(1)} collective-permute-done((bf16[64,1280]{1,0:T(8,128)(2,1)S(1)}, bf16[64,1280]{1,0:T(8,128)(2,1)S(1)}, u32[]{:S(2)}, u32[]{:S(2)}) %collective-permute-start.14) | collective-permute-done | bytes 163872 | tf_op jit(solution)/shard_map/ppermute | solution.py:27
  60.8 1.6 %collective-permute-start.15 = (bf16[64,1280]{1,0:T(8,128)(2,1)S(1)}, bf16[64,1280]{1,0:T(8,128)(2,1)S(1)}, u32[]{:S(2)}, u32[]{:S(2)}) collective-permute-start(bf16[64,1280]{1,0:T(8,128)(2,1)S(1)} %fusion.3), channel_id=1, source_target_pairs={{0,8},{8,16},{16,24},{24,0},{1,9},{9,17},{17,25},{25,1},{2,10},{10... | collective-permute-start | bytes 491528 | tf_op jit(solution)/shard_map/ppermute | solution.py:22
  62.4 1.8 %collective-permute-done.17 = bf16[64,1280]{1,0:T(8,128)(2,1)S(1)} collective-permute-done((bf16[64,1280]{1,0:T(8,128)(2,1)S(1)}, bf16[64,1280]{1,0:T(8,128)(2,1)S(1)}, u32[]{:S(2)}, u32[]{:S(2)}) %collective-permute-start.17) | collective-permute-done | bytes 163872 | tf_op jit(solution)/shard_map/ppermute | solution.py:27
  64.3 1.6 %collective-permute-start.18 = (bf16[64,1280]{1,0:T(8,128)(2,1)S(1)}, bf16[64,1280]{1,0:T(8,128)(2,1)S(1)}, u32[]{:S(2)}, u32[]{:S(2)}) collective-permute-start(bf16[64,1280]{1,0:T(8,128)(2,1)S(1)} %fusion.2), channel_id=1, source_target_pairs={{0,8},{8,16},{16,24},{24,0},{1,9},{9,17},{17,25},{25,1},{2,10},{10... | collective-permute-start | bytes 491528 | tf_op jit(solution)/shard_map/ppermute | solution.py:22
  65.9 1.8 %collective-permute-done.20 = bf16[64,1280]{1,0:T(8,128)(2,1)S(1)} collective-permute-done((bf16[64,1280]{1,0:T(8,128)(2,1)S(1)}, bf16[64,1280]{1,0:T(8,128)(2,1)S(1)}, u32[]{:S(2)}, u32[]{:S(2)}) %collective-permute-start.20) | collective-permute-done | bytes 163872 | tf_op jit(solution)/shard_map/ppermute | solution.py:27
  67.8 1.6 %collective-permute-start.21 = (bf16[64,1280]{1,0:T(8,128)(2,1)S(1)}, bf16[64,1280]{1,0:T(8,128)(2,1)S(1)}, u32[]{:S(2)}, u32[]{:S(2)}) collective-permute-start(bf16[64,1280]{1,0:T(8,128)(2,1)S(1)} %fusion.1), channel_id=1, source_target_pairs={{0,8},{8,16},{16,24},{24,0},{1,9},{9,17},{17,25},{25,1},{2,10},{10... | collective-permute-start | bytes 491528 | tf_op jit(solution)/shard_map/ppermute | solution.py:22
  69.4 0.9 %collective-permute-done.23 = bf16[64,1280]{1,0:T(8,128)(2,1)S(1)} collective-permute-done((bf16[64,1280]{1,0:T(8,128)(2,1)S(1)}, bf16[64,1280]{1,0:T(8,128)(2,1)S(1)}, u32[]{:S(2)}, u32[]{:S(2)}) %collective-permute-start.23) | collective-permute-done | bytes 163872 | tf_op jit(solution)/shard_map/ppermute | solution.py:27
  70.4 1.6 %collective-permute-start.24 = (bf16[64,1280]{1,0:T(8,128)(2,1)S(1)}, bf16[64,1280]{1,0:T(8,128)(2,1)S(1)}, u32[]{:S(2)}, u32[]{:S(2)}) collective-permute-start(bf16[64,1280]{1,0:T(8,128)(2,1)S(1)} %fusion), channel_id=1, source_target_pairs={{0,8},{8,16},{16,24},{24,0},{1,9},{9,17},{17,25},{25,1},{2,10},{10... | collective-permute-start | bytes 491528 | tf_op jit(solution)/shard_map/ppermute | solution.py:22
  72.0 0.4 collective-permute-done.18
  72.4 3.5 %collective-permute-done.21 = bf16[64,1280]{1,0:T(8,128)(2,1)S(1)} collective-permute-done((bf16[64,1280]{1,0:T(8,128)(2,1)S(1)}, bf16[64,1280]{1,0:T(8,128)(2,1)S(1)}, u32[]{:S(2)}, u32[]{:S(2)}) %collective-permute-start.21) | collective-permute-done | bytes 163872 | tf_op jit(solution)/shard_map/ppermute | solution.py:22
  75.9 2.6 %collective-permute-done.24 = bf16[64,1280]{1,0:T(8,128)(2,1)S(1)} collective-permute-done((bf16[64,1280]{1,0:T(8,128)(2,1)S(1)}, bf16[64,1280]{1,0:T(8,128)(2,1)S(1)}, u32[]{:S(2)}, u32[]{:S(2)}) %collective-permute-start.24) | collective-permute-done | bytes 163872 | tf_op jit(solution)/shard_map/ppermute | solution.py:22
  78.5 0.9 %maximum_bitcast_fusion = bf16[1,64,5120]{2,1,0:T(8,128)(2,1)} fusion(bf16[64,1280]{1,0:T(8,128)(2,1)S(1)} %collective-permute-done.24, bf16[64,1280]{1,0:T(8,128)(2,1)S(1)} %collective-permute-done.21, bf16[64,1280]{1,0:T(8,128)(2,1)S(1)} %collective-permute-done.18, bf16[64,1280]{1,0:T(8,128)(2,1)S(1)} %collective-permute-done.15), kind=kLoop, calls=%fused_computation | loop fusion | flops 2621440 | bytes 1310720 | tf_op jit(solution)/shard_map/broadcast_in_dim | solution.py:301
  (30 shorter events, 0.3 us)
Async XLA Ops:
  0.0 1.1 %copy-start = (bf16[1,64,5120]{2,1,0:T(8,128)(2,1)S(1)}, bf16[1,64,5120]{2,1,0:T(8,128)(2,1)}, u32[]{:S(2)}) copy-start(bf16[1,64,5120]{2,1,0:T(8,128)(2,1)} %param.6) | copy-start | bytes 1966084
  0.0 29.0 %copy-start.2 = (bf16[1,2560,256]{2,1,0:T(8,128)(2,1)S(1)}, bf16[1,2560,256]{2,1,0:T(8,128)(2,1)}, u32[]{:S(2)}) copy-start(bf16[1,2560,256]{2,1,0:T(8,128)(2,1)} %param.9) | copy-start | bytes 3932164
  1.8 11.0 %collective-permute-start.6 = (bf16[64,2560]{1,0:T(8,128)(2,1)}, bf16[64,2560]{1,0:T(8,128)(2,1)}, u32[]{:S(2)}, u32[]{:S(2)}) collective-permute-start(bf16[64,2560]{1,0:T(8,128)(2,1)} %dynamic-slice_bitcast_fusion.refs_0_), channel_id=1, source_target_pairs={{0,4},{4,0},{1,5},{5,1},{2,6},{6,2},{3,7},{7,3},{8,12},{12,8},{9,1... | collective-permute-start | bytes 983048 | tf_op jit(solution)/shard_map/ppermute | solution.py:27
  4.8 31.6 %copy-start.5 = (s32[1,8]{1,0:T(1,128)S(1)}, s32[1,8]{1,0:T(1,128)}, u32[]{:S(2)}) copy-start(s32[1,8]{1,0:T(1,128)} %lengths.1) | copy-start | bytes 100
  4.8 10.0 %collective-permute-start.3 = (bf16[64,2560]{1,0:T(8,128)(2,1)S(1)}, bf16[64,2560]{1,0:T(8,128)(2,1)S(1)}, u32[]{:S(2)}, u32[]{:S(2)}) collective-permute-start(bf16[64,2560]{1,0:T(8,128)(2,1)S(1)} %constant_dynamic-slice_fusion.refs_0_), channel_id=1, source_target_pairs={{0,2},{1,3},{2,0},{3,1},{4,6},{5,7},{6,4},{7,5},{8,10},{9,11},{10,... | collective-permute-start | bytes 983048 | tf_op jit(solution)/shard_map/ppermute | solution.py:27
  12.8 11.0 %collective-permute-start.9 = (bf16[64,2560]{1,0:T(8,128)(2,1)}, bf16[64,2560]{1,0:T(8,128)(2,1)}, u32[]{:S(2)}, u32[]{:S(2)}) collective-permute-start(bf16[64,2560]{1,0:T(8,128)(2,1)} %collective-permute-done.6.refs_4_), channel_id=1, source_target_pairs={{0,2},{1,3},{2,0},{3,1},{4,6},{5,7},{6,4},{7,5},{8,10},{9,11},{10,... | collective-permute-start | bytes 983048 | tf_op jit(solution)/shard_map/ppermute | solution.py:27
  14.6 9.2 %collective-permute-start.4 = (bf16[64,2560]{1,0:T(8,128)(2,1)S(1)}, bf16[64,2560]{1,0:T(8,128)(2,1)S(1)}, u32[]{:S(2)}, u32[]{:S(2)}) collective-permute-start(bf16[64,2560]{1,0:T(8,128)(2,1)S(1)} %constant_dynamic-slice_fusion.refs_0_), channel_id=1, source_target_pairs={{0,1},{1,0},{2,3},{3,2},{4,5},{5,4},{6,7},{7,6},{8,9},{9,8},{10,11... | collective-permute-start | bytes 983048 | tf_op jit(solution)/shard_map/ppermute | solution.py:27
  14.6 14.5 %collective-permute-start = (bf16[64,2560]{1,0:T(8,128)(2,1)}, bf16[64,2560]{1,0:T(8,128)(2,1)}, u32[]{:S(2)}, u32[]{:S(2)}) collective-permute-start(bf16[64,2560]{1,0:T(8,128)(2,1)} %dynamic-slice_bitcast_fusion.refs_0_), channel_id=1, source_target_pairs={{0,2},{1,3},{2,0},{3,1},{4,6},{5,7},{6,4},{7,5},{8,10},{9,11},{10,... | collective-permute-start | bytes 983048 | tf_op jit(solution)/shard_map/ppermute | solution.py:27
  14.8 14.2 %collective-permute-start.5 = (bf16[64,2560]{1,0:T(8,128)(2,1)S(1)}, bf16[64,2560]{1,0:T(8,128)(2,1)S(1)}, u32[]{:S(2)}, u32[]{:S(2)}) collective-permute-start(bf16[64,2560]{1,0:T(8,128)(2,1)S(1)} %collective-permute-done.3.refs_1_.refs_2_), channel_id=1, source_target_pairs={{0,1},{1,0},{2,3},{3,2},{4,5},{5,4},{6,7},{7,6},{8,9},{9,8},{10,11... | collective-permute-start | bytes 983048 | tf_op jit(solution)/shard_map/ppermute | solution.py:27
  15.1 14.0 %collective-permute-start.7 = (bf16[64,2560]{1,0:T(8,128)(2,1)}, bf16[64,2560]{1,0:T(8,128)(2,1)}, u32[]{:S(2)}, u32[]{:S(2)}) collective-permute-start(bf16[64,2560]{1,0:T(8,128)(2,1)} %collective-permute-done.6.refs_4_), channel_id=1, source_target_pairs={{0,1},{1,0},{2,3},{3,2},{4,5},{5,4},{6,7},{7,6},{8,9},{9,8},{10,11... | collective-permute-start | bytes 983048 | tf_op jit(solution)/shard_map/ppermute | solution.py:27
  23.8 14.5 %collective-permute-start.10 = (bf16[64,2560]{1,0:T(8,128)(2,1)}, bf16[64,2560]{1,0:T(8,128)(2,1)}, u32[]{:S(2)}, u32[]{:S(2)}) collective-permute-start(bf16[64,2560]{1,0:T(8,128)(2,1)} %collective-permute-done.9.refs_0_), channel_id=1, source_target_pairs={{0,1},{1,0},{2,3},{3,2},{4,5},{5,4},{6,7},{7,6},{8,9},{9,8},{10,11... | collective-permute-start | bytes 983048 | tf_op jit(solution)/shard_map/ppermute | solution.py:27
  23.8 20.7 %collective-permute-start.1 = (bf16[64,2560]{1,0:T(8,128)(2,1)}, bf16[64,2560]{1,0:T(8,128)(2,1)S(1)}, u32[]{:S(2)}, u32[]{:S(2)}) collective-permute-start(bf16[64,2560]{1,0:T(8,128)(2,1)} %dynamic-slice_bitcast_fusion.refs_0_), channel_id=1, source_target_pairs={{0,1},{1,0},{2,3},{3,2},{4,5},{5,4},{6,7},{7,6},{8,9},{9,8},{10,11... | collective-permute-start | bytes 983048 | tf_op jit(solution)/shard_map/ppermute | solution.py:27
  29.0 15.4 %collective-permute-start.2 = (bf16[64,2560]{1,0:T(8,128)(2,1)}, bf16[64,2560]{1,0:T(8,128)(2,1)S(1)}, u32[]{:S(2)}, u32[]{:S(2)}) collective-permute-start(bf16[64,2560]{1,0:T(8,128)(2,1)} %collective-permute-done.refs_1_), channel_id=1, source_target_pairs={{0,1},{1,0},{2,3},{3,2},{4,5},{5,4},{6,7},{7,6},{8,9},{9,8},{10,11... | collective-permute-start | bytes 983048 | tf_op jit(solution)/shard_map/ppermute | solution.py:27
  29.1 1.3 %copy-start.3 = (bf16[1,2560,256]{2,1,0:T(8,128)(2,1)S(1)}, bf16[1,2560,256]{2,1,0:T(8,128)(2,1)}, u32[]{:S(2)}) copy-start(bf16[1,2560,256]{2,1,0:T(8,128)(2,1)} %param.10) | copy-start | bytes 3932164
  30.4 12.9 %copy-start.1 = (bf16[1,5120,768]{2,1,0:T(8,128)(2,1)S(1)}, bf16[1,5120,768]{2,1,0:T(8,128)(2,1)}, u32[]{:S(2)}) copy-start(bf16[1,5120,768]{2,1,0:T(8,128)(2,1)} %param.8) | copy-start | bytes 23592964
  32.8 14.4 %collective-permute-start.11 = (bf16[256,512]{1,0:T(8,128)(2,1)S(1)}, bf16[256,512]{1,0:T(8,128)(2,1)S(1)}, u32[]{:S(2)}, u32[]{:S(2)}) collective-permute-start(bf16[256,512]{1,0:T(8,128)(2,1)S(1)} %get-tuple-element.26), channel_id=1, source_target_pairs={{0,4},{1,5},{2,6},{3,7},{8,12},{9,13},{10,14},{11,15},{16,20},{17,... | collective-permute-start | bytes 786440 | tf_op jit(solution)/shard_map/ppermute | solution.py:265
  38.2 9.0 %collective-permute-start.8 = (bf16[128,512]{1,0:T(8,128)(2,1)S(1)}, bf16[128,512]{1,0:T(8,128)(2,1)S(1)}, u32[]{:S(2)}, u32[]{:S(2)}) collective-permute-start(bf16[128,512]{1,0:T(8,128)(2,1)S(1)} %get-tuple-element.25.far_a), channel_id=1, source_target_pairs={{0,4},{4,0},{1,5},{5,1},{2,6},{6,2},{3,7},{7,3},{8,12},{12,8},{9,1... | collective-permute-start | bytes 393224 | tf_op jit(solution)/shard_map/ppermute | solution.py:27
  38.3 1.3 %copy-start.4 = (bf16[1,2560,256]{2,1,0:T(8,128)(2,1)S(1)}, bf16[1,2560,256]{2,1,0:T(8,128)(2,1)}, u32[]{:S(2)}) copy-start(bf16[1,2560,256]{2,1,0:T(8,128)(2,1)} %param.10) | copy-start | bytes 3932164
  41.2 6.9 %collective-permute-start.12 = (bf16[128,512]{1,0:T(8,128)(2,1)S(1)}, bf16[128,512]{1,0:T(8,128)(2,1)S(1)}, u32[]{:S(2)}, u32[]{:S(2)}) collective-permute-start(bf16[128,512]{1,0:T(8,128)(2,1)S(1)} %shard_map.68.far_b), channel_id=1, source_target_pairs={{0,4},{4,0},{1,5},{5,1},{2,6},{6,2},{3,7},{7,3},{8,12},{12,8},{9,1... | collective-permute-start | bytes 393224 | tf_op jit(solution)/shard_map/ppermute | solution.py:27
  43.3 6.1 %slice-start = ((s8[7864320]{0:T(1024)(128)(4,1)}), s8[4194304]{0:T(1024)(128)(4,1)S(1)}, s32[]{:S(2)}) async-start(s8[7864320]{0:T(1024)(128)(4,1)} %bitcast.12), calls=%async_computation | async-start | bytes 8388608
  44.5 4.9 %slice-start.1 = ((s8[7864320]{0:T(1024)(128)(4,1)}), s8[3670016]{0:T(1024)(128)(4,1)S(1)}, s32[]{:S(2)}) async-start(s8[7864320]{0:T(1024)(128)(4,1)} %bitcast.12), calls=%async_computation.1 | async-start | bytes 7340032
  50.1 3.4 %collective-permute-start.13 = (bf16[128,1280]{1,0:T(8,128)(2,1)S(1)}, bf16[128,1280]{1,0:T(8,128)(2,1)S(1)}, u32[]{:S(2)}, u32[]{:S(2)}) collective-permute-start(bf16[128,1280]{1,0:T(8,128)(2,1)S(1)} %get-tuple-element.30), channel_id=1, source_target_pairs={{0,1},{1,0},{2,3},{3,2},{4,5},{5,4},{6,7},{7,6},{8,9},{9,8},{10,11... | collective-permute-start | bytes 983048 | tf_op jit(solution)/shard_map/ppermute | solution.py:27
  50.9 4.3 %collective-permute-start.16 = (bf16[128,1280]{1,0:T(8,128)(2,1)S(1)}, bf16[128,1280]{1,0:T(8,128)(2,1)S(1)}, u32[]{:S(2)}, u32[]{:S(2)}) collective-permute-start(bf16[128,1280]{1,0:T(8,128)(2,1)S(1)} %get-tuple-element.32), channel_id=1, source_target_pairs={{0,1},{1,0},{2,3},{3,2},{4,5},{5,4},{6,7},{7,6},{8,9},{9,8},{10,11... | collective-permute-start | bytes 983048 | tf_op jit(solution)/shard_map/ppermute | solution.py:27
  52.2 3.7 %collective-permute-start.19 = (bf16[128,1280]{1,0:T(8,128)(2,1)S(1)}, bf16[128,1280]{1,0:T(8,128)(2,1)S(1)}, u32[]{:S(2)}, u32[]{:S(2)}) collective-permute-start(bf16[128,1280]{1,0:T(8,128)(2,1)S(1)} %get-tuple-element.34), channel_id=1, source_target_pairs={{0,1},{1,0},{2,3},{3,2},{4,5},{5,4},{6,7},{7,6},{8,9},{9,8},{10,11... | collective-permute-start | bytes 983048 | tf_op jit(solution)/shard_map/ppermute | solution.py:27
  52.9 4.6 %collective-permute-start.22 = (bf16[128,1280]{1,0:T(8,128)(2,1)S(1)}, bf16[128,1280]{1,0:T(8,128)(2,1)S(1)}, u32[]{:S(2)}, u32[]{:S(2)}) collective-permute-start(bf16[128,1280]{1,0:T(8,128)(2,1)S(1)} %get-tuple-element.36), channel_id=1, source_target_pairs={{0,1},{1,0},{2,3},{3,2},{4,5},{5,4},{6,7},{7,6},{8,9},{9,8},{10,11... | collective-permute-start | bytes 983048 | tf_op jit(solution)/shard_map/ppermute | solution.py:27
  53.6 7.1 %collective-permute-start.14 = (bf16[64,1280]{1,0:T(8,128)(2,1)S(1)}, bf16[64,1280]{1,0:T(8,128)(2,1)S(1)}, u32[]{:S(2)}, u32[]{:S(2)}) collective-permute-start(bf16[64,1280]{1,0:T(8,128)(2,1)S(1)} %slice.63), channel_id=1, source_target_pairs={{0,2},{1,3},{2,0},{3,1},{4,6},{5,7},{6,4},{7,5},{8,10},{9,11},{10,... | collective-permute-start | bytes 491528 | tf_op jit(solution)/shard_map/ppermute | solution.py:27
  55.3 9.0 %collective-permute-start.17 = (bf16[64,1280]{1,0:T(8,128)(2,1)S(1)}, bf16[64,1280]{1,0:T(8,128)(2,1)S(1)}, u32[]{:S(2)}, u32[]{:S(2)}) collective-permute-start(bf16[64,1280]{1,0:T(8,128)(2,1)S(1)} %slice.62), channel_id=1, source_target_pairs={{0,2},{1,3},{2,0},{3,1},{4,6},{5,7},{6,4},{7,5},{8,10},{9,11},{10,... | collective-permute-start | bytes 491528 | tf_op jit(solution)/shard_map/ppermute | solution.py:27
  55.9 11.8 %collective-permute-start.20 = (bf16[64,1280]{1,0:T(8,128)(2,1)S(1)}, bf16[64,1280]{1,0:T(8,128)(2,1)S(1)}, u32[]{:S(2)}, u32[]{:S(2)}) collective-permute-start(bf16[64,1280]{1,0:T(8,128)(2,1)S(1)} %slice.61), channel_id=1, source_target_pairs={{0,2},{1,3},{2,0},{3,1},{4,6},{5,7},{6,4},{7,5},{8,10},{9,11},{10,... | collective-permute-start | bytes 491528 | tf_op jit(solution)/shard_map/ppermute | solution.py:27
  57.6 12.7 %collective-permute-start.23 = (bf16[64,1280]{1,0:T(8,128)(2,1)S(1)}, bf16[64,1280]{1,0:T(8,128)(2,1)S(1)}, u32[]{:S(2)}, u32[]{:S(2)}) collective-permute-start(bf16[64,1280]{1,0:T(8,128)(2,1)S(1)} %slice.60), channel_id=1, source_target_pairs={{0,2},{1,3},{2,0},{3,1},{4,6},{5,7},{6,4},{7,5},{8,10},{9,11},{10,... | collective-permute-start | bytes 491528 | tf_op jit(solution)/shard_map/ppermute | solution.py:27
  60.8 11.2 %collective-permute-start.15 = (bf16[64,1280]{1,0:T(8,128)(2,1)S(1)}, bf16[64,1280]{1,0:T(8,128)(2,1)S(1)}, u32[]{:S(2)}, u32[]{:S(2)}) collective-permute-start(bf16[64,1280]{1,0:T(8,128)(2,1)S(1)} %fusion.3), channel_id=1, source_target_pairs={{0,8},{8,16},{16,24},{24,0},{1,9},{9,17},{17,25},{25,1},{2,10},{10... | collective-permute-start | bytes 491528 | tf_op jit(solution)/shard_map/ppermute | solution.py:22
  64.3 8.1 %collective-permute-start.18 = (bf16[64,1280]{1,0:T(8,128)(2,1)S(1)}, bf16[64,1280]{1,0:T(8,128)(2,1)S(1)}, u32[]{:S(2)}, u32[]{:S(2)}) collective-permute-start(bf16[64,1280]{1,0:T(8,128)(2,1)S(1)} %fusion.2), channel_id=1, source_target_pairs={{0,8},{8,16},{16,24},{24,0},{1,9},{9,17},{17,25},{25,1},{2,10},{10... | collective-permute-start | bytes 491528 | tf_op jit(solution)/shard_map/ppermute | solution.py:22
  67.8 8.1 %collective-permute-start.21 = (bf16[64,1280]{1,0:T(8,128)(2,1)S(1)}, bf16[64,1280]{1,0:T(8,128)(2,1)S(1)}, u32[]{:S(2)}, u32[]{:S(2)}) collective-permute-start(bf16[64,1280]{1,0:T(8,128)(2,1)S(1)} %fusion.1), channel_id=1, source_target_pairs={{0,8},{8,16},{16,24},{24,0},{1,9},{9,17},{17,25},{25,1},{2,10},{10... | collective-permute-start | bytes 491528 | tf_op jit(solution)/shard_map/ppermute | solution.py:22
  70.4 8.1 %collective-permute-start.24 = (bf16[64,1280]{1,0:T(8,128)(2,1)S(1)}, bf16[64,1280]{1,0:T(8,128)(2,1)S(1)}, u32[]{:S(2)}, u32[]{:S(2)}) collective-permute-start(bf16[64,1280]{1,0:T(8,128)(2,1)S(1)} %fusion), channel_id=1, source_target_pairs={{0,8},{8,16},{16,24},{24,0},{1,9},{9,17},{17,25},{25,1},{2,10},{10... | collective-permute-start | bytes 491528 | tf_op jit(solution)/shard_map/ppermute | solution.py:22

commit v3 on v0

--- a/solution.py
+++ b/solution.py
@@ -1,20 +1,385 @@
+import functools
+import math
+
 import jax
 import jax.numpy as jnp
 from jax import lax
+from jax.experimental import pallas as pl
+from jax.experimental.pallas import tpu as pltpu
 from jax.sharding import PartitionSpec as P
 
 HD = 128
 SPAN = 1024
-
-
 ROPE_BASE = 500000.0
 NORM_EPS = 1e-06
+OUT_CHUNKS = 4
+MIB = 1 << 20
+VMEM_MIB = 16
 
 
 def from_behind(value, axis, steps):
     count = lax.axis_size(axis)
     pairs = [(source, (source + steps) % count) for source in range(count)]
     return lax.ppermute(value, axis, pairs)
+
+
+def swap(value, axis, bit):
+    count = lax.axis_size(axis)
+    return lax.ppermute(value, axis, [(source, source ^ bit) for source in range(count)])
+
+
+def norm_rotate_head(head, cosine, sine):
+    head = head * lax.rsqrt(jnp.mean(head * head, axis=-1, keepdims=True) + NORM_EPS)
+    return head * cosine + pltpu.roll(head, HD // 2, 1) * sine
+
+
+def shape(rows, columns, dtype):
+    return jax.ShapeDtypeStruct((rows, columns), dtype)
+
+
+def in_vmem(value):
+    return pltpu.with_memory_space_constraint(value, pltpu.VMEM)
+
+
+def in_hbm(value):
+    return pltpu.with_memory_space_constraint(value, pltpu.HBM)
+
+
+def call(kernel, out_shape, flops, moved, **given):
+    return pl.pallas_call(
+        kernel,
+        out_shape=out_shape,
+        compiler_params=pltpu.CompilerParams(vmem_limit_bytes=VMEM_MIB * MIB),
+        cost_estimate=pl.CostEstimate(flops=flops, bytes_accessed=moved, transcendentals=0),
+        **given,
+    )
+
+
+def after(value, *others):
+    return lax.optimization_barrier((value, *others))[0]
+
+
+def split_kernel(place, value, near, far, sems):
+    wide = near.shape[1]
+    at = pl.multiple_of(place[0] * wide, wide)
+    near_copy = pltpu.make_async_copy(value.at[:, pl.ds(at, wide)], near, sems.at[0])
+    far_copy = pltpu.make_async_copy(value.at[:, pl.ds(wide - at, wide)], far, sems.at[1])
+    near_copy.start()
+    far_copy.start()
+    near_copy.wait()
+    far_copy.wait()
+
+
+def pass_kernel(count, *refs):
+    for value, out in zip(refs[:count], refs[-count:]):
+        out[...] = value[...]
+
+
+def passed(values, *tokens):
+    vmem, anywhere = pl.BlockSpec(memory_space=pltpu.VMEM), pl.BlockSpec(memory_space=pl.ANY)
+    return call(
+        functools.partial(pass_kernel, len(values)),
+        [shape(*value.shape, value.dtype) for value in values],
+        0,
+        1 << 20,
+        in_specs=[vmem] * len(values) + [anywhere] * len(tokens),
+    )(*[in_vmem(value) for value in values], *tokens)
+
+
+def fill_tables(rows, block_rows, place, lengths, cosine, sine, allowed):
+    start, index = place[0] * block_rows, place[1]
+    offsets = [start + shift + rows * (index ^ flip) for shift in (-block_rows, 0) for flip in range(4)]
+    lane = lax.broadcasted_iota(jnp.int32, (1, HD), 1)
+    power = (lane % (HD // 2)).astype(jnp.float32) * (2.0 / HD)
+    frequency = jnp.exp(power * -math.log(ROPE_BASE))
+    sign = jnp.where(lane < HD // 2, -1.0, 1.0)
+    step = lax.broadcasted_iota(jnp.int32, (rows, HD), 0).astype(jnp.float32) * frequency
+    step_cosine, step_sine = jnp.cos(step), jnp.sin(step)
+    order = lax.broadcasted_iota(jnp.int32, (8, HD), 0)
+    origin = jnp.zeros((8, HD), jnp.int32)
+    for at, offset in enumerate(offsets):
+        origin = jnp.where(order == at, offset, origin)
+    origin = origin.astype(jnp.float32) * frequency
+    origin_cosine, origin_sine = jnp.cos(origin), jnp.sin(origin)
+    for at in range(8):
+        part = pl.ds(at * rows, rows)
+        far_cosine, far_sine = origin_cosine[at : at + 1, :], origin_sine[at : at + 1, :]
+        cosine[part, :] = step_cosine * far_cosine - step_sine * far_sine
+        sine[part, :] = (step_sine * far_cosine + step_cosine * far_sine) * sign
+
+    row = lax.broadcasted_iota(jnp.int32, (rows, HD), 0)
+    column = lax.broadcasted_iota(jnp.int32, (1, HD), 1)
+    ends, end = [], 0
+    for doc in range(lengths.shape[1]):
+        end = end + lengths[0, doc]
+        ends.append(end)
+    for at in range(4):
+        q_pos = row + offsets[4 + at]
+        first = q_pos // SPAN * SPAN
+        for end in ends:
+            first = jnp.where(end <= q_pos, jnp.maximum(first, end), first)
+        for to in range(0, 8 * rows, HD):
+            k_pos = column + offsets[to // rows]
+            for half in range(1, HD // rows):
+                other = column + (offsets[to // rows + half] - half * rows)
+                k_pos = jnp.where(column >= half * rows, other, k_pos)
+            inside = (k_pos >= first) & (k_pos <= q_pos)
+            allowed[at * rows : (at + 1) * rows, to : to + HD] = jnp.where(inside, 1.0, 0.0)
+
+
+def stacked(pieces):
+    return jnp.concatenate([piece[...] for piece in pieces], axis=0)
+
+
+def put(total, to, *outs):
+    for out in outs:
+        out[:, to] = total.astype(out.dtype)
+
+
+def own_kernel(block_rows, place, lengths, n0, n1, f0, f1, w_key, w_value, w, *refs):
+    own_sum, own_send, query, key, value, w_near, w_far, cosine, sine, allowed, sems = refs
+    piece, depth = n0.shape
+    near_rows = w.at[pl.ds(pl.multiple_of(place[0] * depth, depth), depth)]
+    far_rows = w.at[pl.ds(pl.multiple_of((1 - place[0]) * depth, depth), depth)]
+    pairs = ((w_key, key), (w_value, value), (near_rows, w_near), (far_rows, w_far))
+    copies = [pltpu.make_async_copy(*pair, sems.at[i]) for i, pair in enumerate(pairs)]
+    for copy in copies:
+        copy.start()
+    fill_tables(piece, block_rows, place, lengths, cosine, sine, allowed)
+    near, far = stacked((n0, n1)), stacked((f0, f1))
+    wide = key.shape[1]
+    for index, weight in enumerate((key, value)):
+        copies[index].wait()
+        total = jnp.dot(near, weight[...], preferred_element_type=jnp.float32)
+        put(total, slice(index * wide, (index + 1) * wide), own_sum, own_send)
+    block = 2 * HD
+    copies[2].wait()
+    columns = range(0, w.shape[1], block)
+    first = [
+        jnp.dot(near, w_near[:, at : at + block], preferred_element_type=jnp.float32)
+        for at in columns
+    ]
+    copies[3].wait()
+    turn = pl.ds(4 * piece, 2 * piece)
+    for at, total in zip(columns, first):
+        total += jnp.dot(far, w_far[:, at : at + block], preferred_element_type=jnp.float32)
+        for head in range(0, block, HD):
+            turned = norm_rotate_head(total[:, head : head + HD], cosine[turn, :], sine[turn, :])
+            query[:, at + head : at + head + HD] = turned.astype(query.dtype)
+
+
+def project_kernel(n0, n1, f0, f1, key, value, own_sum, own_send, far_sum):
+    rows = stacked((n0, n1, f0, f1))
+    whole, wide = own_sum.shape[0], key.shape[1]
+    for index, weight in enumerate((key, value)):
+        to = slice(index * wide, (index + 1) * wide)
+        total = jnp.dot(rows, weight[...], preferred_element_type=jnp.float32)
+        put(total[:whole], to, own_sum, own_send)
+        put(total[whole:], to, far_sum)
+
+
+def query_first_kernel(n0, n1, _, w, out):
+    out[...] = jnp.dot(stacked((n0, n1)), w[...], preferred_element_type=jnp.float32)
+
+
+def project_more_kernel(x0, x1, w0, w1, before, out):
+    rows = stacked((x0, x1))
+    ready, wide = before.shape[0], w0.shape[1]
+    out[:ready, :] = before[...]
+    for index, w in enumerate((w0, w1)):
+        total = jnp.dot(rows, w[...], preferred_element_type=jnp.float32)
+        out[ready:, index * wide : (index + 1) * wide] = total.astype(out.dtype)
+
+
+def query_last_kernel(f0, f1, w, before, cosine, sine, out):
+    rows = stacked((f0, f1))
+    block = 2 * HD
+    turn = pl.ds(3 * rows.shape[0], rows.shape[0])
+    for at in range(0, w.shape[1], block):
+        total = jnp.dot(rows, w[:, at : at + block], preferred_element_type=jnp.float32)
+        total = total + before[:, at : at + block]
+        for head in range(0, block, HD):
+            query = norm_rotate_head(total[:, head : head + HD], cosine[turn, :], sine[turn, :])
+            out[:, at + head : at + head + HD] = query.astype(out.dtype)
+
+
+def finish(total, cosine, sine, out, at):
+    rows, wide = total.shape
+    keys = wide // 2
+    part = pl.ds(at, rows)
+    for head in range(0, keys, HD):
+        key = norm_rotate_head(total[:, head : head + HD], cosine[part, :], sine[part, :])
+        out[part, head : head + HD] = key.astype(out.dtype)
+    out[part, keys:] = total[:, keys:].astype(out.dtype)
+
+
+def finish_kernel(far, early_a, early_b, cosine, sine, out):
+    rows = early_a.shape[0]
+    for at, early in ((0, early_a), (rows, early_b)):
+        total = early[...].astype(jnp.float32) + far[at : at + rows, :].astype(jnp.float32)
+        finish(total, cosine, sine, out, at)
+
+
+def attend_kernel(group, q_first, q_last, done, sum_a, sum_b, arrived, cosine, sine, allowed, out, kv):
+    rows = 2 * q_first.shape[0]
+    ready = done.shape[0]
+    kv[:ready, :] = done[...]
+    half = sum_a.shape[0]
+    for at, own_sum in ((0, sum_a), (half, sum_b)):
+        total = own_sum[...] + arrived[at : at + half, :].astype(jnp.float32)
+        finish(total, cosine, sine, kv, ready + at)
+    keys = kv.shape[1] // 2
+    allow = jnp.concatenate([allowed[...]] * group, axis=0) > 0.5
+    for head in range(0, keys, HD):
+        key = kv[:, head : head + HD]
+        value = kv[:, keys + head : keys + head + HD]
+        at = head * group
+        columns = [slice(at + g * HD, at + (g + 1) * HD) for g in range(group)]
+        query = jnp.concatenate([q[:, c] for c in columns for q in (q_first, q_last)], 0)
+        scores = lax.dot_general(
+            query, key, (((1,), (1,)), ((), ())), preferred_element_type=jnp.float32
+        )
+        weights = jnp.where(allow, jnp.exp(scores * (1.0 / HD**0.5)), 0.0)
+        weights = weights.astype(jnp.bfloat16)
+        total = jnp.sum(weights.astype(jnp.float32), axis=-1, keepdims=True)
+        mixed = jnp.dot(weights, value, preferred_element_type=jnp.float32) / total
+        mixed = mixed.astype(out.dtype)
+        for g, c in enumerate(columns):
+            out[:, c] = mixed[g * rows : (g + 1) * rows, :]
+
+
+def out_kernel(first, attended, w, stay, leave):
+    wide = stay.shape[1]
+    rows = stay.shape[0] // 2
+    block = 2 * HD
+    for at in range(0, wide, block):
+        part = pl.ds(first + at, block)
+        total = jnp.dot(attended[...], w[:, part], preferred_element_type=jnp.float32)
+        for to, (index, out) in enumerate(((0, stay), (1, leave), (2, stay), (3, leave))):
+            piece = total[index * rows : (index + 1) * rows].astype(out.dtype)
+            out[to // 2 * rows : to // 2 * rows + rows, at : at + block] = piece
+
+
+def project_out(attended, w, first, wide):
+    rows, depth = attended.shape
+    return call(
+        functools.partial(out_kernel, first),
+        [shape(rows // 2, wide, jnp.float32), shape(rows // 2, wide, jnp.bfloat16)],
+        2 * rows * depth * wide,
+        2 * rows * depth,
+    )(attended, w)
+
+
+def on_four_by_two(inputs, doc_lengths, w_query, w_key, w_value, w_out):
+    own = inputs[0]
+    w_query, w_key, w_value, w_out = w_query[0], w_key[0], w_value[0], w_out[0]
+    rows = own.shape[0]
+    half = w_key.shape[0]
+    group = w_query.shape[1] // w_key.shape[1]
+    ctx, tp = lax.axis_index("ctx"), lax.axis_index("tp")
+    block_rows = rows * lax.axis_size("tp")
+
+    smem, vmem = pl.BlockSpec(memory_space=pltpu.SMEM), pl.BlockSpec(memory_space=pltpu.VMEM)
+    anywhere = pl.BlockSpec(memory_space=pl.ANY)
+
+    place = jnp.stack([ctx, tp])
+    x_near, x_far = call(
+        split_kernel,
+        [shape(rows, half, own.dtype)] * 2,
+        0,
+        1 << 20,
+        in_specs=[smem, anywhere],
+        scratch_shapes=[pltpu.SemaphoreType.DMA((2,))],
+    )(place, in_hbm(own))
+    far_a = swap(x_far, "ctx", 1)
+    near_b = swap(x_near, "tp", 2)
+    x_near_s = swap(x_near, "tp", 1)
+    x_far_s = swap(x_far, "tp", 1)
+
+    wide = w_query.shape[1]
+    kv_wide = 2 * w_key.shape[1]
+    kv_flops = 4 * rows * half * kv_wide
+    sums = [shape(2 * rows, kv_wide, jnp.float32), shape(2 * rows, kv_wide, jnp.bfloat16)]
+    sum_a, send_a, q_first, key, value, w_near, w_far, cosine, sine, allowed = call(
+        functools.partial(own_kernel, block_rows),
+        [
+            *sums,
+            shape(2 * rows, wide, jnp.bfloat16),
+            *[shape(*w_key.shape, jnp.bfloat16)] * 2,
+            *[shape(half, wide, jnp.bfloat16)] * 2,
+            *[shape(8 * rows, HD, jnp.float32)] * 2,
+            shape(4 * rows, 8 * rows, jnp.float32),
+        ],
+        kv_flops + 8 * rows * half * wide,
+        8 * rows * half,
+        in_specs=[smem] * 2 + [vmem] * 4 + [anywhere] * 3,
+        scratch_shapes=[pltpu.SemaphoreType.DMA((4,))],
+    )(
+        place,
+        doc_lengths,
+        *(x_near, x_near_s, x_far, x_far_s),
+        *(in_hbm(w_key), in_hbm(w_value), in_hbm(w_query)),
+    )
+    key, value, w_near, w_far = in_vmem(key), in_vmem(value), in_vmem(w_near), in_vmem(w_far)
+
+    far_a, near_b, send_a = passed([far_a, near_b, send_a])
+    far_b = swap(far_a, "tp", 2)
+    early_a = swap(send_a, "ctx", 1)
+    near_b_s = swap(near_b, "tp", 1)
+    far_a_s = swap(far_a, "tp", 1)
+    sum_b, send_b, far_sum_a = call(
+        project_kernel, [*sums, sums[1]], 2 * kv_flops, 8 * rows * half
+    )(near_b, near_b_s, far_a, far_a_s, key, value)
+    early_b = swap(send_b, "ctx", 1)
+    before = call(
+        query_first_kernel,
+        shape(2 * rows, wide, jnp.float32),
+        4 * rows * half * wide,
+        4 * rows * half,
+        in_specs=[vmem] * 2 + [anywhere, vmem],
+    )(near_b, near_b_s, send_b, w_near)
+
+    x_again, far_b = passed([x_far, far_b], before, early_a, early_b)
+    far_c = swap(x_again, "tp", 2)
+    far_b_s = swap(far_b, "tp", 1)
+    far_sum = call(
+        project_more_kernel,
+        shape(4 * rows, kv_wide, jnp.bfloat16),
+        kv_flops,
+        4 * rows * half,
+    )(far_b, far_b_s, key, value, far_sum_a)
+    arrived = swap(far_sum, "ctx", 1)
+    far_c = passed([far_c], arrived)[0]
+    far_c_s = swap(far_c, "tp", 1)
+    q_last = call(
+        query_last_kernel,
+        shape(2 * rows, wide, jnp.bfloat16),
+        4 * rows * half * wide,
+        8 * rows * half,
+    )(far_c, far_c_s, w_far, before, cosine, sine)
+
+    kv_shape = shape(4 * rows, kv_wide, jnp.bfloat16)
+    done = call(finish_kernel, kv_shape, 1 << 24, 1 << 20)(
+        far_sum, early_a, early_b, cosine, sine
+    )
+    attended = call(
+        functools.partial(attend_kernel, group),
+        shape(4 * rows, wide, jnp.bfloat16),
+        8 * rows * 8 * rows * wide,
+        1 << 20,
+        scratch_shapes=[pltpu.VMEM((8 * rows, kv_wide), jnp.bfloat16)],
+    )(q_first, q_last, done, sum_a, sum_b, arrived, cosine, sine, allowed)
+
+    w_out = in_vmem(w_out)
+    wide = w_out.shape[1] // OUT_CHUNKS
+    parts = []
+    for chunk in range(OUT_CHUNKS):
+        stay, leave = project_out(attended, w_out, chunk * wide, wide)
+        stay = stay + swap(leave, "tp", 1).astype(jnp.float32)
+        arrived = swap(stay[rows:].astype(jnp.bfloat16), "tp", 2)
+        mixed = (stay[:rows] + arrived.astype(jnp.float32)).astype(jnp.bfloat16)
+        parts.append(from_behind(mixed, "pipe", 1))
+    return jnp.concatenate(parts, axis=1)[None]
 
 
 def doc_index(positions, lengths):
@@ -61,7 +426,7 @@
     return (numerator, denominator)
 
 
-def on_device(inputs, doc_lengths, w_query, w_key, w_value, w_out):
+def on_any(inputs, doc_lengths, w_query, w_key, w_value, w_out):
     tok_rows = lax.all_gather(inputs[0], "tp", axis=0, tiled=True)
     block_rows = tok_rows.shape[0]
     q_heads = w_query.shape[2] // HD
@@ -109,8 +474,7 @@
         scatter_dimension=0,
         tiled=True,
     )
-    received = from_behind(mixed, "pipe", 1)
-    return received[None]
+    return from_behind(mixed, "pipe", 1)[None]
 
 
 def solution(mesh):
@@ -123,6 +487,11 @@
         P("pipe", "tp", None),
     )
     out_specs = P("pipe", ("ctx", "tp"), None)
+    paired = mesh.shape["ctx"] == 2 and mesh.shape["tp"] == 4
     return jax.shard_map(
-        on_device, mesh=mesh, in_specs=in_specs, out_specs=out_specs, check_vma=False
-    )
+        on_four_by_two if paired else on_any,
+        mesh=mesh,
+        in_specs=in_specs,
+        out_specs=out_specs,
+        check_vma=False,
+    )

time: 187 us -> 69.7 us (0.37)
  waiting for transfers between devices: 129 us -> 28.2 us
  starting transfers between devices: 1.56 us -> 23.6 us
  matrix products: 15.5 us -> 0 us
  Pallas kernels: 0 us -> 15.4 us
  local copies, waits for them, and re-layouts: 14.8 us -> 0.74 us
  between operations: 13.3 us -> 0.25 us
  blocking collectives: 8.85 us -> 0 us
    all_gather x2 -> x0, waiting for transfers between devices: 76.9 us -> none  [the longest x1 63.6 us: on_device(): lax.all_gather(stacked_weights, 'ctx', axis=1, tiled=True)]
    reduce_scatter x1 -> x0, waiting for transfers between devices: 34.8 us -> none  [on_device(): lax.psum_scatter(jnp.dot(attended, w_out[0], preferred_element_type=jnp.f...]
    ppermute x0 -> x21, waiting for transfers between devices: none -> 21.9 us  [swap(): lax.ppermute(value, axis, [(source, source ^ bit) for source in range(cou...]
    ppermute x0 -> x21, starting transfers between devices: none -> 17.1 us  [swap(): lax.ppermute(value, axis, [(source, source ^ bit) for source in range(cou...]
    dot_general x5 -> x0, matrix products: 15.5 us -> none  [the longest x1 6.27 us: on_device(): queries = jnp.dot(tok_rows, w_query[0], preferred_element_type=jnp.float32)]
    pallas_call x0 -> x15, Pallas kernels: none -> 15.4 us  [the longest x1 6.33 us: on_four_by_two(): call(functools.partial(own_kernel, block_rows), [*sums, shape(2 * rows, w...]
    unnamed x12 -> x6, local copies, waits for them, and re-layouts: 14.8 us -> 0.66 us
    ppermute x1 -> x4, waiting for transfers between devices: 17 us -> 6.34 us  [from_behind(): return lax.ppermute(value, axis, pairs)]
  transfers between devices with their start and end apart: 4 -> 25, of which waited for: 4 -> 12; matrix products, arithmetic and copies ran while one was open for 12% -> 1% of each run, Pallas kernels for 0% -> 15%
where the time goes in v3:
time: 69.7 us; the launch traced here: 69.5 us
  waiting for transfers between devices  28.2 us (40%)
  starting transfers between devices  23.6 us (34%)
  Pallas kernels  15.4 us (22%)
  other arithmetic  1.3 us (2%)
  local copies, waits for them, and re-layouts  0.74 us (1%)
    ppermute x21, waiting for transfers between devices, swap(): lax.ppermute(value, axis, [(source, source ^ bit) for source in range(cou...  21.9 us
    ppermute x21, starting transfers between devices, swap(): lax.ppermute(value, axis, [(source, source ^ bit) for source in range(cou...  17.1 us
    ppermute x4, starting transfers between devices, from_behind(): return lax.ppermute(value, axis, pairs)  6.5 us
    ppermute x4, waiting for transfers between devices, from_behind(): return lax.ppermute(value, axis, pairs)  6.34 us
    pallas_call x1, Pallas kernels, on_four_by_two(): call(functools.partial(own_kernel, block_rows), [*sums, shape(2 * rows, w...  6.33 us
    pallas_call x4, Pallas kernels, project_out(): call(functools.partial(out_kernel, first), [shape(rows // 2, wide, jnp.fl...  2.73 us
    pallas_call x1, Pallas kernels, on_four_by_two(): call(split_kernel, [shape(rows, half, own.dtype)] * 2, 0, 1 << 20, in_spe...  1.63 us
  transfers between devices with their start and end apart: 25, of which 12 were waited for; matrix products, arithmetic and copies ran while one was open for 1% of the time, Pallas kernels for 15%

profile of v3, /device:TPU:0, one launch (start us, length us, event | category | flops | bytes accessed | tf_op | source)
XLA Modules:
  0.0 69.5 jit_solution(15973290332541113857)
XLA Ops:
  0.0 0.1 pad_add_fusion.place
  0.1 1.6 %shard_map.64 = (bf16[64,2560]{1,0:T(8,128)(2,1)S(1)}, bf16[64,2560]{1,0:T(8,128)(2,1)S(1)}) custom-call(s32[2]{0:T(128)S(1)} %pad_add_fusion.place, bf16[64,5120]{1,0:T(8,128)(2,1)} %bitcast.18), custom_call_target="tpu_custom_call" | custom-call | bytes 1048576 | tf_op jit(solution)/shard_map/pallas_call | solution.py:286
  1.7 0.5 collective-permute-start.1
  2.2 0.1 collective-permute-start
  2.3 2.9 %collective-permute-start.2 = (bf16[64,2560]{1,0:T(8,128)(2,1)S(1)}, bf16[64,2560]{1,0:T(8,128)(2,1)S(1)}, u32[]{:S(2)}, u32[]{:S(2)}) collective-permute-start(bf16[64,2560]{1,0:T(8,128)(2,1)S(1)} %get-tuple-element.34.f0.refs_0_), channel_id=1, source_target_pairs={{0,4},{4,0},{1,5},{5,1},{2,6},{6,2},{3,7},{7,3},{8,12},{12,8},{9,1... | collective-permute-start | bytes 983048 | tf_op jit(solution)/shard_map/ppermute | solution.py:28
  5.2 1.5 %collective-permute-start.3 = (bf16[64,2560]{1,0:T(8,128)(2,1)S(1)}, bf16[64,2560]{1,0:T(8,128)(2,1)S(1)}, u32[]{:S(2)}, u32[]{:S(2)}) collective-permute-start(bf16[64,2560]{1,0:T(8,128)(2,1)S(1)} %get-tuple-element.33.n0), channel_id=1, source_target_pairs={{0,2},{1,3},{2,0},{3,1},{4,6},{5,7},{6,4},{7,5},{8,10},{9,11},{10,... | collective-permute-start | bytes 983048 | tf_op jit(solution)/shard_map/ppermute | solution.py:28
  6.8 0.0 collective-permute-done.1.f1
  6.8 0.7 copy-done
  7.4 6.3 %shard_map.65 = (f32[128,512]{1,0:T(8,128)S(1)}, bf16[128,512]{1,0:T(8,128)(2,1)S(1)}, bf16[128,768]{1,0:T(8,128)(2,1)S(1)}, bf16[2560,256]{1,0:T(8,128)(2,1)S(1...) custom-call(s32[2]{0:T(128)S(1)} %pad_add_fusion.place, ...), custom_call_target="tpu_custom_call" | custom-call | flops 1342177280 | bytes 1310720 | tf_op jit(solution)/shard_map/pallas_call | solution.py:303
  13.8 0.0 collective-permute-done.2.refs_0_
  13.8 0.9 %collective-permute-done.3.refs_1_ = bf16[64,2560]{1,0:T(8,128)(2,1)S(1)} collective-permute-done((bf16[64,2560]{1,0:T(8,128)(2,1)S(1)}, bf16[64,2560]{1,0:T(8,128)(2,1)S(1)}, u32[]{:S(2)}, u32[]{:S(2)}) %collective-permute-start.3) | collective-permute-done | bytes 327712 | tf_op jit(solution)/shard_map/ppermute | solution.py:28
  14.6 0.1 shard_map.66
  14.7 0.1 collective-permute-start.5
  14.8 0.5 collective-permute-start.6
  15.3 1.5 %collective-permute-start.4 = (bf16[64,2560]{1,0:T(8,128)(2,1)S(1)}, bf16[64,2560]{1,0:T(8,128)(2,1)S(1)}, u32[]{:S(2)}, u32[]{:S(2)}) collective-permute-start(bf16[64,2560]{1,0:T(8,128)(2,1)S(1)} %get-tuple-element.37.f0), channel_id=1, source_target_pairs={{0,2},{1,3},{2,0},{3,1},{4,6},{5,7},{6,4},{7,5},{8,10},{9,11},{10,... | collective-permute-start | bytes 983048 | tf_op jit(solution)/shard_map/ppermute | solution.py:28
  16.8 0.5 collective-permute-start.7
  17.3 0.0 collective-permute-done.5.n1
  17.3 0.8 %shard_map.67 = (f32[128,512]{1,0:T(8,128)S(1)}, bf16[128,512]{1,0:T(8,128)(2,1)S(1)}, bf16[128,512]{1,0:T(8,128)(2,1)S(1)}) custom-call(bf16[64,2560]{1,0:T(8,128)(2,1)S(1)} %get-tuple-element.38.n0, bf16[64,2560]{1,0:T(8,128)(2,1)S(1)} %collective-permute-done.5.n1, bf16[64,2560]{1,0:T(8,128)(2,1)S(1)} %get-tuple-element.37.f0, ...), custom_call_target="tpu_custom_call" | custom-call | flops 671088640 | bytes 1310720 | tf_op jit(solution)/shard_map/pallas_call | solution.py:330
  18.2 1.6 %collective-permute-start.8 = (bf16[128,512]{1,0:T(8,128)(2,1)S(1)}, bf16[128,512]{1,0:T(8,128)(2,1)S(1)}, u32[]{:S(2)}, u32[]{:S(2)}) collective-permute-start(bf16[128,512]{1,0:T(8,128)(2,1)S(1)} %get-tuple-element.41._), channel_id=1, source_target_pairs={{0,4},{4,0},{1,5},{5,1},{2,6},{6,2},{3,7},{7,3},{8,12},{12,8},{9,1... | collective-permute-start | bytes 393224 | tf_op jit(solution)/shard_map/ppermute | solution.py:28
  19.7 0.7 shard_map.68.refs_2_.before
  20.4 2.8 %collective-permute-done.7.refs_3_.early_a = bf16[128,512]{1,0:T(8,128)(2,1)S(1)} collective-permute-done((bf16[128,512]{1,0:T(8,128)(2,1)S(1)}, bf16[128,512]{1,0:T(8,128)(2,1)S(1)}, u32[]{:S(2)}, u32[]{:S(2)}) %collective-permute-start.7) | collective-permute-done | bytes 131104 | tf_op jit(solution)/shard_map/ppermute | solution.py:28
  23.2 1.8 %collective-permute-done.4.refs_1_ = bf16[64,2560]{1,0:T(8,128)(2,1)S(1)} collective-permute-done((bf16[64,2560]{1,0:T(8,128)(2,1)S(1)}, bf16[64,2560]{1,0:T(8,128)(2,1)S(1)}, u32[]{:S(2)}, u32[]{:S(2)}) %collective-permute-start.4) | collective-permute-done | bytes 327712 | tf_op jit(solution)/shard_map/ppermute | solution.py:28
  25.0 0.1 collective-permute-start.10
  25.1 1.6 %collective-permute-start.9 = (bf16[64,2560]{1,0:T(8,128)(2,1)S(1)}, bf16[64,2560]{1,0:T(8,128)(2,1)S(1)}, u32[]{:S(2)}, u32[]{:S(2)}) collective-permute-start(bf16[64,2560]{1,0:T(8,128)(2,1)S(1)} %get-tuple-element.44), channel_id=1, source_target_pairs={{0,2},{1,3},{2,0},{3,1},{4,6},{5,7},{6,4},{7,5},{8,10},{9,11},{10,... | collective-permute-start | bytes 983048 | tf_op jit(solution)/shard_map/ppermute | solution.py:28
  26.7 0.0 collective-permute-done.10.x1
  26.7 0.5 shard_map.70.far
  27.2 0.6 collective-permute-start.11
  27.8 7.4 %collective-permute-done.9.refs_0_ = bf16[64,2560]{1,0:T(8,128)(2,1)S(1)} collective-permute-done((bf16[64,2560]{1,0:T(8,128)(2,1)S(1)}, bf16[64,2560]{1,0:T(8,128)(2,1)S(1)}, u32[]{:S(2)}, u32[]{:S(2)}) %collective-permute-start.9) | collective-permute-done | bytes 327712 | tf_op jit(solution)/shard_map/ppermute | solution.py:28
  35.2 0.4 collective-permute-done.11.refs_1_.arrived
  35.7 0.1 collective-permute-start.12
  35.8 0.3 shard_map.73.done
  36.1 1.3 %collective-permute-done.12.f1 = bf16[64,2560]{1,0:T(8,128)(2,1)S(1)} collective-permute-done((bf16[64,2560]{1,0:T(8,128)(2,1)S(1)}, bf16[64,2560]{1,0:T(8,128)(2,1)S(1)}, u32[]{:S(2)}, u32[]{:S(2)}) %collective-permute-start.12) | collective-permute-done | bytes 327712 | tf_op jit(solution)/shard_map/ppermute | solution.py:28
  37.4 0.9 %shard_map.72.q_last = bf16[128,768]{1,0:T(8,128)(2,1)S(1)} custom-call(bf16[64,2560]{1,0:T(8,128)(2,1)S(1)} %shard_map.71.f0, bf16[64,2560]{1,0:T(8,128)(2,1)S(1)} %collective-permute-done.12.f1, bf16[2560,768]{1,0:T(8,128)(2,1)S(1)} %get-tuple-element.47.w, f32[128,768]{1,0:T(8,128)S(1)} %shard_map.68.refs_2_.before, ...), custom_call_target="tpu_custom_call" | custom-call | flops 503316480 | bytes 1310720 | tf_op jit(solution)/shard_map/pallas_call | solution.py:354
  38.3 1.3 %shard_map.74.attended = bf16[256,768]{1,0:T(8,128)(2,1)S(1)} custom-call(bf16[128,768]{1,0:T(8,128)(2,1)S(1)} %get-tuple-element.35.q_first, bf16[128,768]{1,0:T(8,128)(2,1)S(1)} %shard_map.72.q_last, bf16[256,512]{1,0:T(8,128)(2,1)S(1)} %shard_map.73.done, f32[128,512]{1,0:T(8,128)S(1)} %get-tuple-element.50.sum_a, ...), custom_call_target="tpu_custom_call" | custom-call | flops 201326592 | bytes 1048576 | tf_op jit(solution)/shard_map/pallas_call | solution.py:365
  39.6 0.7 shard_map.75
  40.3 0.2 collective-permute-start.13
  40.5 0.7 shard_map.76
  41.2 0.4 collective-permute-start.16
  41.7 0.7 shard_map.77
  42.4 0.2 collective-permute-start.19
  42.5 0.7 shard_map.78
  43.2 0.4 collective-permute-start.22
  43.7 0.0 collective-permute-done.13
  43.7 0.1 convert_add_fusion.3
  43.8 1.6 %collective-permute-start.14 = (bf16[64,1280]{1,0:T(8,128)(2,1)S(1)}, bf16[64,1280]{1,0:T(8,128)(2,1)S(1)}, u32[]{:S(2)}, u32[]{:S(2)}) collective-permute-start(bf16[64,1280]{1,0:T(8,128)(2,1)S(1)} %slice.63), channel_id=1, source_target_pairs={{0,2},{1,3},{2,0},{3,1},{4,6},{5,7},{6,4},{7,5},{8,10},{9,11},{10,... | collective-permute-start | bytes 491528 | tf_op jit(solution)/shard_map/ppermute | solution.py:28
  45.4 0.0 collective-permute-done.16
  45.4 0.1 convert_add_fusion.2
  45.5 0.6 collective-permute-start.17
  46.0 0.0 collective-permute-done.19
  46.0 0.1 convert_add_fusion.1
  46.1 1.6 %collective-permute-start.20 = (bf16[64,1280]{1,0:T(8,128)(2,1)S(1)}, bf16[64,1280]{1,0:T(8,128)(2,1)S(1)}, u32[]{:S(2)}, u32[]{:S(2)}) collective-permute-start(bf16[64,1280]{1,0:T(8,128)(2,1)S(1)} %slice.61), channel_id=1, source_target_pairs={{0,2},{1,3},{2,0},{3,1},{4,6},{5,7},{6,4},{7,5},{8,10},{9,11},{10,... | collective-permute-start | bytes 491528 | tf_op jit(solution)/shard_map/ppermute | solution.py:28
  47.7 0.1 convert_add_fusion
  47.8 0.6 collective-permute-start.23
  48.4 2.5 %collective-permute-done.14 = bf16[64,1280]{1,0:T(8,128)(2,1)S(1)} collective-permute-done((bf16[64,1280]{1,0:T(8,128)(2,1)S(1)}, bf16[64,1280]{1,0:T(8,128)(2,1)S(1)}, u32[]{:S(2)}, u32[]{:S(2)}) %collective-permute-start.14) | collective-permute-done | bytes 163872 | tf_op jit(solution)/shard_map/ppermute | solution.py:28
  50.9 1.6 %collective-permute-start.15 = (bf16[64,1280]{1,0:T(8,128)(2,1)S(1)}, bf16[64,1280]{1,0:T(8,128)(2,1)S(1)}, u32[]{:S(2)}, u32[]{:S(2)}) collective-permute-start(bf16[64,1280]{1,0:T(8,128)(2,1)S(1)} %fusion.3), channel_id=1, source_target_pairs={{0,8},{8,16},{16,24},{24,0},{1,9},{9,17},{17,25},{25,1},{2,10},{10... | collective-permute-start | bytes 491528 | tf_op jit(solution)/shard_map/ppermute | solution.py:23
  52.5 1.9 %collective-permute-done.17 = bf16[64,1280]{1,0:T(8,128)(2,1)S(1)} collective-permute-done((bf16[64,1280]{1,0:T(8,128)(2,1)S(1)}, bf16[64,1280]{1,0:T(8,128)(2,1)S(1)}, u32[]{:S(2)}, u32[]{:S(2)}) %collective-permute-start.17) | collective-permute-done | bytes 163872 | tf_op jit(solution)/shard_map/ppermute | solution.py:28
  54.4 1.6 %collective-permute-start.18 = (bf16[64,1280]{1,0:T(8,128)(2,1)S(1)}, bf16[64,1280]{1,0:T(8,128)(2,1)S(1)}, u32[]{:S(2)}, u32[]{:S(2)}) collective-permute-start(bf16[64,1280]{1,0:T(8,128)(2,1)S(1)} %fusion.2), channel_id=1, source_target_pairs={{0,8},{8,16},{16,24},{24,0},{1,9},{9,17},{17,25},{25,1},{2,10},{10... | collective-permute-start | bytes 491528 | tf_op jit(solution)/shard_map/ppermute | solution.py:23
  56.1 1.9 %collective-permute-done.20 = bf16[64,1280]{1,0:T(8,128)(2,1)S(1)} collective-permute-done((bf16[64,1280]{1,0:T(8,128)(2,1)S(1)}, bf16[64,1280]{1,0:T(8,128)(2,1)S(1)}, u32[]{:S(2)}, u32[]{:S(2)}) %collective-permute-start.20) | collective-permute-done | bytes 163872 | tf_op jit(solution)/shard_map/ppermute | solution.py:28
  57.9 1.6 %collective-permute-start.21 = (bf16[64,1280]{1,0:T(8,128)(2,1)S(1)}, bf16[64,1280]{1,0:T(8,128)(2,1)S(1)}, u32[]{:S(2)}, u32[]{:S(2)}) collective-permute-start(bf16[64,1280]{1,0:T(8,128)(2,1)S(1)} %fusion.1), channel_id=1, source_target_pairs={{0,8},{8,16},{16,24},{24,0},{1,9},{9,17},{17,25},{25,1},{2,10},{10... | collective-permute-start | bytes 491528 | tf_op jit(solution)/shard_map/ppermute | solution.py:23
  59.6 1.0 %collective-permute-done.23 = bf16[64,1280]{1,0:T(8,128)(2,1)S(1)} collective-permute-done((bf16[64,1280]{1,0:T(8,128)(2,1)S(1)}, bf16[64,1280]{1,0:T(8,128)(2,1)S(1)}, u32[]{:S(2)}, u32[]{:S(2)}) %collective-permute-start.23) | collective-permute-done | bytes 163872 | tf_op jit(solution)/shard_map/ppermute | solution.py:28
  60.6 1.6 %collective-permute-start.24 = (bf16[64,1280]{1,0:T(8,128)(2,1)S(1)}, bf16[64,1280]{1,0:T(8,128)(2,1)S(1)}, u32[]{:S(2)}, u32[]{:S(2)}) collective-permute-start(bf16[64,1280]{1,0:T(8,128)(2,1)S(1)} %fusion), channel_id=1, source_target_pairs={{0,8},{8,16},{16,24},{24,0},{1,9},{9,17},{17,25},{25,1},{2,10},{10... | collective-permute-start | bytes 491528 | tf_op jit(solution)/shard_map/ppermute | solution.py:23
  62.3 3.5 %collective-permute-done.21 = bf16[64,1280]{1,0:T(8,128)(2,1)S(1)} collective-permute-done((bf16[64,1280]{1,0:T(8,128)(2,1)S(1)}, bf16[64,1280]{1,0:T(8,128)(2,1)S(1)}, u32[]{:S(2)}, u32[]{:S(2)}) %collective-permute-start.21) | collective-permute-done | bytes 163872 | tf_op jit(solution)/shard_map/ppermute | solution.py:23
  65.8 2.9 %collective-permute-done.24 = bf16[64,1280]{1,0:T(8,128)(2,1)S(1)} collective-permute-done((bf16[64,1280]{1,0:T(8,128)(2,1)S(1)}, bf16[64,1280]{1,0:T(8,128)(2,1)S(1)}, u32[]{:S(2)}, u32[]{:S(2)}) %collective-permute-start.24) | collective-permute-done | bytes 163872 | tf_op jit(solution)/shard_map/ppermute | solution.py:23
  68.6 0.9 %maximum_bitcast_fusion = bf16[1,64,5120]{2,1,0:T(8,128)(2,1)} fusion(bf16[64,1280]{1,0:T(8,128)(2,1)S(1)} %collective-permute-done.24, bf16[64,1280]{1,0:T(8,128)(2,1)S(1)} %collective-permute-done.21, bf16[64,1280]{1,0:T(8,128)(2,1)S(1)} %collective-permute-done.18, bf16[64,1280]{1,0:T(8,128)(2,1)S(1)} %collective-permute-done.15), kind=kLoop, calls=%fused_computation | loop fusion | flops 2621440 | bytes 1310720 | tf_op jit(solution)/shard_map/broadcast_in_dim | solution.py:382
  (22 shorter events, 0.3 us)
Async XLA Ops:
  1.7 5.0 %collective-permute-start.1 = (bf16[64,2560]{1,0:T(8,128)(2,1)S(1)}, bf16[64,2560]{1,0:T(8,128)(2,1)S(1)}, u32[]{:S(2)}, u32[]{:S(2)}) collective-permute-start(bf16[64,2560]{1,0:T(8,128)(2,1)S(1)} %get-tuple-element.34.f0.refs_0_), channel_id=1, source_target_pairs={{0,1},{1,0},{2,3},{3,2},{4,5},{5,4},{6,7},{7,6},{8,9},{9,8},{10,11... | collective-permute-start | bytes 983048 | tf_op jit(solution)/shard_map/ppermute | solution.py:28
  2.2 4.5 %collective-permute-start = (bf16[64,2560]{1,0:T(8,128)(2,1)S(1)}, bf16[64,2560]{1,0:T(8,128)(2,1)S(1)}, u32[]{:S(2)}, u32[]{:S(2)}) collective-permute-start(bf16[64,2560]{1,0:T(8,128)(2,1)S(1)} %get-tuple-element.33.n0), channel_id=1, source_target_pairs={{0,1},{1,0},{2,3},{3,2},{4,5},{5,4},{6,7},{7,6},{8,9},{9,8},{10,11... | collective-permute-start | bytes 983048 | tf_op jit(solution)/shard_map/ppermute | solution.py:28
  2.3 11.4 %collective-permute-start.2 = (bf16[64,2560]{1,0:T(8,128)(2,1)S(1)}, bf16[64,2560]{1,0:T(8,128)(2,1)S(1)}, u32[]{:S(2)}, u32[]{:S(2)}) collective-permute-start(bf16[64,2560]{1,0:T(8,128)(2,1)S(1)} %get-tuple-element.34.f0.refs_0_), channel_id=1, source_target_pairs={{0,4},{4,0},{1,5},{5,1},{2,6},{6,2},{3,7},{7,3},{8,12},{12,8},{9,1... | collective-permute-start | bytes 983048 | tf_op jit(solution)/shard_map/ppermute | solution.py:28
  5.2 9.4 %collective-permute-start.3 = (bf16[64,2560]{1,0:T(8,128)(2,1)S(1)}, bf16[64,2560]{1,0:T(8,128)(2,1)S(1)}, u32[]{:S(2)}, u32[]{:S(2)}) collective-permute-start(bf16[64,2560]{1,0:T(8,128)(2,1)S(1)} %get-tuple-element.33.n0), channel_id=1, source_target_pairs={{0,2},{1,3},{2,0},{3,1},{4,6},{5,7},{6,4},{7,5},{8,10},{9,11},{10,... | collective-permute-start | bytes 983048 | tf_op jit(solution)/shard_map/ppermute | solution.py:28
  6.8 0.7 copy-start
  14.7 2.6 %collective-permute-start.5 = (bf16[64,2560]{1,0:T(8,128)(2,1)S(1)}, bf16[64,2560]{1,0:T(8,128)(2,1)S(1)}, u32[]{:S(2)}, u32[]{:S(2)}) collective-permute-start(bf16[64,2560]{1,0:T(8,128)(2,1)S(1)} %get-tuple-element.38.n0), channel_id=1, source_target_pairs={{0,1},{1,0},{2,3},{3,2},{4,5},{5,4},{6,7},{7,6},{8,9},{9,8},{10,11... | collective-permute-start | bytes 983048 | tf_op jit(solution)/shard_map/ppermute | solution.py:28
  14.8 2.6 %collective-permute-start.6 = (bf16[64,2560]{1,0:T(8,128)(2,1)S(1)}, bf16[64,2560]{1,0:T(8,128)(2,1)S(1)}, u32[]{:S(2)}, u32[]{:S(2)}) collective-permute-start(bf16[64,2560]{1,0:T(8,128)(2,1)S(1)} %get-tuple-element.37.f0), channel_id=1, source_target_pairs={{0,1},{1,0},{2,3},{3,2},{4,5},{5,4},{6,7},{7,6},{8,9},{9,8},{10,11... | collective-permute-start | bytes 983048 | tf_op jit(solution)/shard_map/ppermute | solution.py:28
  15.3 9.7 %collective-permute-start.4 = (bf16[64,2560]{1,0:T(8,128)(2,1)S(1)}, bf16[64,2560]{1,0:T(8,128)(2,1)S(1)}, u32[]{:S(2)}, u32[]{:S(2)}) collective-permute-start(bf16[64,2560]{1,0:T(8,128)(2,1)S(1)} %get-tuple-element.37.f0), channel_id=1, source_target_pairs={{0,2},{1,3},{2,0},{3,1},{4,6},{5,7},{6,4},{7,5},{8,10},{9,11},{10,... | collective-permute-start | bytes 983048 | tf_op jit(solution)/shard_map/ppermute | solution.py:28
  16.8 6.4 %collective-permute-start.7 = (bf16[128,512]{1,0:T(8,128)(2,1)S(1)}, bf16[128,512]{1,0:T(8,128)(2,1)S(1)}, u32[]{:S(2)}, u32[]{:S(2)}) collective-permute-start(bf16[128,512]{1,0:T(8,128)(2,1)S(1)} %get-tuple-element.43), channel_id=1, source_target_pairs={{0,4},{4,0},{1,5},{5,1},{2,6},{6,2},{3,7},{7,3},{8,12},{12,8},{9,1... | collective-permute-start | bytes 393224 | tf_op jit(solution)/shard_map/ppermute | solution.py:28
  18.2 6.8 %collective-permute-start.8 = (bf16[128,512]{1,0:T(8,128)(2,1)S(1)}, bf16[128,512]{1,0:T(8,128)(2,1)S(1)}, u32[]{:S(2)}, u32[]{:S(2)}) collective-permute-start(bf16[128,512]{1,0:T(8,128)(2,1)S(1)} %get-tuple-element.41._), channel_id=1, source_target_pairs={{0,4},{4,0},{1,5},{5,1},{2,6},{6,2},{3,7},{7,3},{8,12},{12,8},{9,1... | collective-permute-start | bytes 393224 | tf_op jit(solution)/shard_map/ppermute | solution.py:28
  25.0 1.7 %collective-permute-start.10 = (bf16[64,2560]{1,0:T(8,128)(2,1)S(1)}, bf16[64,2560]{1,0:T(8,128)(2,1)S(1)}, u32[]{:S(2)}, u32[]{:S(2)}) collective-permute-start(bf16[64,2560]{1,0:T(8,128)(2,1)S(1)} %get-tuple-element.45.x0), channel_id=1, source_target_pairs={{0,1},{1,0},{2,3},{3,2},{4,5},{5,4},{6,7},{7,6},{8,9},{9,8},{10,11... | collective-permute-start | bytes 983048 | tf_op jit(solution)/shard_map/ppermute | solution.py:28
  25.1 10.1 %collective-permute-start.9 = (bf16[64,2560]{1,0:T(8,128)(2,1)S(1)}, bf16[64,2560]{1,0:T(8,128)(2,1)S(1)}, u32[]{:S(2)}, u32[]{:S(2)}) collective-permute-start(bf16[64,2560]{1,0:T(8,128)(2,1)S(1)} %get-tuple-element.44), channel_id=1, source_target_pairs={{0,2},{1,3},{2,0},{3,1},{4,6},{5,7},{6,4},{7,5},{8,10},{9,11},{10,... | collective-permute-start | bytes 983048 | tf_op jit(solution)/shard_map/ppermute | solution.py:28
  26.7 12.9 %slice-start = ((s8[7864320]{0:T(1024)(128)(4,1)}), s8[4194304]{0:T(1024)(128)(4,1)S(1)}, s32[]{:S(2)}) async-start(s8[7864320]{0:T(1024)(128)(4,1)} %bitcast.9), calls=%async_computation | async-start | bytes 8388608
  27.2 8.4 %collective-permute-start.11 = (bf16[256,512]{1,0:T(8,128)(2,1)S(1)}, bf16[256,512]{1,0:T(8,128)(2,1)S(1)}, u32[]{:S(2)}, u32[]{:S(2)}) collective-permute-start(bf16[256,512]{1,0:T(8,128)(2,1)S(1)} %shard_map.70.far), channel_id=1, source_target_pairs={{0,4},{4,0},{1,5},{5,1},{2,6},{6,2},{3,7},{7,3},{8,12},{12,8},{9,1... | collective-permute-start | bytes 786440 | tf_op jit(solution)/shard_map/ppermute | solution.py:28
  35.7 1.7 %collective-permute-start.12 = (bf16[64,2560]{1,0:T(8,128)(2,1)S(1)}, bf16[64,2560]{1,0:T(8,128)(2,1)S(1)}, u32[]{:S(2)}, u32[]{:S(2)}) collective-permute-start(bf16[64,2560]{1,0:T(8,128)(2,1)S(1)} %shard_map.71.f0), channel_id=1, source_target_pairs={{0,1},{1,0},{2,3},{3,2},{4,5},{5,4},{6,7},{7,6},{8,9},{9,8},{10,11... | collective-permute-start | bytes 983048 | tf_op jit(solution)/shard_map/ppermute | solution.py:28
  37.4 2.3 %slice-start.1 = ((s8[7864320]{0:T(1024)(128)(4,1)}), s8[3670016]{0:T(1024)(128)(4,1)S(1)}, s32[]{:S(2)}) async-start(s8[7864320]{0:T(1024)(128)(4,1)} %bitcast.9), calls=%async_computation.1 | async-start | bytes 7340032
  40.3 3.4 %collective-permute-start.13 = (bf16[128,1280]{1,0:T(8,128)(2,1)S(1)}, bf16[128,1280]{1,0:T(8,128)(2,1)S(1)}, u32[]{:S(2)}, u32[]{:S(2)}) collective-permute-start(bf16[128,1280]{1,0:T(8,128)(2,1)S(1)} %get-tuple-element.54), channel_id=1, source_target_pairs={{0,1},{1,0},{2,3},{3,2},{4,5},{5,4},{6,7},{7,6},{8,9},{9,8},{10,11... | collective-permute-start | bytes 983048 | tf_op jit(solution)/shard_map/ppermute | solution.py:28
  41.2 4.1 %collective-permute-start.16 = (bf16[128,1280]{1,0:T(8,128)(2,1)S(1)}, bf16[128,1280]{1,0:T(8,128)(2,1)S(1)}, u32[]{:S(2)}, u32[]{:S(2)}) collective-permute-start(bf16[128,1280]{1,0:T(8,128)(2,1)S(1)} %get-tuple-element.56), channel_id=1, source_target_pairs={{0,1},{1,0},{2,3},{3,2},{4,5},{5,4},{6,7},{7,6},{8,9},{9,8},{10,11... | collective-permute-start | bytes 983048 | tf_op jit(solution)/shard_map/ppermute | solution.py:28
  42.4 3.7 %collective-permute-start.19 = (bf16[128,1280]{1,0:T(8,128)(2,1)S(1)}, bf16[128,1280]{1,0:T(8,128)(2,1)S(1)}, u32[]{:S(2)}, u32[]{:S(2)}) collective-permute-start(bf16[128,1280]{1,0:T(8,128)(2,1)S(1)} %get-tuple-element.58), channel_id=1, source_target_pairs={{0,1},{1,0},{2,3},{3,2},{4,5},{5,4},{6,7},{7,6},{8,9},{9,8},{10,11... | collective-permute-start | bytes 983048 | tf_op jit(solution)/shard_map/ppermute | solution.py:28
  43.2 4.5 %collective-permute-start.22 = (bf16[128,1280]{1,0:T(8,128)(2,1)S(1)}, bf16[128,1280]{1,0:T(8,128)(2,1)S(1)}, u32[]{:S(2)}, u32[]{:S(2)}) collective-permute-start(bf16[128,1280]{1,0:T(8,128)(2,1)S(1)} %get-tuple-element.60), channel_id=1, source_target_pairs={{0,1},{1,0},{2,3},{3,2},{4,5},{5,4},{6,7},{7,6},{8,9},{9,8},{10,11... | collective-permute-start | bytes 983048 | tf_op jit(solution)/shard_map/ppermute | solution.py:28
  43.8 7.1 %collective-permute-start.14 = (bf16[64,1280]{1,0:T(8,128)(2,1)S(1)}, bf16[64,1280]{1,0:T(8,128)(2,1)S(1)}, u32[]{:S(2)}, u32[]{:S(2)}) collective-permute-start(bf16[64,1280]{1,0:T(8,128)(2,1)S(1)} %slice.63), channel_id=1, source_target_pairs={{0,2},{1,3},{2,0},{3,1},{4,6},{5,7},{6,4},{7,5},{8,10},{9,11},{10,... | collective-permute-start | bytes 491528 | tf_op jit(solution)/shard_map/ppermute | solution.py:28
  45.5 9.0 %collective-permute-start.17 = (bf16[64,1280]{1,0:T(8,128)(2,1)S(1)}, bf16[64,1280]{1,0:T(8,128)(2,1)S(1)}, u32[]{:S(2)}, u32[]{:S(2)}) collective-permute-start(bf16[64,1280]{1,0:T(8,128)(2,1)S(1)} %slice.62), channel_id=1, source_target_pairs={{0,2},{1,3},{2,0},{3,1},{4,6},{5,7},{6,4},{7,5},{8,10},{9,11},{10,... | collective-permute-start | bytes 491528 | tf_op jit(solution)/shard_map/ppermute | solution.py:28
  46.1 11.8 %collective-permute-start.20 = (bf16[64,1280]{1,0:T(8,128)(2,1)S(1)}, bf16[64,1280]{1,0:T(8,128)(2,1)S(1)}, u32[]{:S(2)}, u32[]{:S(2)}) collective-permute-start(bf16[64,1280]{1,0:T(8,128)(2,1)S(1)} %slice.61), channel_id=1, source_target_pairs={{0,2},{1,3},{2,0},{3,1},{4,6},{5,7},{6,4},{7,5},{8,10},{9,11},{10,... | collective-permute-start | bytes 491528 | tf_op jit(solution)/shard_map/ppermute | solution.py:28
  47.8 12.8 %collective-permute-start.23 = (bf16[64,1280]{1,0:T(8,128)(2,1)S(1)}, bf16[64,1280]{1,0:T(8,128)(2,1)S(1)}, u32[]{:S(2)}, u32[]{:S(2)}) collective-permute-start(bf16[64,1280]{1,0:T(8,128)(2,1)S(1)} %slice.60), channel_id=1, source_target_pairs={{0,2},{1,3},{2,0},{3,1},{4,6},{5,7},{6,4},{7,5},{8,10},{9,11},{10,... | collective-permute-start | bytes 491528 | tf_op jit(solution)/shard_map/ppermute | solution.py:28
  50.9 11.4 %collective-permute-start.15 = (bf16[64,1280]{1,0:T(8,128)(2,1)S(1)}, bf16[64,1280]{1,0:T(8,128)(2,1)S(1)}, u32[]{:S(2)}, u32[]{:S(2)}) collective-permute-start(bf16[64,1280]{1,0:T(8,128)(2,1)S(1)} %fusion.3), channel_id=1, source_target_pairs={{0,8},{8,16},{16,24},{24,0},{1,9},{9,17},{17,25},{25,1},{2,10},{10... | collective-permute-start | bytes 491528 | tf_op jit(solution)/shard_map/ppermute | solution.py:23
  54.4 7.9 %collective-permute-start.18 = (bf16[64,1280]{1,0:T(8,128)(2,1)S(1)}, bf16[64,1280]{1,0:T(8,128)(2,1)S(1)}, u32[]{:S(2)}, u32[]{:S(2)}) collective-permute-start(bf16[64,1280]{1,0:T(8,128)(2,1)S(1)} %fusion.2), channel_id=1, source_target_pairs={{0,8},{8,16},{16,24},{24,0},{1,9},{9,17},{17,25},{25,1},{2,10},{10... | collective-permute-start | bytes 491528 | tf_op jit(solution)/shard_map/ppermute | solution.py:23
  57.9 7.8 %collective-permute-start.21 = (bf16[64,1280]{1,0:T(8,128)(2,1)S(1)}, bf16[64,1280]{1,0:T(8,128)(2,1)S(1)}, u32[]{:S(2)}, u32[]{:S(2)}) collective-permute-start(bf16[64,1280]{1,0:T(8,128)(2,1)S(1)} %fusion.1), channel_id=1, source_target_pairs={{0,8},{8,16},{16,24},{24,0},{1,9},{9,17},{17,25},{25,1},{2,10},{10... | collective-permute-start | bytes 491528 | tf_op jit(solution)/shard_map/ppermute | solution.py:23
  60.6 8.0 %collective-permute-start.24 = (bf16[64,1280]{1,0:T(8,128)(2,1)S(1)}, bf16[64,1280]{1,0:T(8,128)(2,1)S(1)}, u32[]{:S(2)}, u32[]{:S(2)}) collective-permute-start(bf16[64,1280]{1,0:T(8,128)(2,1)S(1)} %fusion), channel_id=1, source_target_pairs={{0,8},{8,16},{16,24},{24,0},{1,9},{9,17},{17,25},{25,1},{2,10},{10... | collective-permute-start | bytes 491528 | tf_op jit(solution)/shard_map/ppermute | solution.py:23

commit v4 on v3

--- a/solution.py
+++ b/solution.py
@@ -70,20 +70,31 @@
     far_copy.wait()
 
 
-def pass_kernel(count, *refs):
-    for value, out in zip(refs[:count], refs[-count:]):
-        out[...] = value[...]
-
-
-def passed(values, *tokens):
+def pass_kernel(ranges, *refs):
+    count = len(ranges)
+    for value, out, (start, stop) in zip(refs[:count], refs[-count:], ranges):
+        out[...] = value[:, start:stop]
+
+
+def passed(values, *tokens, ranges=None):
     vmem, anywhere = pl.BlockSpec(memory_space=pltpu.VMEM), pl.BlockSpec(memory_space=pl.ANY)
+    ranges = ranges or [(0, value.shape[1]) for value in values]
     return call(
-        functools.partial(pass_kernel, len(values)),
-        [shape(*value.shape, value.dtype) for value in values],
+        functools.partial(pass_kernel, ranges),
+        [
+            shape(value.shape[0], stop - start, value.dtype)
+            for value, (start, stop) in zip(values, ranges)
+        ],
         0,
         1 << 20,
         in_specs=[vmem] * len(values) + [anywhere] * len(tokens),
     )(*[in_vmem(value) for value in values], *tokens)
+
+
+def split_columns(wide, count):
+    tiles = wide // HD
+    cuts = [tiles * at // count * HD for at in range(count + 1)]
+    return list(zip(cuts[:-1], cuts[1:]))
 
 
 def fill_tables(rows, block_rows, place, lengths, cosine, sine, allowed):
@@ -129,6 +140,11 @@
 
 def stacked(pieces):
     return jnp.concatenate([piece[...] for piece in pieces], axis=0)
+
+
+def stacked_parts(own, parts):
+    other = jnp.concatenate([part[...] for part in parts], axis=1) if len(parts) > 1 else parts[0][...]
+    return jnp.concatenate([own[...], other], axis=0)
 
 
 def put(total, to, *outs):
@@ -168,22 +184,23 @@
             query[:, at + head : at + head + HD] = turned.astype(query.dtype)
 
 
-def project_kernel(n0, n1, f0, f1, key, value, own_sum, own_send, far_sum):
+def project_kernel(n0, n1, f0, f1, key, value, own_sum, send, rest):
     rows = stacked((n0, n1, f0, f1))
-    whole, wide = own_sum.shape[0], key.shape[1]
+    whole, ready, wide = own_sum.shape[0], send.shape[0], key.shape[1]
     for index, weight in enumerate((key, value)):
         to = slice(index * wide, (index + 1) * wide)
         total = jnp.dot(rows, weight[...], preferred_element_type=jnp.float32)
-        put(total[:whole], to, own_sum, own_send)
-        put(total[whole:], to, far_sum)
+        put(total[:whole], to, own_sum)
+        put(total[:ready], to, send)
+        put(total[ready:], to, rest)
 
 
 def query_first_kernel(n0, n1, _, w, out):
     out[...] = jnp.dot(stacked((n0, n1)), w[...], preferred_element_type=jnp.float32)
 
 
-def project_more_kernel(x0, x1, w0, w1, before, out):
-    rows = stacked((x0, x1))
+def project_more_kernel(before, x0, w0, w1, *refs):
+    rows, out = stacked_parts(x0, refs[:-1]), refs[-1]
     ready, wide = before.shape[0], w0.shape[1]
     out[:ready, :] = before[...]
     for index, w in enumerate((w0, w1)):
@@ -191,8 +208,8 @@
         out[ready:, index * wide : (index + 1) * wide] = total.astype(out.dtype)
 
 
-def query_last_kernel(f0, f1, w, before, cosine, sine, out):
-    rows = stacked((f0, f1))
+def query_last_kernel(f0, w, before, cosine, sine, *refs):
+    rows, out = stacked_parts(f0, refs[:-1]), refs[-1]
     block = 2 * HD
     turn = pl.ds(3 * rows.shape[0], rows.shape[0])
     for at in range(0, w.shape[1], block):
@@ -213,21 +230,21 @@
     out[part, keys:] = total[:, keys:].astype(out.dtype)
 
 
-def finish_kernel(far, early_a, early_b, cosine, sine, out):
+def finish_kernel(send, far, early_a, early_b, cosine, sine, out):
     rows = early_a.shape[0]
-    for at, early in ((0, early_a), (rows, early_b)):
-        total = early[...].astype(jnp.float32) + far[at : at + rows, :].astype(jnp.float32)
-        finish(total, cosine, sine, out, at)
-
-
-def attend_kernel(group, q_first, q_last, done, sum_a, sum_b, arrived, cosine, sine, allowed, out, kv):
+    early = jnp.concatenate([early_a[...], early_b[:rows, :]], axis=0)
+    far = jnp.concatenate([send[rows:, :], far[...]], axis=0)
+    finish(early.astype(jnp.float32) + far.astype(jnp.float32), cosine, sine, out, 0)
+
+
+def attend_kernel(group, q_first, q_last, done, sum_a, sum_b, more_a, more_b, cosine, sine, allowed, out, kv):
     rows = 2 * q_first.shape[0]
     ready = done.shape[0]
     kv[:ready, :] = done[...]
     half = sum_a.shape[0]
-    for at, own_sum in ((0, sum_a), (half, sum_b)):
-        total = own_sum[...] + arrived[at : at + half, :].astype(jnp.float32)
-        finish(total, cosine, sine, kv, ready + at)
+    total = jnp.concatenate([sum_a[...], sum_b[...]], axis=0)
+    more = jnp.concatenate([more_a[half:, :], more_b[...]], axis=0)
+    finish(total + more.astype(jnp.float32), cosine, sine, kv, ready)
     keys = kv.shape[1] // 2
     allow = jnp.concatenate([allowed[...]] * group, axis=0) > 0.5
     for head in range(0, keys, HD):
@@ -327,8 +344,11 @@
     early_a = swap(send_a, "ctx", 1)
     near_b_s = swap(near_b, "tp", 1)
     far_a_s = swap(far_a, "tp", 1)
-    sum_b, send_b, far_sum_a = call(
-        project_kernel, [*sums, sums[1]], 2 * kv_flops, 8 * rows * half
+    sum_b, send_b, rest = call(
+        project_kernel,
+        [sums[0], shape(3 * rows, kv_wide, jnp.bfloat16), shape(rows, kv_wide, jnp.bfloat16)],
+        2 * kv_flops,
+        8 * rows * half,
     )(near_b, near_b_s, far_a, far_a_s, key, value)
     early_b = swap(send_b, "ctx", 1)
     before = call(
@@ -337,30 +357,34 @@
         4 * rows * half * wide,
         4 * rows * half,
         in_specs=[vmem] * 2 + [anywhere, vmem],
-    )(near_b, near_b_s, send_b, w_near)
-
-    x_again, far_b = passed([x_far, far_b], before, early_a, early_b)
-    far_c = swap(x_again, "tp", 2)
-    far_b_s = swap(far_b, "tp", 1)
-    far_sum = call(
+    )(near_b, near_b_s, early_a, w_near)
+
+    far_c = swap(passed([x_far], before)[0], "tp", 2)
+    parts = split_columns(half, 2)
+    far_b, *pieces = passed(
+        [far_b] * (len(parts) + 1), before, early_b, ranges=[(0, half), *parts]
+    )
+    pieces = [swap(piece, "tp", 1) for piece in pieces]
+    far_sum_b = call(
         project_more_kernel,
-        shape(4 * rows, kv_wide, jnp.bfloat16),
+        shape(3 * rows, kv_wide, jnp.bfloat16),
         kv_flops,
         4 * rows * half,
-    )(far_b, far_b_s, key, value, far_sum_a)
-    arrived = swap(far_sum, "ctx", 1)
-    far_c = passed([far_c], arrived)[0]
-    far_c_s = swap(far_c, "tp", 1)
+    )(rest, far_b, key, value, *pieces)
+    more_b = swap(far_sum_b, "ctx", 1)
+    parts = split_columns(half, 3)
+    pieces = passed([far_c] * len(parts), far_sum_b, ranges=parts)
+    pieces = [swap(piece, "tp", 1) for piece in pieces]
     q_last = call(
         query_last_kernel,
         shape(2 * rows, wide, jnp.bfloat16),
         4 * rows * half * wide,
         8 * rows * half,
-    )(far_c, far_c_s, w_far, before, cosine, sine)
+    )(far_c, w_far, before, cosine, sine, *pieces)
 
     kv_shape = shape(4 * rows, kv_wide, jnp.bfloat16)
     done = call(finish_kernel, kv_shape, 1 << 24, 1 << 20)(
-        far_sum, early_a, early_b, cosine, sine
+        send_b, far_sum_b, early_a, early_b, cosine, sine
     )
     attended = call(
         functools.partial(attend_kernel, group),
@@ -368,7 +392,7 @@
         8 * rows * 8 * rows * wide,
         1 << 20,
         scratch_shapes=[pltpu.VMEM((8 * rows, kv_wide), jnp.bfloat16)],
-    )(q_first, q_last, done, sum_a, sum_b, arrived, cosine, sine, allowed)
+    )(q_first, q_last, done, sum_a, sum_b, early_b, more_b, cosine, sine, allowed)
 
     w_out = in_vmem(w_out)
     wide = w_out.shape[1] // OUT_CHUNKS

time: 69.7 us -> 67 us (0.961)
  waiting for transfers between devices: 28.2 us -> 25.9 us
    ppermute x21 -> x24, waiting for transfers between devices: 21.9 us -> 19.5 us  [swap(): lax.ppermute(value, axis, [(source, source ^ bit) for source in range(cou...]
    ppermute x21 -> x24, starting transfers between devices: 17.1 us -> 16.7 us  [swap(): lax.ppermute(value, axis, [(source, source ^ bit) for source in range(cou...]
    pallas_call x5 -> x6, Pallas kernels: 1.47 us -> 1.5 us  [the longest x1 0.84 us: on_four_by_two(): call(project_kernel, [sums[0], shape(3 * rows, kv_wide, jnp.bfloat16), sh...]
  transfers between devices with their start and end apart: 25 -> 28, of which waited for: 12 -> 16; matrix products, arithmetic and copies ran while one was open for 1% -> 1% of each run, Pallas kernels for 15% -> 18%
where the time goes in v4:
time: 67 us; the launch traced here: 66.9 us
  waiting for transfers between devices  25.9 us (39%)
  starting transfers between devices  23.2 us (35%)
  Pallas kernels  15.4 us (23%)
  other arithmetic  1.3 us (2%)
  local copies, waits for them, and re-layouts  0.74 us (1%)
    ppermute x24, waiting for transfers between devices, swap(): lax.ppermute(value, axis, [(source, source ^ bit) for source in range(cou...  19.5 us
    ppermute x24, starting transfers between devices, swap(): lax.ppermute(value, axis, [(source, source ^ bit) for source in range(cou...  16.7 us
    ppermute x4, starting transfers between devices, from_behind(): return lax.ppermute(value, axis, pairs)  6.49 us
    ppermute x4, waiting for transfers between devices, from_behind(): return lax.ppermute(value, axis, pairs)  6.48 us
    pallas_call x1, Pallas kernels, on_four_by_two(): call(functools.partial(own_kernel, block_rows), [*sums, shape(2 * rows, w...  6.33 us
    pallas_call x4, Pallas kernels, project_out(): call(functools.partial(out_kernel, first), [shape(rows // 2, wide, jnp.fl...  2.73 us
    pallas_call x1, Pallas kernels, on_four_by_two(): call(split_kernel, [shape(rows, half, own.dtype)] * 2, 0, 1 << 20, in_spe...  1.63 us
  transfers between devices with their start and end apart: 28, of which 16 were waited for; matrix products, arithmetic and copies ran while one was open for 1% of the time, Pallas kernels for 18%

profile of v4, /device:TPU:0, one launch (start us, length us, event | category | flops | bytes accessed | tf_op | source)
XLA Modules:
  0.0 66.9 jit_solution(10570104090125612518)
XLA Ops:
  0.0 0.1 pad_add_fusion.place
  0.1 1.6 %shard_map.64 = (bf16[64,2560]{1,0:T(8,128)(2,1)S(1)}, bf16[64,2560]{1,0:T(8,128)(2,1)S(1)}) custom-call(s32[2]{0:T(128)S(1)} %pad_add_fusion.place, bf16[64,5120]{1,0:T(8,128)(2,1)} %bitcast.18), custom_call_target="tpu_custom_call" | custom-call | bytes 1048576 | tf_op jit(solution)/shard_map/pallas_call | solution.py:303
  1.7 0.5 collective-permute-start
  2.2 0.1 collective-permute-start.1
  2.3 2.9 %collective-permute-start.2 = (bf16[64,2560]{1,0:T(8,128)(2,1)S(1)}, bf16[64,2560]{1,0:T(8,128)(2,1)S(1)}, u32[]{:S(2)}, u32[]{:S(2)}) collective-permute-start(bf16[64,2560]{1,0:T(8,128)(2,1)S(1)} %get-tuple-element.38.f0.refs_0_), channel_id=1, source_target_pairs={{0,4},{4,0},{1,5},{5,1},{2,6},{6,2},{3,7},{7,3},{8,12},{12,8},{9,1... | collective-permute-start | bytes 983048 | tf_op jit(solution)/shard_map/ppermute | solution.py:28
  5.2 1.5 %collective-permute-start.3 = (bf16[64,2560]{1,0:T(8,128)(2,1)S(1)}, bf16[64,2560]{1,0:T(8,128)(2,1)S(1)}, u32[]{:S(2)}, u32[]{:S(2)}) collective-permute-start(bf16[64,2560]{1,0:T(8,128)(2,1)S(1)} %get-tuple-element.37.n0), channel_id=1, source_target_pairs={{0,2},{1,3},{2,0},{3,1},{4,6},{5,7},{6,4},{7,5},{8,10},{9,11},{10,... | collective-permute-start | bytes 983048 | tf_op jit(solution)/shard_map/ppermute | solution.py:28
  6.8 0.7 copy-done
  7.4 6.3 %shard_map.65 = (f32[128,512]{1,0:T(8,128)S(1)}, bf16[128,512]{1,0:T(8,128)(2,1)S(1)}, bf16[128,768]{1,0:T(8,128)(2,1)S(1)}, bf16[2560,256]{1,0:T(8,128)(2,1)S(1...) custom-call(s32[2]{0:T(128)S(1)} %pad_add_fusion.place, ...), custom_call_target="tpu_custom_call" | custom-call | flops 1342177280 | bytes 1310720 | tf_op jit(solution)/shard_map/pallas_call | solution.py:320
  13.8 0.9 %collective-permute-done.3.refs_1_ = bf16[64,2560]{1,0:T(8,128)(2,1)S(1)} collective-permute-done((bf16[64,2560]{1,0:T(8,128)(2,1)S(1)}, bf16[64,2560]{1,0:T(8,128)(2,1)S(1)}, u32[]{:S(2)}, u32[]{:S(2)}) %collective-permute-start.3) | collective-permute-done | bytes 327712 | tf_op jit(solution)/shard_map/ppermute | solution.py:28
  14.6 0.1 shard_map.66
  14.7 0.1 collective-permute-start.4
  14.8 0.5 collective-permute-start.7
  15.3 1.5 %collective-permute-start.8 = (bf16[64,2560]{1,0:T(8,128)(2,1)S(1)}, bf16[64,2560]{1,0:T(8,128)(2,1)S(1)}, u32[]{:S(2)}, u32[]{:S(2)}) collective-permute-start(bf16[64,2560]{1,0:T(8,128)(2,1)S(1)} %get-tuple-element.47.f0), channel_id=1, source_target_pairs={{0,2},{1,3},{2,0},{3,1},{4,6},{5,7},{6,4},{7,5},{8,10},{9,11},{10,... | collective-permute-start | bytes 983048 | tf_op jit(solution)/shard_map/ppermute | solution.py:28
  16.8 0.5 collective-permute-start.5
  17.3 0.8 %shard_map.69 = (f32[128,512]{1,0:T(8,128)S(1)}, bf16[192,512]{1,0:T(8,128)(2,1)S(1)}, bf16[64,512]{1,0:T(8,128)(2,1)S(1)}) custom-call(bf16[64,2560]{1,0:T(8,128)(2,1)S(1)} %get-tuple-element.41.n0, bf16[64,2560]{1,0:T(8,128)(2,1)S(1)} %collective-permute-done.4.n1, bf16[64,2560]{1,0:T(8,128)(2,1)S(1)} %get-tuple-element.47.f0, ...), custom_call_target="tpu_custom_call" | custom-call | flops 671088640 | bytes 1310720 | tf_op jit(solution)/shard_map/pallas_call | solution.py:347
  18.2 1.6 %collective-permute-start.9 = (bf16[192,512]{1,0:T(8,128)(2,1)S(1)}, bf16[192,512]{1,0:T(8,128)(2,1)S(1)}, u32[]{:S(2)}, u32[]{:S(2)}) collective-permute-start(bf16[192,512]{1,0:T(8,128)(2,1)S(1)} %get-tuple-element.51.send), channel_id=1, source_target_pairs={{0,4},{4,0},{1,5},{5,1},{2,6},{6,2},{3,7},{7,3},{8,12},{12,8},{9,1... | collective-permute-start | bytes 589832 | tf_op jit(solution)/shard_map/ppermute | solution.py:28
  19.7 3.4 %collective-permute-done.5._.early_a = bf16[128,512]{1,0:T(8,128)(2,1)S(1)} collective-permute-done((bf16[128,512]{1,0:T(8,128)(2,1)S(1)}, bf16[128,512]{1,0:T(8,128)(2,1)S(1)}, u32[]{:S(2)}, u32[]{:S(2)}) %collective-permute-start.5) | collective-permute-done | bytes 131104 | tf_op jit(solution)/shard_map/ppermute | solution.py:28
  23.2 0.7 %shard_map.67.refs_1_.refs_3_.before = f32[128,768]{1,0:T(8,128)S(1)} custom-call(bf16[64,2560]{1,0:T(8,128)(2,1)S(1)} %get-tuple-element.41.n0, bf16[64,2560]{1,0:T(8,128)(2,1)S(1)} %collective-permute-done.4.n1, bf16[128,512]{1,0:T(8,128)(2,1)S(1)} %collective-permute-done.5._.early_a, bf16[2560,768]{1,0:T(8,128)(2,1)S(1)} %get-tuple-element.43.w), custom_call_target="tpu_custom_call" | custom-call | flops 503316480 | bytes 655360 | tf_op jit(solution)/shard_map/pallas_call | solution.py:354
  23.9 0.1 collective-permute-start.6
  24.0 1.6 %collective-permute-done.8.refs_0_.refs_1_.refs_2_ = bf16[64,2560]{1,0:T(8,128)(2,1)S(1)} collective-permute-done((bf16[64,2560]{1,0:T(8,128)(2,1)S(1)}, bf16[64,2560]{1,0:T(8,128)(2,1)S(1)}, u32[]{:S(2)}, u32[]{:S(2)}) %collective-permute-start.8) | collective-permute-done | bytes 327712 | tf_op jit(solution)/shard_map/ppermute | solution.py:28
  25.6 0.6 collective-permute-done.9.refs_4_.early_b.more_a
  26.3 0.1 collective-permute-start.10
  26.3 0.5 collective-permute-start.11
  26.8 0.9 %collective-permute-done.10.refs_0_ = bf16[64,1280]{1,0:T(8,128)(2,1)S(1)} collective-permute-done((bf16[64,1280]{1,0:T(8,128)(2,1)S(1)}, bf16[64,1280]{1,0:T(8,128)(2,1)S(1)}, u32[]{:S(2)}, u32[]{:S(2)}) %collective-permute-start.10) | collective-permute-done | bytes 163872 | tf_op jit(solution)/shard_map/ppermute | solution.py:28
  27.7 0.2 collective-permute-done.11.refs_1_
  28.0 0.5 shard_map.71.refs_3_.far
  28.5 0.6 collective-permute-start.15
  29.1 2.9 %collective-permute-done.6.refs_0_.refs_1_.refs_2_.f0 = bf16[64,2560]{1,0:T(8,128)(2,1)S(1)} collective-permute-done((bf16[64,2560]{1,0:T(8,128)(2,1)S(1)}, bf16[64,2560]{1,0:T(8,128)(2,1)S(1)}, u32[]{:S(2)}, u32[]{:S(2)}) %collective-permute-start.6) | collective-permute-done | bytes 327712 | tf_op jit(solution)/shard_map/ppermute | solution.py:28
  32.0 0.1 collective-permute-start.13
  32.1 0.5 collective-permute-start.14
  32.6 0.1 collective-permute-start.12
  32.7 0.3 shard_map.74.done
  33.0 0.9 %collective-permute-done.12.refs_0_ = bf16[64,768]{1,0:T(8,128)(2,1)S(1)} collective-permute-done((bf16[64,768]{1,0:T(8,128)(2,1)S(1)}, bf16[64,768]{1,0:T(8,128)(2,1)S(1)}, u32[]{:S(2)}, u32[]{:S(2)}) %collective-permute-start.12) | collective-permute-done | bytes 98336 | tf_op jit(solution)/shard_map/ppermute | solution.py:28
  33.9 0.9 %shard_map.73.q_last = bf16[128,768]{1,0:T(8,128)(2,1)S(1)} custom-call(bf16[64,2560]{1,0:T(8,128)(2,1)S(1)} %collective-permute-done.6.refs_0_.refs_1_.refs_2_.f0, bf16[2560,768]{1,0:T(8,128)(2,1)S(1)} %get-tuple-element.44.w, f32[128,768]{1,0:T(8,128)S(1)} %shard_map.67.refs_1_.refs_3_.before, f32[512,128]{1,0:T(8,128)S(1)} %get-tuple-element.45.cosine, ...), custom_call_target="tpu_custom_call" | custom-call | flops 503316480 | bytes 1310720 | tf_op jit(solution)/shard_map/pallas_call | solution.py:378
  34.8 0.8 %collective-permute-done.15.more_b = bf16[192,512]{1,0:T(8,128)(2,1)S(1)} collective-permute-done((bf16[192,512]{1,0:T(8,128)(2,1)S(1)}, bf16[192,512]{1,0:T(8,128)(2,1)S(1)}, u32[]{:S(2)}, u32[]{:S(2)}) %collective-permute-start.15) | collective-permute-done | bytes 196640 | tf_op jit(solution)/shard_map/ppermute | solution.py:28
  35.6 1.3 %shard_map.75.attended = bf16[256,768]{1,0:T(8,128)(2,1)S(1)} custom-call(bf16[128,768]{1,0:T(8,128)(2,1)S(1)} %get-tuple-element.39.q_first, bf16[128,768]{1,0:T(8,128)(2,1)S(1)} %shard_map.73.q_last, bf16[256,512]{1,0:T(8,128)(2,1)S(1)} %shard_map.74.done, f32[128,512]{1,0:T(8,128)S(1)} %get-tuple-element.58.sum_a, ...), custom_call_target="tpu_custom_call" | custom-call | flops 201326592 | bytes 1048576 | tf_op jit(solution)/shard_map/pallas_call | solution.py:389
  37.0 0.7 %shard_map.79 = (f32[128,1280]{1,0:T(8,128)S(1)}, bf16[128,1280]{1,0:T(8,128)(2,1)S(1)}) custom-call(bf16[256,768]{1,0:T(8,128)(2,1)S(1)} %shard_map.75.attended, bf16[768,5120]{1,0:T(8,128)(2,1)S(1)} %bitcast.11), custom_call_target="tpu_custom_call" | custom-call | flops 503316480 | bytes 393216 | tf_op jit(solution)/shard_map/pallas_call | solution.py:282
  37.7 0.1 collective-permute-start.25
  37.8 0.7 %shard_map.78 = (f32[128,1280]{1,0:T(8,128)S(1)}, bf16[128,1280]{1,0:T(8,128)(2,1)S(1)}) custom-call(bf16[256,768]{1,0:T(8,128)(2,1)S(1)} %shard_map.75.attended, bf16[768,5120]{1,0:T(8,128)(2,1)S(1)} %bitcast.12), custom_call_target="tpu_custom_call" | custom-call | flops 503316480 | bytes 393216 | tf_op jit(solution)/shard_map/pallas_call | solution.py:282
  38.4 0.6 collective-permute-start.22
  39.0 0.7 %shard_map.77 = (f32[128,1280]{1,0:T(8,128)S(1)}, bf16[128,1280]{1,0:T(8,128)(2,1)S(1)}) custom-call(bf16[256,768]{1,0:T(8,128)(2,1)S(1)} %shard_map.75.attended, bf16[768,5120]{1,0:T(8,128)(2,1)S(1)} %bitcast.13), custom_call_target="tpu_custom_call" | custom-call | flops 503316480 | bytes 393216 | tf_op jit(solution)/shard_map/pallas_call | solution.py:282
  39.7 0.1 collective-permute-start.19
  39.8 0.7 %shard_map.76 = (f32[128,1280]{1,0:T(8,128)S(1)}, bf16[128,1280]{1,0:T(8,128)(2,1)S(1)}) custom-call(bf16[256,768]{1,0:T(8,128)(2,1)S(1)} %shard_map.75.attended, bf16[768,5120]{1,0:T(8,128)(2,1)S(1)} %bitcast.14), custom_call_target="tpu_custom_call" | custom-call | flops 503316480 | bytes 393216 | tf_op jit(solution)/shard_map/pallas_call | solution.py:282
  40.5 0.6 collective-permute-start.16
  41.0 0.1 convert_add_fusion
  41.1 1.2 %collective-permute-start.26 = (bf16[64,1280]{1,0:T(8,128)(2,1)S(1)}, bf16[64,1280]{1,0:T(8,128)(2,1)S(1)}, u32[]{:S(2)}, u32[]{:S(2)}) collective-permute-start(bf16[64,1280]{1,0:T(8,128)(2,1)S(1)} %slice.60), channel_id=1, source_target_pairs={{0,2},{1,3},{2,0},{3,1},{4,6},{5,7},{6,4},{7,5},{8,10},{9,11},{10,... | collective-permute-start | bytes 491528 | tf_op jit(solution)/shard_map/ppermute | solution.py:28
  42.3 0.1 convert_add_fusion.1
  42.4 0.9 %collective-permute-start.23 = (bf16[64,1280]{1,0:T(8,128)(2,1)S(1)}, bf16[64,1280]{1,0:T(8,128)(2,1)S(1)}, u32[]{:S(2)}, u32[]{:S(2)}) collective-permute-start(bf16[64,1280]{1,0:T(8,128)(2,1)S(1)} %slice.61), channel_id=1, source_target_pairs={{0,2},{1,3},{2,0},{3,1},{4,6},{5,7},{6,4},{7,5},{8,10},{9,11},{10,... | collective-permute-start | bytes 491528 | tf_op jit(solution)/shard_map/ppermute | solution.py:28
  43.4 0.1 convert_add_fusion.2
  43.5 1.2 %collective-permute-start.20 = (bf16[64,1280]{1,0:T(8,128)(2,1)S(1)}, bf16[64,1280]{1,0:T(8,128)(2,1)S(1)}, u32[]{:S(2)}, u32[]{:S(2)}) collective-permute-start(bf16[64,1280]{1,0:T(8,128)(2,1)S(1)} %slice.62), channel_id=1, source_target_pairs={{0,2},{1,3},{2,0},{3,1},{4,6},{5,7},{6,4},{7,5},{8,10},{9,11},{10,... | collective-permute-start | bytes 491528 | tf_op jit(solution)/shard_map/ppermute | solution.py:28
  44.7 0.1 convert_add_fusion.3
  44.8 0.9 %collective-permute-start.17 = (bf16[64,1280]{1,0:T(8,128)(2,1)S(1)}, bf16[64,1280]{1,0:T(8,128)(2,1)S(1)}, u32[]{:S(2)}, u32[]{:S(2)}) collective-permute-start(bf16[64,1280]{1,0:T(8,128)(2,1)S(1)} %slice.63), channel_id=1, source_target_pairs={{0,2},{1,3},{2,0},{3,1},{4,6},{5,7},{6,4},{7,5},{8,10},{9,11},{10,... | collective-permute-start | bytes 491528 | tf_op jit(solution)/shard_map/ppermute | solution.py:28
  45.7 2.5 %collective-permute-done.26 = bf16[64,1280]{1,0:T(8,128)(2,1)S(1)} collective-permute-done((bf16[64,1280]{1,0:T(8,128)(2,1)S(1)}, bf16[64,1280]{1,0:T(8,128)(2,1)S(1)}, u32[]{:S(2)}, u32[]{:S(2)}) %collective-permute-start.26) | collective-permute-done | bytes 163872 | tf_op jit(solution)/shard_map/ppermute | solution.py:28
  48.3 1.6 %collective-permute-start.27 = (bf16[64,1280]{1,0:T(8,128)(2,1)S(1)}, bf16[64,1280]{1,0:T(8,128)(2,1)S(1)}, u32[]{:S(2)}, u32[]{:S(2)}) collective-permute-start(bf16[64,1280]{1,0:T(8,128)(2,1)S(1)} %fusion), channel_id=1, source_target_pairs={{0,8},{8,16},{16,24},{24,0},{1,9},{9,17},{17,25},{25,1},{2,10},{10... | collective-permute-start | bytes 491528 | tf_op jit(solution)/shard_map/ppermute | solution.py:23
  49.9 1.9 %collective-permute-done.23 = bf16[64,1280]{1,0:T(8,128)(2,1)S(1)} collective-permute-done((bf16[64,1280]{1,0:T(8,128)(2,1)S(1)}, bf16[64,1280]{1,0:T(8,128)(2,1)S(1)}, u32[]{:S(2)}, u32[]{:S(2)}) %collective-permute-start.23) | collective-permute-done | bytes 163872 | tf_op jit(solution)/shard_map/ppermute | solution.py:28
  51.8 1.6 %collective-permute-start.24 = (bf16[64,1280]{1,0:T(8,128)(2,1)S(1)}, bf16[64,1280]{1,0:T(8,128)(2,1)S(1)}, u32[]{:S(2)}, u32[]{:S(2)}) collective-permute-start(bf16[64,1280]{1,0:T(8,128)(2,1)S(1)} %fusion.1), channel_id=1, source_target_pairs={{0,8},{8,16},{16,24},{24,0},{1,9},{9,17},{17,25},{25,1},{2,10},{10... | collective-permute-start | bytes 491528 | tf_op jit(solution)/shard_map/ppermute | solution.py:23
  53.4 1.9 %collective-permute-done.20 = bf16[64,1280]{1,0:T(8,128)(2,1)S(1)} collective-permute-done((bf16[64,1280]{1,0:T(8,128)(2,1)S(1)}, bf16[64,1280]{1,0:T(8,128)(2,1)S(1)}, u32[]{:S(2)}, u32[]{:S(2)}) %collective-permute-start.20) | collective-permute-done | bytes 163872 | tf_op jit(solution)/shard_map/ppermute | solution.py:28
  55.3 1.6 %collective-permute-start.21 = (bf16[64,1280]{1,0:T(8,128)(2,1)S(1)}, bf16[64,1280]{1,0:T(8,128)(2,1)S(1)}, u32[]{:S(2)}, u32[]{:S(2)}) collective-permute-start(bf16[64,1280]{1,0:T(8,128)(2,1)S(1)} %fusion.2), channel_id=1, source_target_pairs={{0,8},{8,16},{16,24},{24,0},{1,9},{9,17},{17,25},{25,1},{2,10},{10... | collective-permute-start | bytes 491528 | tf_op jit(solution)/shard_map/ppermute | solution.py:23
  56.9 0.9 %collective-permute-done.17 = bf16[64,1280]{1,0:T(8,128)(2,1)S(1)} collective-permute-done((bf16[64,1280]{1,0:T(8,128)(2,1)S(1)}, bf16[64,1280]{1,0:T(8,128)(2,1)S(1)}, u32[]{:S(2)}, u32[]{:S(2)}) %collective-permute-start.17) | collective-permute-done | bytes 163872 | tf_op jit(solution)/shard_map/ppermute | solution.py:28
  57.9 1.6 %collective-permute-start.18 = (bf16[64,1280]{1,0:T(8,128)(2,1)S(1)}, bf16[64,1280]{1,0:T(8,128)(2,1)S(1)}, u32[]{:S(2)}, u32[]{:S(2)}) collective-permute-start(bf16[64,1280]{1,0:T(8,128)(2,1)S(1)} %fusion.3), channel_id=1, source_target_pairs={{0,8},{8,16},{16,24},{24,0},{1,9},{9,17},{17,25},{25,1},{2,10},{10... | collective-permute-start | bytes 491528 | tf_op jit(solution)/shard_map/ppermute | solution.py:23
  59.5 0.4 collective-permute-done.24
  59.9 3.5 %collective-permute-done.21 = bf16[64,1280]{1,0:T(8,128)(2,1)S(1)} collective-permute-done((bf16[64,1280]{1,0:T(8,128)(2,1)S(1)}, bf16[64,1280]{1,0:T(8,128)(2,1)S(1)}, u32[]{:S(2)}, u32[]{:S(2)}) %collective-permute-start.21) | collective-permute-done | bytes 163872 | tf_op jit(solution)/shard_map/ppermute | solution.py:23
  63.4 2.6 %collective-permute-done.18 = bf16[64,1280]{1,0:T(8,128)(2,1)S(1)} collective-permute-done((bf16[64,1280]{1,0:T(8,128)(2,1)S(1)}, bf16[64,1280]{1,0:T(8,128)(2,1)S(1)}, u32[]{:S(2)}, u32[]{:S(2)}) %collective-permute-start.18) | collective-permute-done | bytes 163872 | tf_op jit(solution)/shard_map/ppermute | solution.py:23
  66.0 0.9 %maximum_bitcast_fusion = bf16[1,64,5120]{2,1,0:T(8,128)(2,1)} fusion(bf16[64,1280]{1,0:T(8,128)(2,1)S(1)} %collective-permute-done.27, bf16[64,1280]{1,0:T(8,128)(2,1)S(1)} %collective-permute-done.24, bf16[64,1280]{1,0:T(8,128)(2,1)S(1)} %collective-permute-done.21, bf16[64,1280]{1,0:T(8,128)(2,1)S(1)} %collective-permute-done.18), kind=kLoop, calls=%fused_computation | loop fusion | flops 2621440 | bytes 1310720 | tf_op jit(solution)/shard_map/broadcast_in_dim | solution.py:406
  (29 shorter events, 0.3 us)
Async XLA Ops:
  1.7 5.0 %collective-permute-start = (bf16[64,2560]{1,0:T(8,128)(2,1)S(1)}, bf16[64,2560]{1,0:T(8,128)(2,1)S(1)}, u32[]{:S(2)}, u32[]{:S(2)}) collective-permute-start(bf16[64,2560]{1,0:T(8,128)(2,1)S(1)} %get-tuple-element.37.n0), channel_id=1, source_target_pairs={{0,1},{1,0},{2,3},{3,2},{4,5},{5,4},{6,7},{7,6},{8,9},{9,8},{10,11... | collective-permute-start | bytes 983048 | tf_op jit(solution)/shard_map/ppermute | solution.py:28
  2.2 4.5 %collective-permute-start.1 = (bf16[64,2560]{1,0:T(8,128)(2,1)S(1)}, bf16[64,2560]{1,0:T(8,128)(2,1)S(1)}, u32[]{:S(2)}, u32[]{:S(2)}) collective-permute-start(bf16[64,2560]{1,0:T(8,128)(2,1)S(1)} %get-tuple-element.38.f0.refs_0_), channel_id=1, source_target_pairs={{0,1},{1,0},{2,3},{3,2},{4,5},{5,4},{6,7},{7,6},{8,9},{9,8},{10,11... | collective-permute-start | bytes 983048 | tf_op jit(solution)/shard_map/ppermute | solution.py:28
  2.3 11.4 %collective-permute-start.2 = (bf16[64,2560]{1,0:T(8,128)(2,1)S(1)}, bf16[64,2560]{1,0:T(8,128)(2,1)S(1)}, u32[]{:S(2)}, u32[]{:S(2)}) collective-permute-start(bf16[64,2560]{1,0:T(8,128)(2,1)S(1)} %get-tuple-element.38.f0.refs_0_), channel_id=1, source_target_pairs={{0,4},{4,0},{1,5},{5,1},{2,6},{6,2},{3,7},{7,3},{8,12},{12,8},{9,1... | collective-permute-start | bytes 983048 | tf_op jit(solution)/shard_map/ppermute | solution.py:28
  5.2 9.4 %collective-permute-start.3 = (bf16[64,2560]{1,0:T(8,128)(2,1)S(1)}, bf16[64,2560]{1,0:T(8,128)(2,1)S(1)}, u32[]{:S(2)}, u32[]{:S(2)}) collective-permute-start(bf16[64,2560]{1,0:T(8,128)(2,1)S(1)} %get-tuple-element.37.n0), channel_id=1, source_target_pairs={{0,2},{1,3},{2,0},{3,1},{4,6},{5,7},{6,4},{7,5},{8,10},{9,11},{10,... | collective-permute-start | bytes 983048 | tf_op jit(solution)/shard_map/ppermute | solution.py:28
  6.8 0.7 copy-start
  14.7 2.6 %collective-permute-start.4 = (bf16[64,2560]{1,0:T(8,128)(2,1)S(1)}, bf16[64,2560]{1,0:T(8,128)(2,1)S(1)}, u32[]{:S(2)}, u32[]{:S(2)}) collective-permute-start(bf16[64,2560]{1,0:T(8,128)(2,1)S(1)} %get-tuple-element.41.n0), channel_id=1, source_target_pairs={{0,1},{1,0},{2,3},{3,2},{4,5},{5,4},{6,7},{7,6},{8,9},{9,8},{10,11... | collective-permute-start | bytes 983048 | tf_op jit(solution)/shard_map/ppermute | solution.py:28
  14.8 2.6 %collective-permute-start.7 = (bf16[64,2560]{1,0:T(8,128)(2,1)S(1)}, bf16[64,2560]{1,0:T(8,128)(2,1)S(1)}, u32[]{:S(2)}, u32[]{:S(2)}) collective-permute-start(bf16[64,2560]{1,0:T(8,128)(2,1)S(1)} %get-tuple-element.47.f0), channel_id=1, source_target_pairs={{0,1},{1,0},{2,3},{3,2},{4,5},{5,4},{6,7},{7,6},{8,9},{9,8},{10,11... | collective-permute-start | bytes 983048 | tf_op jit(solution)/shard_map/ppermute | solution.py:28
  15.3 10.3 %collective-permute-start.8 = (bf16[64,2560]{1,0:T(8,128)(2,1)S(1)}, bf16[64,2560]{1,0:T(8,128)(2,1)S(1)}, u32[]{:S(2)}, u32[]{:S(2)}) collective-permute-start(bf16[64,2560]{1,0:T(8,128)(2,1)S(1)} %get-tuple-element.47.f0), channel_id=1, source_target_pairs={{0,2},{1,3},{2,0},{3,1},{4,6},{5,7},{6,4},{7,5},{8,10},{9,11},{10,... | collective-permute-start | bytes 983048 | tf_op jit(solution)/shard_map/ppermute | solution.py:28
  16.8 6.4 %collective-permute-start.5 = (bf16[128,512]{1,0:T(8,128)(2,1)S(1)}, bf16[128,512]{1,0:T(8,128)(2,1)S(1)}, u32[]{:S(2)}, u32[]{:S(2)}) collective-permute-start(bf16[128,512]{1,0:T(8,128)(2,1)S(1)} %get-tuple-element.42), channel_id=1, source_target_pairs={{0,4},{4,0},{1,5},{5,1},{2,6},{6,2},{3,7},{7,3},{8,12},{12,8},{9,1... | collective-permute-start | bytes 393224 | tf_op jit(solution)/shard_map/ppermute | solution.py:28
  18.2 8.0 %collective-permute-start.9 = (bf16[192,512]{1,0:T(8,128)(2,1)S(1)}, bf16[192,512]{1,0:T(8,128)(2,1)S(1)}, u32[]{:S(2)}, u32[]{:S(2)}) collective-permute-start(bf16[192,512]{1,0:T(8,128)(2,1)S(1)} %get-tuple-element.51.send), channel_id=1, source_target_pairs={{0,4},{4,0},{1,5},{5,1},{2,6},{6,2},{3,7},{7,3},{8,12},{12,8},{9,1... | collective-permute-start | bytes 589832 | tf_op jit(solution)/shard_map/ppermute | solution.py:28
  23.9 8.1 %collective-permute-start.6 = (bf16[64,2560]{1,0:T(8,128)(2,1)S(1)}, bf16[64,2560]{1,0:T(8,128)(2,1)S(1)}, u32[]{:S(2)}, u32[]{:S(2)}) collective-permute-start(bf16[64,2560]{1,0:T(8,128)(2,1)S(1)} %shard_map.68), channel_id=1, source_target_pairs={{0,2},{1,3},{2,0},{3,1},{4,6},{5,7},{6,4},{7,5},{8,10},{9,11},{10,... | collective-permute-start | bytes 983048 | tf_op jit(solution)/shard_map/ppermute | solution.py:28
  26.3 1.5 %collective-permute-start.10 = (bf16[64,1280]{1,0:T(8,128)(2,1)S(1)}, bf16[64,1280]{1,0:T(8,128)(2,1)S(1)}, u32[]{:S(2)}, u32[]{:S(2)}) collective-permute-start(bf16[64,1280]{1,0:T(8,128)(2,1)S(1)} %get-tuple-element.53), channel_id=1, source_target_pairs={{0,1},{1,0},{2,3},{3,2},{4,5},{5,4},{6,7},{7,6},{8,9},{9,8},{10,11... | collective-permute-start | bytes 491528 | tf_op jit(solution)/shard_map/ppermute | solution.py:28
  26.3 1.6 %collective-permute-start.11 = (bf16[64,1280]{1,0:T(8,128)(2,1)S(1)}, bf16[64,1280]{1,0:T(8,128)(2,1)S(1)}, u32[]{:S(2)}, u32[]{:S(2)}) collective-permute-start(bf16[64,1280]{1,0:T(8,128)(2,1)S(1)} %get-tuple-element.54), channel_id=1, source_target_pairs={{0,1},{1,0},{2,3},{3,2},{4,5},{5,4},{6,7},{7,6},{8,9},{9,8},{10,11... | collective-permute-start | bytes 491528 | tf_op jit(solution)/shard_map/ppermute | solution.py:28
  28.0 9.0 %slice-start = ((s8[7864320]{0:T(1024)(128)(4,1)}), s8[4194304]{0:T(1024)(128)(4,1)S(1)}, s32[]{:S(2)}) async-start(s8[7864320]{0:T(1024)(128)(4,1)} %bitcast.9), calls=%async_computation | async-start | bytes 8388608
  28.5 7.2 %collective-permute-start.15 = (bf16[192,512]{1,0:T(8,128)(2,1)S(1)}, bf16[192,512]{1,0:T(8,128)(2,1)S(1)}, u32[]{:S(2)}, u32[]{:S(2)}) collective-permute-start(bf16[192,512]{1,0:T(8,128)(2,1)S(1)} %shard_map.71.refs_3_.far), channel_id=1, source_target_pairs={{0,4},{4,0},{1,5},{5,1},{2,6},{6,2},{3,7},{7,3},{8,12},{12,8},{9,1... | collective-permute-start | bytes 589832 | tf_op jit(solution)/shard_map/ppermute | solution.py:28
  32.0 1.9 %collective-permute-start.13 = (bf16[64,896]{1,0:T(8,128)(2,1)S(1)}, bf16[64,896]{1,0:T(8,128)(2,1)S(1)}, u32[]{:S(2)}, u32[]{:S(2)}) collective-permute-start(bf16[64,896]{1,0:T(8,128)(2,1)S(1)} %get-tuple-element.56), channel_id=1, source_target_pairs={{0,1},{1,0},{2,3},{3,2},{4,5},{5,4},{6,7},{7,6},{8,9},{9,8},{10,11... | collective-permute-start | bytes 344072 | tf_op jit(solution)/shard_map/ppermute | solution.py:28
  32.1 1.8 %collective-permute-start.14 = (bf16[64,896]{1,0:T(8,128)(2,1)S(1)}, bf16[64,896]{1,0:T(8,128)(2,1)S(1)}, u32[]{:S(2)}, u32[]{:S(2)}) collective-permute-start(bf16[64,896]{1,0:T(8,128)(2,1)S(1)} %get-tuple-element.57), channel_id=1, source_target_pairs={{0,1},{1,0},{2,3},{3,2},{4,5},{5,4},{6,7},{7,6},{8,9},{9,8},{10,11... | collective-permute-start | bytes 344072 | tf_op jit(solution)/shard_map/ppermute | solution.py:28
  32.6 1.3 %collective-permute-start.12 = (bf16[64,768]{1,0:T(8,128)(2,1)S(1)}, bf16[64,768]{1,0:T(8,128)(2,1)S(1)}, u32[]{:S(2)}, u32[]{:S(2)}) collective-permute-start(bf16[64,768]{1,0:T(8,128)(2,1)S(1)} %get-tuple-element.55), channel_id=1, source_target_pairs={{0,1},{1,0},{2,3},{3,2},{4,5},{5,4},{6,7},{7,6},{8,9},{9,8},{10,11... | collective-permute-start | bytes 294920 | tf_op jit(solution)/shard_map/ppermute | solution.py:28
  33.9 3.1 %slice-start.1 = ((s8[7864320]{0:T(1024)(128)(4,1)}), s8[3670016]{0:T(1024)(128)(4,1)S(1)}, s32[]{:S(2)}) async-start(s8[7864320]{0:T(1024)(128)(4,1)} %bitcast.9), calls=%async_computation.1 | async-start | bytes 7340032
  37.7 3.4 %collective-permute-start.25 = (bf16[128,1280]{1,0:T(8,128)(2,1)S(1)}, bf16[128,1280]{1,0:T(8,128)(2,1)S(1)}, u32[]{:S(2)}, u32[]{:S(2)}) collective-permute-start(bf16[128,1280]{1,0:T(8,128)(2,1)S(1)} %get-tuple-element.68), channel_id=1, source_target_pairs={{0,1},{1,0},{2,3},{3,2},{4,5},{5,4},{6,7},{7,6},{8,9},{9,8},{10,11... | collective-permute-start | bytes 983048 | tf_op jit(solution)/shard_map/ppermute | solution.py:28
  38.4 3.9 %collective-permute-start.22 = (bf16[128,1280]{1,0:T(8,128)(2,1)S(1)}, bf16[128,1280]{1,0:T(8,128)(2,1)S(1)}, u32[]{:S(2)}, u32[]{:S(2)}) collective-permute-start(bf16[128,1280]{1,0:T(8,128)(2,1)S(1)} %get-tuple-element.66), channel_id=1, source_target_pairs={{0,1},{1,0},{2,3},{3,2},{4,5},{5,4},{6,7},{7,6},{8,9},{9,8},{10,11... | collective-permute-start | bytes 983048 | tf_op jit(solution)/shard_map/ppermute | solution.py:28
  39.7 3.7 %collective-permute-start.19 = (bf16[128,1280]{1,0:T(8,128)(2,1)S(1)}, bf16[128,1280]{1,0:T(8,128)(2,1)S(1)}, u32[]{:S(2)}, u32[]{:S(2)}) collective-permute-start(bf16[128,1280]{1,0:T(8,128)(2,1)S(1)} %get-tuple-element.64), channel_id=1, source_target_pairs={{0,1},{1,0},{2,3},{3,2},{4,5},{5,4},{6,7},{7,6},{8,9},{9,8},{10,11... | collective-permute-start | bytes 983048 | tf_op jit(solution)/shard_map/ppermute | solution.py:28
  40.5 4.2 %collective-permute-start.16 = (bf16[128,1280]{1,0:T(8,128)(2,1)S(1)}, bf16[128,1280]{1,0:T(8,128)(2,1)S(1)}, u32[]{:S(2)}, u32[]{:S(2)}) collective-permute-start(bf16[128,1280]{1,0:T(8,128)(2,1)S(1)} %get-tuple-element.62), channel_id=1, source_target_pairs={{0,1},{1,0},{2,3},{3,2},{4,5},{5,4},{6,7},{7,6},{8,9},{9,8},{10,11... | collective-permute-start | bytes 983048 | tf_op jit(solution)/shard_map/ppermute | solution.py:28
  41.1 7.1 %collective-permute-start.26 = (bf16[64,1280]{1,0:T(8,128)(2,1)S(1)}, bf16[64,1280]{1,0:T(8,128)(2,1)S(1)}, u32[]{:S(2)}, u32[]{:S(2)}) collective-permute-start(bf16[64,1280]{1,0:T(8,128)(2,1)S(1)} %slice.60), channel_id=1, source_target_pairs={{0,2},{1,3},{2,0},{3,1},{4,6},{5,7},{6,4},{7,5},{8,10},{9,11},{10,... | collective-permute-start | bytes 491528 | tf_op jit(solution)/shard_map/ppermute | solution.py:28
  42.4 9.3 %collective-permute-start.23 = (bf16[64,1280]{1,0:T(8,128)(2,1)S(1)}, bf16[64,1280]{1,0:T(8,128)(2,1)S(1)}, u32[]{:S(2)}, u32[]{:S(2)}) collective-permute-start(bf16[64,1280]{1,0:T(8,128)(2,1)S(1)} %slice.61), channel_id=1, source_target_pairs={{0,2},{1,3},{2,0},{3,1},{4,6},{5,7},{6,4},{7,5},{8,10},{9,11},{10,... | collective-permute-start | bytes 491528 | tf_op jit(solution)/shard_map/ppermute | solution.py:28
  43.5 11.8 %collective-permute-start.20 = (bf16[64,1280]{1,0:T(8,128)(2,1)S(1)}, bf16[64,1280]{1,0:T(8,128)(2,1)S(1)}, u32[]{:S(2)}, u32[]{:S(2)}) collective-permute-start(bf16[64,1280]{1,0:T(8,128)(2,1)S(1)} %slice.62), channel_id=1, source_target_pairs={{0,2},{1,3},{2,0},{3,1},{4,6},{5,7},{6,4},{7,5},{8,10},{9,11},{10,... | collective-permute-start | bytes 491528 | tf_op jit(solution)/shard_map/ppermute | solution.py:28
  44.8 13.1 %collective-permute-start.17 = (bf16[64,1280]{1,0:T(8,128)(2,1)S(1)}, bf16[64,1280]{1,0:T(8,128)(2,1)S(1)}, u32[]{:S(2)}, u32[]{:S(2)}) collective-permute-start(bf16[64,1280]{1,0:T(8,128)(2,1)S(1)} %slice.63), channel_id=1, source_target_pairs={{0,2},{1,3},{2,0},{3,1},{4,6},{5,7},{6,4},{7,5},{8,10},{9,11},{10,... | collective-permute-start | bytes 491528 | tf_op jit(solution)/shard_map/ppermute | solution.py:28
  48.3 11.2 %collective-permute-start.27 = (bf16[64,1280]{1,0:T(8,128)(2,1)S(1)}, bf16[64,1280]{1,0:T(8,128)(2,1)S(1)}, u32[]{:S(2)}, u32[]{:S(2)}) collective-permute-start(bf16[64,1280]{1,0:T(8,128)(2,1)S(1)} %fusion), channel_id=1, source_target_pairs={{0,8},{8,16},{16,24},{24,0},{1,9},{9,17},{17,25},{25,1},{2,10},{10... | collective-permute-start | bytes 491528 | tf_op jit(solution)/shard_map/ppermute | solution.py:23
  51.8 8.1 %collective-permute-start.24 = (bf16[64,1280]{1,0:T(8,128)(2,1)S(1)}, bf16[64,1280]{1,0:T(8,128)(2,1)S(1)}, u32[]{:S(2)}, u32[]{:S(2)}) collective-permute-start(bf16[64,1280]{1,0:T(8,128)(2,1)S(1)} %fusion.1), channel_id=1, source_target_pairs={{0,8},{8,16},{16,24},{24,0},{1,9},{9,17},{17,25},{25,1},{2,10},{10... | collective-permute-start | bytes 491528 | tf_op jit(solution)/shard_map/ppermute | solution.py:23
  55.3 8.1 %collective-permute-start.21 = (bf16[64,1280]{1,0:T(8,128)(2,1)S(1)}, bf16[64,1280]{1,0:T(8,128)(2,1)S(1)}, u32[]{:S(2)}, u32[]{:S(2)}) collective-permute-start(bf16[64,1280]{1,0:T(8,128)(2,1)S(1)} %fusion.2), channel_id=1, source_target_pairs={{0,8},{8,16},{16,24},{24,0},{1,9},{9,17},{17,25},{25,1},{2,10},{10... | collective-permute-start | bytes 491528 | tf_op jit(solution)/shard_map/ppermute | solution.py:23
  57.9 8.1 %collective-permute-start.18 = (bf16[64,1280]{1,0:T(8,128)(2,1)S(1)}, bf16[64,1280]{1,0:T(8,128)(2,1)S(1)}, u32[]{:S(2)}, u32[]{:S(2)}) collective-permute-start(bf16[64,1280]{1,0:T(8,128)(2,1)S(1)} %fusion.3), channel_id=1, source_target_pairs={{0,8},{8,16},{16,24},{24,0},{1,9},{9,17},{17,25},{25,1},{2,10},{10... | collective-permute-start | bytes 491528 | tf_op jit(solution)/shard_map/ppermute | solution.py:23

commit v5 on v4

--- a/solution.py
+++ b/solution.py
@@ -12,7 +12,7 @@
 SPAN = 1024
 ROPE_BASE = 500000.0
 NORM_EPS = 1e-06
-OUT_CHUNKS = 4
+OUT_CHUNKS = 5
 MIB = 1 << 20
 VMEM_MIB = 16
 
@@ -55,13 +55,9 @@
     )
 
 
-def after(value, *others):
-    return lax.optimization_barrier((value, *others))[0]
-
-
-def split_kernel(place, value, near, far, sems):
+def split_kernel(value, near, far, sems):
     wide = near.shape[1]
-    at = pl.multiple_of(place[0] * wide, wide)
+    at = pl.multiple_of(lax.axis_index("ctx") * wide, wide)
     near_copy = pltpu.make_async_copy(value.at[:, pl.ds(at, wide)], near, sems.at[0])
     far_copy = pltpu.make_async_copy(value.at[:, pl.ds(wide - at, wide)], far, sems.at[1])
     near_copy.start()
@@ -97,8 +93,8 @@
     return list(zip(cuts[:-1], cuts[1:]))
 
 
-def fill_tables(rows, block_rows, place, lengths, cosine, sine, allowed):
-    start, index = place[0] * block_rows, place[1]
+def fill_tables(rows, block_rows, lengths, cosine, sine, allowed):
+    start, index = lax.axis_index("ctx") * block_rows, lax.axis_index("tp")
     offsets = [start + shift + rows * (index ^ flip) for shift in (-block_rows, 0) for flip in range(4)]
     lane = lax.broadcasted_iota(jnp.int32, (1, HD), 1)
     power = (lane % (HD // 2)).astype(jnp.float32) * (2.0 / HD)
@@ -152,16 +148,17 @@
         out[:, to] = total.astype(out.dtype)
 
 
-def own_kernel(block_rows, place, lengths, n0, n1, f0, f1, w_key, w_value, w, *refs):
+def own_kernel(block_rows, lengths, n0, n1, f0, f1, w_key, w_value, w, *refs):
     own_sum, own_send, query, key, value, w_near, w_far, cosine, sine, allowed, sems = refs
     piece, depth = n0.shape
-    near_rows = w.at[pl.ds(pl.multiple_of(place[0] * depth, depth), depth)]
-    far_rows = w.at[pl.ds(pl.multiple_of((1 - place[0]) * depth, depth), depth)]
+    ctx = lax.axis_index("ctx")
+    near_rows = w.at[pl.ds(pl.multiple_of(ctx * depth, depth), depth)]
+    far_rows = w.at[pl.ds(pl.multiple_of((1 - ctx) * depth, depth), depth)]
     pairs = ((w_key, key), (w_value, value), (near_rows, w_near), (far_rows, w_far))
     copies = [pltpu.make_async_copy(*pair, sems.at[i]) for i, pair in enumerate(pairs)]
     for copy in copies:
         copy.start()
-    fill_tables(piece, block_rows, place, lengths, cosine, sine, allowed)
+    fill_tables(piece, block_rows, lengths, cosine, sine, allowed)
     near, far = stacked((n0, n1)), stacked((f0, f1))
     wide = key.shape[1]
     for index, weight in enumerate((key, value)):
@@ -265,26 +262,36 @@
             out[:, c] = mixed[g * rows : (g + 1) * rows, :]
 
 
-def out_kernel(first, attended, w, stay, leave):
-    wide = stay.shape[1]
-    rows = stay.shape[0] // 2
+def out_kernel(attended, w, *refs):
+    stays, leaves = refs[::2], refs[1::2]
+    half, wide = stays[0].shape
+    rows = half // 2
     block = 2 * HD
-    for at in range(0, wide, block):
-        part = pl.ds(first + at, block)
-        total = jnp.dot(attended[...], w[:, part], preferred_element_type=jnp.float32)
-        for to, (index, out) in enumerate(((0, stay), (1, leave), (2, stay), (3, leave))):
-            piece = total[index * rows : (index + 1) * rows].astype(out.dtype)
-            out[to // 2 * rows : to // 2 * rows + rows, at : at + block] = piece
-
-
-def project_out(attended, w, first, wide):
+    for chunk, (stay, leave) in enumerate(zip(stays, leaves)):
+        for at in range(0, wide, block):
+            part = pl.ds(chunk * wide + at, block)
+            total = jnp.dot(attended[...], w[:, part], preferred_element_type=jnp.float32)
+            for to, (index, out) in enumerate(((0, stay), (1, leave), (2, stay), (3, leave))):
+                piece = total[index * rows : (index + 1) * rows].astype(out.dtype)
+                out[to // 2 * rows : to // 2 * rows + rows, at : at + block] = piece
+
+
+def project_out(attended, w, chunks):
     rows, depth = attended.shape
-    return call(
-        functools.partial(out_kernel, first),
-        [shape(rows // 2, wide, jnp.float32), shape(rows // 2, wide, jnp.bfloat16)],
-        2 * rows * depth * wide,
-        2 * rows * depth,
-    )(attended, w)
+    wide = w.shape[1] // chunks
+    pair = [shape(rows // 2, wide, jnp.float32), shape(rows // 2, wide, jnp.bfloat16)]
+    outs = call(out_kernel, pair * chunks, 2 * rows * depth * w.shape[1], 2 * rows * depth)(
+        attended, w
+    )
+    return list(zip(outs[::2], outs[1::2]))
+
+
+def mix_kernel(stay, arrived, out):
+    out[...] = (stay[...] + arrived[...].astype(jnp.float32)).astype(out.dtype)
+
+
+def mix(stay, arrived):
+    return call(mix_kernel, shape(*arrived.shape, arrived.dtype), 0, 1 << 20)(stay, arrived)
 
 
 def on_four_by_two(inputs, doc_lengths, w_query, w_key, w_value, w_out):
@@ -293,21 +300,19 @@
     rows = own.shape[0]
     half = w_key.shape[0]
     group = w_query.shape[1] // w_key.shape[1]
-    ctx, tp = lax.axis_index("ctx"), lax.axis_index("tp")
     block_rows = rows * lax.axis_size("tp")
 
     smem, vmem = pl.BlockSpec(memory_space=pltpu.SMEM), pl.BlockSpec(memory_space=pltpu.VMEM)
     anywhere = pl.BlockSpec(memory_space=pl.ANY)
 
-    place = jnp.stack([ctx, tp])
     x_near, x_far = call(
         split_kernel,
         [shape(rows, half, own.dtype)] * 2,
         0,
         1 << 20,
-        in_specs=[smem, anywhere],
+        in_specs=[anywhere],
         scratch_shapes=[pltpu.SemaphoreType.DMA((2,))],
-    )(place, in_hbm(own))
+    )(in_hbm(own))
     far_a = swap(x_far, "ctx", 1)
     near_b = swap(x_near, "tp", 2)
     x_near_s = swap(x_near, "tp", 1)
@@ -329,11 +334,10 @@
         ],
         kv_flops + 8 * rows * half * wide,
         8 * rows * half,
-        in_specs=[smem] * 2 + [vmem] * 4 + [anywhere] * 3,
+        in_specs=[smem] + [vmem] * 4 + [anywhere] * 3,
         scratch_shapes=[pltpu.SemaphoreType.DMA((4,))],
     )(
-        place,
-        doc_lengths,
+        in_hbm(doc_lengths),
         *(x_near, x_near_s, x_far, x_far_s),
         *(in_hbm(w_key), in_hbm(w_value), in_hbm(w_query)),
     )
@@ -395,15 +399,14 @@
     )(q_first, q_last, done, sum_a, sum_b, early_b, more_b, cosine, sine, allowed)
 
     w_out = in_vmem(w_out)
-    wide = w_out.shape[1] // OUT_CHUNKS
-    parts = []
-    for chunk in range(OUT_CHUNKS):
-        stay, leave = project_out(attended, w_out, chunk * wide, wide)
+    out, first = jnp.zeros((rows, w_out.shape[1]), jnp.bfloat16), 0
+    for stay, leave in project_out(attended, w_out, OUT_CHUNKS):
         stay = stay + swap(leave, "tp", 1).astype(jnp.float32)
         arrived = swap(stay[rows:].astype(jnp.bfloat16), "tp", 2)
-        mixed = (stay[:rows] + arrived.astype(jnp.float32)).astype(jnp.bfloat16)
-        parts.append(from_behind(mixed, "pipe", 1))
-    return jnp.concatenate(parts, axis=1)[None]
+        part = from_behind(mix(stay[:rows], arrived), "pipe", 1)
+        out = lax.dynamic_update_slice(out, part, (0, first))
+        first += part.shape[1]
+    return out[None]
 
 
 def doc_index(positions, lengths):

time: 67 us -> 65.6 us (0.979)
  starting transfers between devices: 23.2 us -> 25.9 us
  waiting for transfers between devices: 25.9 us -> 23.3 us
  other arithmetic: 1.3 us -> 0.32 us
  Pallas kernels: 15.4 us -> 14.6 us
    ppermute x24 -> x26, waiting for transfers between devices: 19.5 us -> 17.4 us  [swap(): lax.ppermute(value, axis, [(source, source ^ bit) for source in range(cou...]
    ppermute x4 -> x5, starting transfers between devices: 6.49 us -> 8.15 us  [from_behind(): return lax.ppermute(value, axis, pairs)]
    ppermute x24 -> x26, starting transfers between devices: 16.7 us -> 17.8 us  [swap(): lax.ppermute(value, axis, [(source, source ^ bit) for source in range(cou...]
    broadcast_in_dim x1 -> x0, other arithmetic: 0.88 us -> none  [on_four_by_two(): return jnp.concatenate(parts, axis=1)[None]]
    dynamic_update_slice x0 -> x4, local copies, waits for them, and re-layouts: none -> 0.69 us  [on_four_by_two(): out = lax.dynamic_update_slice(out, part, (0, first))]
    ppermute x4 -> x5, waiting for transfers between devices: 6.48 us -> 5.87 us  [from_behind(): return lax.ppermute(value, axis, pairs)]
    pallas_call x4 -> x6, Pallas kernels: 2.73 us -> 2.33 us  [the longest x1 2.2 us: project_out(): call(out_kernel, pair * chunks, 2 * rows * depth * w.shape[1], 2 * rows *...]
  transfers between devices with their start and end apart: 28 -> 31, of which waited for: 16 -> 18; matrix products, arithmetic and copies ran while one was open for 1% -> 1% of each run, Pallas kernels for 18% -> 15%
where the time goes in v5:
time: 65.6 us; the launch traced here: 65.4 us
  starting transfers between devices  25.9 us (39%)
  waiting for transfers between devices  23.3 us (36%)
  Pallas kernels  14.6 us (22%)
  local copies, waits for them, and re-layouts  0.92 us (1%)
    ppermute x26, starting transfers between devices, swap(): lax.ppermute(value, axis, [(source, source ^ bit) for source in range(cou...  17.8 us
    ppermute x26, waiting for transfers between devices, swap(): lax.ppermute(value, axis, [(source, source ^ bit) for source in range(cou...  17.4 us
    ppermute x5, starting transfers between devices, from_behind(): return lax.ppermute(value, axis, pairs)  8.15 us
    pallas_call x1, Pallas kernels, on_four_by_two(): call(functools.partial(own_kernel, block_rows), [*sums, shape(2 * rows, w...  6.44 us
    ppermute x5, waiting for transfers between devices, from_behind(): return lax.ppermute(value, axis, pairs)  5.87 us
    pallas_call x1, Pallas kernels, project_out(): call(out_kernel, pair * chunks, 2 * rows * depth * w.shape[1], 2 * rows *...  2.2 us
    pallas_call x1, Pallas kernels, on_four_by_two(): call(functools.partial(attend_kernel, group), shape(4 * rows, wide, jnp.b...  1.32 us
  transfers between devices with their start and end apart: 31, of which 18 were waited for; matrix products, arithmetic and copies ran while one was open for 1% of the time, Pallas kernels for 15%

profile of v5, /device:TPU:0, one launch (start us, length us, event | category | flops | bytes accessed | tf_op | source)
XLA Modules:
  0.0 65.4 jit_solution(4690379296183460233)
XLA Ops:
  0.0 1.1 %shard_map.64 = (bf16[64,2560]{1,0:T(8,128)(2,1)S(1)}, bf16[64,2560]{1,0:T(8,128)(2,1)S(1)}) custom-call(bf16[64,5120]{1,0:T(8,128)(2,1)} %bitcast.21), custom_call_target="tpu_custom_call" | custom-call | bytes 1048576 | tf_op jit(solution)/shard_map/pallas_call | solution.py:308
  1.1 0.5 collective-permute-start
  1.6 0.1 collective-permute-start.1
  1.7 2.9 %collective-permute-start.2 = (bf16[64,2560]{1,0:T(8,128)(2,1)S(1)}, bf16[64,2560]{1,0:T(8,128)(2,1)S(1)}, u32[]{:S(2)}, u32[]{:S(2)}) collective-permute-start(bf16[64,2560]{1,0:T(8,128)(2,1)S(1)} %get-tuple-element.40.f0.refs_0_), channel_id=1, source_target_pairs={{0,4},{4,0},{1,5},{5,1},{2,6},{6,2},{3,7},{7,3},{8,12},{12,8},{9,1... | collective-permute-start | bytes 983048 | tf_op jit(solution)/shard_map/ppermute | solution.py:28
  4.6 1.5 %collective-permute-start.3 = (bf16[64,2560]{1,0:T(8,128)(2,1)S(1)}, bf16[64,2560]{1,0:T(8,128)(2,1)S(1)}, u32[]{:S(2)}, u32[]{:S(2)}) collective-permute-start(bf16[64,2560]{1,0:T(8,128)(2,1)S(1)} %get-tuple-element.39.n0), channel_id=1, source_target_pairs={{0,2},{1,3},{2,0},{3,1},{4,6},{5,7},{6,4},{7,5},{8,10},{9,11},{10,... | collective-permute-start | bytes 983048 | tf_op jit(solution)/shard_map/ppermute | solution.py:28
  6.1 6.4 %shard_map.65 = (f32[128,512]{1,0:T(8,128)S(1)}, bf16[128,512]{1,0:T(8,128)(2,1)S(1)}, bf16[128,768]{1,0:T(8,128)(2,1)S(1)}, bf16[2560,256]{1,0:T(8,128)(2,1)S(1...) custom-call(s32[1,8]{1,0:T(1,128)} %lengths.1, ...), custom_call_target="tpu_custom_call" | custom-call | flops 1342177280 | bytes 1310720 | tf_op jit(solution)/shard_map/pallas_call | solution.py:325
  12.6 1.4 %collective-permute-done.3.refs_1_ = bf16[64,2560]{1,0:T(8,128)(2,1)S(1)} collective-permute-done((bf16[64,2560]{1,0:T(8,128)(2,1)S(1)}, bf16[64,2560]{1,0:T(8,128)(2,1)S(1)}, u32[]{:S(2)}, u32[]{:S(2)}) %collective-permute-start.3) | collective-permute-done | bytes 327712 | tf_op jit(solution)/shard_map/ppermute | solution.py:28
  14.1 0.1 collective-permute-start.4
  14.2 0.5 collective-permute-start.7
  14.7 1.5 %collective-permute-start.8 = (bf16[64,2560]{1,0:T(8,128)(2,1)S(1)}, bf16[64,2560]{1,0:T(8,128)(2,1)S(1)}, u32[]{:S(2)}, u32[]{:S(2)}) collective-permute-start(bf16[64,2560]{1,0:T(8,128)(2,1)S(1)} %get-tuple-element.49.f0), channel_id=1, source_target_pairs={{0,2},{1,3},{2,0},{3,1},{4,6},{5,7},{6,4},{7,5},{8,10},{9,11},{10,... | collective-permute-start | bytes 983048 | tf_op jit(solution)/shard_map/ppermute | solution.py:28
  16.2 0.5 collective-permute-start.5
  16.7 0.8 %shard_map.69 = (f32[128,512]{1,0:T(8,128)S(1)}, bf16[192,512]{1,0:T(8,128)(2,1)S(1)}, bf16[64,512]{1,0:T(8,128)(2,1)S(1)}) custom-call(bf16[64,2560]{1,0:T(8,128)(2,1)S(1)} %get-tuple-element.43.n0, bf16[64,2560]{1,0:T(8,128)(2,1)S(1)} %collective-permute-done.4.n1, bf16[64,2560]{1,0:T(8,128)(2,1)S(1)} %get-tuple-element.49.f0, ...), custom_call_target="tpu_custom_call" | custom-call | flops 671088640 | bytes 1310720 | tf_op jit(solution)/shard_map/pallas_call | solution.py:351
  17.6 1.6 %collective-permute-start.9 = (bf16[192,512]{1,0:T(8,128)(2,1)S(1)}, bf16[192,512]{1,0:T(8,128)(2,1)S(1)}, u32[]{:S(2)}, u32[]{:S(2)}) collective-permute-start(bf16[192,512]{1,0:T(8,128)(2,1)S(1)} %get-tuple-element.53.send), channel_id=1, source_target_pairs={{0,4},{4,0},{1,5},{5,1},{2,6},{6,2},{3,7},{7,3},{8,12},{12,8},{9,1... | collective-permute-start | bytes 589832 | tf_op jit(solution)/shard_map/ppermute | solution.py:28
  19.1 3.4 %collective-permute-done.5._.early_a = bf16[128,512]{1,0:T(8,128)(2,1)S(1)} collective-permute-done((bf16[128,512]{1,0:T(8,128)(2,1)S(1)}, bf16[128,512]{1,0:T(8,128)(2,1)S(1)}, u32[]{:S(2)}, u32[]{:S(2)}) %collective-permute-start.5) | collective-permute-done | bytes 131104 | tf_op jit(solution)/shard_map/ppermute | solution.py:28
  22.6 0.7 %shard_map.67.refs_1_.refs_3_.before = f32[128,768]{1,0:T(8,128)S(1)} custom-call(bf16[64,2560]{1,0:T(8,128)(2,1)S(1)} %get-tuple-element.43.n0, bf16[64,2560]{1,0:T(8,128)(2,1)S(1)} %collective-permute-done.4.n1, bf16[128,512]{1,0:T(8,128)(2,1)S(1)} %collective-permute-done.5._.early_a, bf16[2560,768]{1,0:T(8,128)(2,1)S(1)} %get-tuple-element.45.w), custom_call_target="tpu_custom_call" | custom-call | flops 503316480 | bytes 655360 | tf_op jit(solution)/shard_map/pallas_call | solution.py:358
  23.3 0.1 collective-permute-start.6
  23.4 1.6 %collective-permute-done.8.refs_0_.refs_1_.refs_2_ = bf16[64,2560]{1,0:T(8,128)(2,1)S(1)} collective-permute-done((bf16[64,2560]{1,0:T(8,128)(2,1)S(1)}, bf16[64,2560]{1,0:T(8,128)(2,1)S(1)}, u32[]{:S(2)}, u32[]{:S(2)}) %collective-permute-start.8) | collective-permute-done | bytes 327712 | tf_op jit(solution)/shard_map/ppermute | solution.py:28
  25.0 0.6 collective-permute-done.9.refs_4_.early_b.more_a
  25.6 0.1 collective-permute-start.10
  25.7 0.5 collective-permute-start.11
  26.2 0.9 %collective-permute-done.10.refs_0_ = bf16[64,1280]{1,0:T(8,128)(2,1)S(1)} collective-permute-done((bf16[64,1280]{1,0:T(8,128)(2,1)S(1)}, bf16[64,1280]{1,0:T(8,128)(2,1)S(1)}, u32[]{:S(2)}, u32[]{:S(2)}) %collective-permute-start.10) | collective-permute-done | bytes 163872 | tf_op jit(solution)/shard_map/ppermute | solution.py:28
  27.1 0.2 collective-permute-done.11.refs_1_
  27.3 0.5 shard_map.71.refs_3_.far
  27.9 0.6 collective-permute-start.15
  28.5 2.9 %collective-permute-done.6.refs_0_.refs_1_.refs_2_.f0 = bf16[64,2560]{1,0:T(8,128)(2,1)S(1)} collective-permute-done((bf16[64,2560]{1,0:T(8,128)(2,1)S(1)}, bf16[64,2560]{1,0:T(8,128)(2,1)S(1)}, u32[]{:S(2)}, u32[]{:S(2)}) %collective-permute-start.6) | collective-permute-done | bytes 327712 | tf_op jit(solution)/shard_map/ppermute | solution.py:28
  31.4 0.1 collective-permute-start.13
  31.5 0.5 collective-permute-start.14
  32.0 0.1 collective-permute-start.12
  32.1 0.3 shard_map.74.done
  32.4 0.9 %collective-permute-done.12.refs_0_ = bf16[64,768]{1,0:T(8,128)(2,1)S(1)} collective-permute-done((bf16[64,768]{1,0:T(8,128)(2,1)S(1)}, bf16[64,768]{1,0:T(8,128)(2,1)S(1)}, u32[]{:S(2)}, u32[]{:S(2)}) %collective-permute-start.12) | collective-permute-done | bytes 98336 | tf_op jit(solution)/shard_map/ppermute | solution.py:28
  33.3 0.9 %shard_map.73.q_last = bf16[128,768]{1,0:T(8,128)(2,1)S(1)} custom-call(bf16[64,2560]{1,0:T(8,128)(2,1)S(1)} %collective-permute-done.6.refs_0_.refs_1_.refs_2_.f0, bf16[2560,768]{1,0:T(8,128)(2,1)S(1)} %get-tuple-element.46.w, f32[128,768]{1,0:T(8,128)S(1)} %shard_map.67.refs_1_.refs_3_.before, f32[512,128]{1,0:T(8,128)S(1)} %get-tuple-element.47.cosine, ...), custom_call_target="tpu_custom_call" | custom-call | flops 503316480 | bytes 1310720 | tf_op jit(solution)/shard_map/pallas_call | solution.py:382
  34.2 0.8 %collective-permute-done.15.more_b = bf16[192,512]{1,0:T(8,128)(2,1)S(1)} collective-permute-done((bf16[192,512]{1,0:T(8,128)(2,1)S(1)}, bf16[192,512]{1,0:T(8,128)(2,1)S(1)}, u32[]{:S(2)}, u32[]{:S(2)}) %collective-permute-start.15) | collective-permute-done | bytes 196640 | tf_op jit(solution)/shard_map/ppermute | solution.py:28
  35.0 1.3 %shard_map.75.attended = bf16[256,768]{1,0:T(8,128)(2,1)S(1)} custom-call(bf16[128,768]{1,0:T(8,128)(2,1)S(1)} %get-tuple-element.41.q_first, bf16[128,768]{1,0:T(8,128)(2,1)S(1)} %shard_map.73.q_last, bf16[256,512]{1,0:T(8,128)(2,1)S(1)} %shard_map.74.done, f32[128,512]{1,0:T(8,128)S(1)} %get-tuple-element.60.sum_a, ...), custom_call_target="tpu_custom_call" | custom-call | flops 201326592 | bytes 1048576 | tf_op jit(solution)/shard_map/pallas_call | solution.py:393
  36.4 2.2 %shard_map.76 = (f32[128,1024]{1,0:T(8,128)S(1)}, bf16[128,1024]{1,0:T(8,128)(2,1)S(1)}, f32[128,1024]{1,0:T(8,128)S(1)}, bf16[128,1024]{1,0:T(8,128)(2,1)S(1)},...) custom-call(bf16[256,768]{1,0:T(8,128)(2,1)S(1)} %shard_map.75.atten, ...), custom_call_target="tpu_custom_call" | custom-call | flops 2013265920 | bytes 393216 | tf_op jit(solution)/shard_map/pallas_call | solution.py:283
  38.6 0.1 collective-permute-start.16
  38.6 0.5 collective-permute-start.19
  39.1 0.1 collective-permute-start.22
  39.2 0.4 collective-permute-start.25
  39.7 0.1 collective-permute-start.28
  39.7 0.4 collective-permute-done.16
  40.2 0.1 convert_add_fusion.4
  40.2 1.2 %collective-permute-start.17 = (bf16[64,1024]{1,0:T(8,128)(2,1)S(1)}, bf16[64,1024]{1,0:T(8,128)(2,1)S(1)}, u32[]{:S(2)}, u32[]{:S(2)}) collective-permute-start(bf16[64,1024]{1,0:T(8,128)(2,1)S(1)} %slice.64), channel_id=1, source_target_pairs={{0,2},{1,3},{2,0},{3,1},{4,6},{5,7},{6,4},{7,5},{8,10},{9,11},{10,... | collective-permute-start | bytes 393224 | tf_op jit(solution)/shard_map/ppermute | solution.py:28
  41.5 0.1 convert_add_fusion.3
  41.6 0.9 %collective-permute-start.20 = (bf16[64,1024]{1,0:T(8,128)(2,1)S(1)}, bf16[64,1024]{1,0:T(8,128)(2,1)S(1)}, u32[]{:S(2)}, u32[]{:S(2)}) collective-permute-start(bf16[64,1024]{1,0:T(8,128)(2,1)S(1)} %slice.63), channel_id=1, source_target_pairs={{0,2},{1,3},{2,0},{3,1},{4,6},{5,7},{6,4},{7,5},{8,10},{9,11},{10,... | collective-permute-start | bytes 393224 | tf_op jit(solution)/shard_map/ppermute | solution.py:28
  42.5 0.1 convert_add_fusion.2
  42.6 1.2 %collective-permute-start.23 = (bf16[64,1024]{1,0:T(8,128)(2,1)S(1)}, bf16[64,1024]{1,0:T(8,128)(2,1)S(1)}, u32[]{:S(2)}, u32[]{:S(2)}) collective-permute-start(bf16[64,1024]{1,0:T(8,128)(2,1)S(1)} %slice.62), channel_id=1, source_target_pairs={{0,2},{1,3},{2,0},{3,1},{4,6},{5,7},{6,4},{7,5},{8,10},{9,11},{10,... | collective-permute-start | bytes 393224 | tf_op jit(solution)/shard_map/ppermute | solution.py:28
  43.8 0.1 convert_add_fusion.1
  43.9 0.9 %collective-permute-start.26 = (bf16[64,1024]{1,0:T(8,128)(2,1)S(1)}, bf16[64,1024]{1,0:T(8,128)(2,1)S(1)}, u32[]{:S(2)}, u32[]{:S(2)}) collective-permute-start(bf16[64,1024]{1,0:T(8,128)(2,1)S(1)} %slice.61), channel_id=1, source_target_pairs={{0,2},{1,3},{2,0},{3,1},{4,6},{5,7},{6,4},{7,5},{8,10},{9,11},{10,... | collective-permute-start | bytes 393224 | tf_op jit(solution)/shard_map/ppermute | solution.py:28
  44.9 0.1 convert_add_fusion
  45.0 1.2 %collective-permute-start.29 = (bf16[64,1024]{1,0:T(8,128)(2,1)S(1)}, bf16[64,1024]{1,0:T(8,128)(2,1)S(1)}, u32[]{:S(2)}, u32[]{:S(2)}) collective-permute-start(bf16[64,1024]{1,0:T(8,128)(2,1)S(1)} %slice.60), channel_id=1, source_target_pairs={{0,2},{1,3},{2,0},{3,1},{4,6},{5,7},{6,4},{7,5},{8,10},{9,11},{10,... | collective-permute-start | bytes 393224 | tf_op jit(solution)/shard_map/ppermute | solution.py:28
  46.2 0.4 collective-permute-done.17.arrived
  46.7 1.6 %collective-permute-start.18 = (bf16[64,1024]{1,0:T(8,128)(2,1)S(1)}, bf16[64,1024]{1,0:T(8,128)(2,1)S(1)}, u32[]{:S(2)}, u32[]{:S(2)}) collective-permute-start(bf16[64,1024]{1,0:T(8,128)(2,1)S(1)} %shard_map.77), channel_id=1, source_target_pairs={{0,8},{8,16},{16,24},{24,0},{1,9},{9,17},{17,25},{25,1},{2,10},{10... | collective-permute-start | bytes 393224 | tf_op jit(solution)/shard_map/ppermute | solution.py:23
  48.4 1.0 %collective-permute-done.20.arrived = bf16[64,1024]{1,0:T(8,128)(2,1)S(1)} collective-permute-done((bf16[64,1024]{1,0:T(8,128)(2,1)S(1)}, bf16[64,1024]{1,0:T(8,128)(2,1)S(1)}, u32[]{:S(2)}, u32[]{:S(2)}) %collective-permute-start.20) | collective-permute-done | bytes 131104 | tf_op jit(solution)/shard_map/ppermute | solution.py:28
  49.5 1.6 %collective-permute-start.21 = (bf16[64,1024]{1,0:T(8,128)(2,1)S(1)}, bf16[64,1024]{1,0:T(8,128)(2,1)S(1)}, u32[]{:S(2)}, u32[]{:S(2)}) collective-permute-start(bf16[64,1024]{1,0:T(8,128)(2,1)S(1)} %shard_map.78), channel_id=1, source_target_pairs={{0,8},{8,16},{16,24},{24,0},{1,9},{9,17},{17,25},{25,1},{2,10},{10... | collective-permute-start | bytes 393224 | tf_op jit(solution)/shard_map/ppermute | solution.py:23
  51.1 1.1 %collective-permute-done.23.arrived = bf16[64,1024]{1,0:T(8,128)(2,1)S(1)} collective-permute-done((bf16[64,1024]{1,0:T(8,128)(2,1)S(1)}, bf16[64,1024]{1,0:T(8,128)(2,1)S(1)}, u32[]{:S(2)}, u32[]{:S(2)}) %collective-permute-start.23) | collective-permute-done | bytes 131104 | tf_op jit(solution)/shard_map/ppermute | solution.py:28
  52.3 1.6 %collective-permute-start.24 = (bf16[64,1024]{1,0:T(8,128)(2,1)S(1)}, bf16[64,1024]{1,0:T(8,128)(2,1)S(1)}, u32[]{:S(2)}, u32[]{:S(2)}) collective-permute-start(bf16[64,1024]{1,0:T(8,128)(2,1)S(1)} %shard_map.79), channel_id=1, source_target_pairs={{0,8},{8,16},{16,24},{24,0},{1,9},{9,17},{17,25},{25,1},{2,10},{10... | collective-permute-start | bytes 393224 | tf_op jit(solution)/shard_map/ppermute | solution.py:23
  53.9 1.1 %collective-permute-done.26.arrived = bf16[64,1024]{1,0:T(8,128)(2,1)S(1)} collective-permute-done((bf16[64,1024]{1,0:T(8,128)(2,1)S(1)}, bf16[64,1024]{1,0:T(8,128)(2,1)S(1)}, u32[]{:S(2)}, u32[]{:S(2)}) %collective-permute-start.26) | collective-permute-done | bytes 131104 | tf_op jit(solution)/shard_map/ppermute | solution.py:28
  55.1 1.6 %collective-permute-start.27 = (bf16[64,1024]{1,0:T(8,128)(2,1)S(1)}, bf16[64,1024]{1,0:T(8,128)(2,1)S(1)}, u32[]{:S(2)}, u32[]{:S(2)}) collective-permute-start(bf16[64,1024]{1,0:T(8,128)(2,1)S(1)} %shard_map.80), channel_id=1, source_target_pairs={{0,8},{8,16},{16,24},{24,0},{1,9},{9,17},{17,25},{25,1},{2,10},{10... | collective-permute-start | bytes 393224 | tf_op jit(solution)/shard_map/ppermute | solution.py:23
  56.7 0.3 collective-permute-done.29.arrived
  57.1 1.6 %collective-permute-start.30 = (bf16[64,1024]{1,0:T(8,128)(2,1)S(1)}, bf16[64,1024]{1,0:T(8,128)(2,1)S(1)}, u32[]{:S(2)}, u32[]{:S(2)}) collective-permute-start(bf16[64,1024]{1,0:T(8,128)(2,1)S(1)} %shard_map.81), channel_id=1, source_target_pairs={{0,8},{8,16},{16,24},{24,0},{1,9},{9,17},{17,25},{25,1},{2,10},{10... | collective-permute-start | bytes 393224 | tf_op jit(solution)/shard_map/ppermute | solution.py:23
  58.8 1.4 %collective-permute-done.24 = bf16[64,1024]{1,0:T(8,128)(2,1)S(1)} collective-permute-done((bf16[64,1024]{1,0:T(8,128)(2,1)S(1)}, bf16[64,1024]{1,0:T(8,128)(2,1)S(1)}, u32[]{:S(2)}, u32[]{:S(2)}) %collective-permute-start.24) | collective-permute-done | bytes 131104 | tf_op jit(solution)/shard_map/ppermute | solution.py:23
  60.2 2.8 %collective-permute-done.27 = bf16[64,1024]{1,0:T(8,128)(2,1)S(1)} collective-permute-done((bf16[64,1024]{1,0:T(8,128)(2,1)S(1)}, bf16[64,1024]{1,0:T(8,128)(2,1)S(1)}, u32[]{:S(2)}, u32[]{:S(2)}) %collective-permute-start.27) | collective-permute-done | bytes 131104 | tf_op jit(solution)/shard_map/ppermute | solution.py:23
  63.0 1.7 %collective-permute-done.30 = bf16[64,1024]{1,0:T(8,128)(2,1)S(1)} collective-permute-done((bf16[64,1024]{1,0:T(8,128)(2,1)S(1)}, bf16[64,1024]{1,0:T(8,128)(2,1)S(1)}, u32[]{:S(2)}, u32[]{:S(2)}) %collective-permute-start.30) | collective-permute-done | bytes 131104 | tf_op jit(solution)/shard_map/ppermute | solution.py:23
  64.7 0.7 %bitcast_dynamic-update-slice_fusion = bf16[1,64,5120]{2,1,0:T(8,128)(2,1)} fusion(bf16[1,64,5120]{2,1,0:T(8,128)(2,1)} %copy-done, bf16[64,1024]{1,0:T(8,128)(2,1)S(1)} %collective-permute-done.30), kind=kLoop, calls=%fused_computation.11 | loop fusion | bytes 262144 | tf_op jit(solution)/shard_map/dynamic_update_slice | solution.py:407
  (43 shorter events, 0.6 us)
Async XLA Ops:
  1.1 5.0 %collective-permute-start = (bf16[64,2560]{1,0:T(8,128)(2,1)S(1)}, bf16[64,2560]{1,0:T(8,128)(2,1)S(1)}, u32[]{:S(2)}, u32[]{:S(2)}) collective-permute-start(bf16[64,2560]{1,0:T(8,128)(2,1)S(1)} %get-tuple-element.39.n0), channel_id=1, source_target_pairs={{0,1},{1,0},{2,3},{3,2},{4,5},{5,4},{6,7},{7,6},{8,9},{9,8},{10,11... | collective-permute-start | bytes 983048 | tf_op jit(solution)/shard_map/ppermute | solution.py:28
  1.6 4.5 %collective-permute-start.1 = (bf16[64,2560]{1,0:T(8,128)(2,1)S(1)}, bf16[64,2560]{1,0:T(8,128)(2,1)S(1)}, u32[]{:S(2)}, u32[]{:S(2)}) collective-permute-start(bf16[64,2560]{1,0:T(8,128)(2,1)S(1)} %get-tuple-element.40.f0.refs_0_), channel_id=1, source_target_pairs={{0,1},{1,0},{2,3},{3,2},{4,5},{5,4},{6,7},{7,6},{8,9},{9,8},{10,11... | collective-permute-start | bytes 983048 | tf_op jit(solution)/shard_map/ppermute | solution.py:28
  1.7 10.9 %collective-permute-start.2 = (bf16[64,2560]{1,0:T(8,128)(2,1)S(1)}, bf16[64,2560]{1,0:T(8,128)(2,1)S(1)}, u32[]{:S(2)}, u32[]{:S(2)}) collective-permute-start(bf16[64,2560]{1,0:T(8,128)(2,1)S(1)} %get-tuple-element.40.f0.refs_0_), channel_id=1, source_target_pairs={{0,4},{4,0},{1,5},{5,1},{2,6},{6,2},{3,7},{7,3},{8,12},{12,8},{9,1... | collective-permute-start | bytes 983048 | tf_op jit(solution)/shard_map/ppermute | solution.py:28
  4.6 9.4 %collective-permute-start.3 = (bf16[64,2560]{1,0:T(8,128)(2,1)S(1)}, bf16[64,2560]{1,0:T(8,128)(2,1)S(1)}, u32[]{:S(2)}, u32[]{:S(2)}) collective-permute-start(bf16[64,2560]{1,0:T(8,128)(2,1)S(1)} %get-tuple-element.39.n0), channel_id=1, source_target_pairs={{0,2},{1,3},{2,0},{3,1},{4,6},{5,7},{6,4},{7,5},{8,10},{9,11},{10,... | collective-permute-start | bytes 983048 | tf_op jit(solution)/shard_map/ppermute | solution.py:28
  14.1 2.6 %collective-permute-start.4 = (bf16[64,2560]{1,0:T(8,128)(2,1)S(1)}, bf16[64,2560]{1,0:T(8,128)(2,1)S(1)}, u32[]{:S(2)}, u32[]{:S(2)}) collective-permute-start(bf16[64,2560]{1,0:T(8,128)(2,1)S(1)} %get-tuple-element.43.n0), channel_id=1, source_target_pairs={{0,1},{1,0},{2,3},{3,2},{4,5},{5,4},{6,7},{7,6},{8,9},{9,8},{10,11... | collective-permute-start | bytes 983048 | tf_op jit(solution)/shard_map/ppermute | solution.py:28
  14.2 2.6 %collective-permute-start.7 = (bf16[64,2560]{1,0:T(8,128)(2,1)S(1)}, bf16[64,2560]{1,0:T(8,128)(2,1)S(1)}, u32[]{:S(2)}, u32[]{:S(2)}) collective-permute-start(bf16[64,2560]{1,0:T(8,128)(2,1)S(1)} %get-tuple-element.49.f0), channel_id=1, source_target_pairs={{0,1},{1,0},{2,3},{3,2},{4,5},{5,4},{6,7},{7,6},{8,9},{9,8},{10,11... | collective-permute-start | bytes 983048 | tf_op jit(solution)/shard_map/ppermute | solution.py:28
  14.7 10.3 %collective-permute-start.8 = (bf16[64,2560]{1,0:T(8,128)(2,1)S(1)}, bf16[64,2560]{1,0:T(8,128)(2,1)S(1)}, u32[]{:S(2)}, u32[]{:S(2)}) collective-permute-start(bf16[64,2560]{1,0:T(8,128)(2,1)S(1)} %get-tuple-element.49.f0), channel_id=1, source_target_pairs={{0,2},{1,3},{2,0},{3,1},{4,6},{5,7},{6,4},{7,5},{8,10},{9,11},{10,... | collective-permute-start | bytes 983048 | tf_op jit(solution)/shard_map/ppermute | solution.py:28
  16.2 6.4 %collective-permute-start.5 = (bf16[128,512]{1,0:T(8,128)(2,1)S(1)}, bf16[128,512]{1,0:T(8,128)(2,1)S(1)}, u32[]{:S(2)}, u32[]{:S(2)}) collective-permute-start(bf16[128,512]{1,0:T(8,128)(2,1)S(1)} %get-tuple-element.44), channel_id=1, source_target_pairs={{0,4},{4,0},{1,5},{5,1},{2,6},{6,2},{3,7},{7,3},{8,12},{12,8},{9,1... | collective-permute-start | bytes 393224 | tf_op jit(solution)/shard_map/ppermute | solution.py:28
  17.6 8.0 %collective-permute-start.9 = (bf16[192,512]{1,0:T(8,128)(2,1)S(1)}, bf16[192,512]{1,0:T(8,128)(2,1)S(1)}, u32[]{:S(2)}, u32[]{:S(2)}) collective-permute-start(bf16[192,512]{1,0:T(8,128)(2,1)S(1)} %get-tuple-element.53.send), channel_id=1, source_target_pairs={{0,4},{4,0},{1,5},{5,1},{2,6},{6,2},{3,7},{7,3},{8,12},{12,8},{9,1... | collective-permute-start | bytes 589832 | tf_op jit(solution)/shard_map/ppermute | solution.py:28
  23.3 8.1 %collective-permute-start.6 = (bf16[64,2560]{1,0:T(8,128)(2,1)S(1)}, bf16[64,2560]{1,0:T(8,128)(2,1)S(1)}, u32[]{:S(2)}, u32[]{:S(2)}) collective-permute-start(bf16[64,2560]{1,0:T(8,128)(2,1)S(1)} %shard_map.68), channel_id=1, source_target_pairs={{0,2},{1,3},{2,0},{3,1},{4,6},{5,7},{6,4},{7,5},{8,10},{9,11},{10,... | collective-permute-start | bytes 983048 | tf_op jit(solution)/shard_map/ppermute | solution.py:28
  25.6 1.5 %collective-permute-start.10 = (bf16[64,1280]{1,0:T(8,128)(2,1)S(1)}, bf16[64,1280]{1,0:T(8,128)(2,1)S(1)}, u32[]{:S(2)}, u32[]{:S(2)}) collective-permute-start(bf16[64,1280]{1,0:T(8,128)(2,1)S(1)} %get-tuple-element.55), channel_id=1, source_target_pairs={{0,1},{1,0},{2,3},{3,2},{4,5},{5,4},{6,7},{7,6},{8,9},{9,8},{10,11... | collective-permute-start | bytes 491528 | tf_op jit(solution)/shard_map/ppermute | solution.py:28
  25.7 1.6 %collective-permute-start.11 = (bf16[64,1280]{1,0:T(8,128)(2,1)S(1)}, bf16[64,1280]{1,0:T(8,128)(2,1)S(1)}, u32[]{:S(2)}, u32[]{:S(2)}) collective-permute-start(bf16[64,1280]{1,0:T(8,128)(2,1)S(1)} %get-tuple-element.56), channel_id=1, source_target_pairs={{0,1},{1,0},{2,3},{3,2},{4,5},{5,4},{6,7},{7,6},{8,9},{9,8},{10,11... | collective-permute-start | bytes 491528 | tf_op jit(solution)/shard_map/ppermute | solution.py:28
  27.3 9.0 %slice-start = ((s8[7864320]{0:T(1024)(128)(4,1)}), s8[4194304]{0:T(1024)(128)(4,1)S(1)}, s32[]{:S(2)}) async-start(s8[7864320]{0:T(1024)(128)(4,1)} %bitcast.15), calls=%async_computation | async-start | bytes 8388608
  27.9 7.1 %collective-permute-start.15 = (bf16[192,512]{1,0:T(8,128)(2,1)S(1)}, bf16[192,512]{1,0:T(8,128)(2,1)S(1)}, u32[]{:S(2)}, u32[]{:S(2)}) collective-permute-start(bf16[192,512]{1,0:T(8,128)(2,1)S(1)} %shard_map.71.refs_3_.far), channel_id=1, source_target_pairs={{0,4},{4,0},{1,5},{5,1},{2,6},{6,2},{3,7},{7,3},{8,12},{12,8},{9,1... | collective-permute-start | bytes 589832 | tf_op jit(solution)/shard_map/ppermute | solution.py:28
  31.4 1.9 %collective-permute-start.13 = (bf16[64,896]{1,0:T(8,128)(2,1)S(1)}, bf16[64,896]{1,0:T(8,128)(2,1)S(1)}, u32[]{:S(2)}, u32[]{:S(2)}) collective-permute-start(bf16[64,896]{1,0:T(8,128)(2,1)S(1)} %get-tuple-element.58), channel_id=1, source_target_pairs={{0,1},{1,0},{2,3},{3,2},{4,5},{5,4},{6,7},{7,6},{8,9},{9,8},{10,11... | collective-permute-start | bytes 344072 | tf_op jit(solution)/shard_map/ppermute | solution.py:28
  31.5 1.8 %collective-permute-start.14 = (bf16[64,896]{1,0:T(8,128)(2,1)S(1)}, bf16[64,896]{1,0:T(8,128)(2,1)S(1)}, u32[]{:S(2)}, u32[]{:S(2)}) collective-permute-start(bf16[64,896]{1,0:T(8,128)(2,1)S(1)} %get-tuple-element.59), channel_id=1, source_target_pairs={{0,1},{1,0},{2,3},{3,2},{4,5},{5,4},{6,7},{7,6},{8,9},{9,8},{10,11... | collective-permute-start | bytes 344072 | tf_op jit(solution)/shard_map/ppermute | solution.py:28
  32.0 1.3 %collective-permute-start.12 = (bf16[64,768]{1,0:T(8,128)(2,1)S(1)}, bf16[64,768]{1,0:T(8,128)(2,1)S(1)}, u32[]{:S(2)}, u32[]{:S(2)}) collective-permute-start(bf16[64,768]{1,0:T(8,128)(2,1)S(1)} %get-tuple-element.57), channel_id=1, source_target_pairs={{0,1},{1,0},{2,3},{3,2},{4,5},{5,4},{6,7},{7,6},{8,9},{9,8},{10,11... | collective-permute-start | bytes 294920 | tf_op jit(solution)/shard_map/ppermute | solution.py:28
  33.3 3.1 %slice-start.1 = ((s8[7864320]{0:T(1024)(128)(4,1)}), s8[3670016]{0:T(1024)(128)(4,1)S(1)}, s32[]{:S(2)}) async-start(s8[7864320]{0:T(1024)(128)(4,1)} %bitcast.15), calls=%async_computation.1 | async-start | bytes 7340032
  38.6 1.6 %collective-permute-start.16 = (bf16[128,1024]{1,0:T(8,128)(2,1)S(1)}, bf16[128,1024]{1,0:T(8,128)(2,1)S(1)}, u32[]{:S(2)}, u32[]{:S(2)}) collective-permute-start(bf16[128,1024]{1,0:T(8,128)(2,1)S(1)} %get-tuple-element.64), channel_id=1, source_target_pairs={{0,1},{1,0},{2,3},{3,2},{4,5},{5,4},{6,7},{7,6},{8,9},{9,8},{10,11... | collective-permute-start | bytes 786440 | tf_op jit(solution)/shard_map/ppermute | solution.py:28
  38.6 2.8 %collective-permute-start.19 = (bf16[128,1024]{1,0:T(8,128)(2,1)S(1)}, bf16[128,1024]{1,0:T(8,128)(2,1)S(1)}, u32[]{:S(2)}, u32[]{:S(2)}) collective-permute-start(bf16[128,1024]{1,0:T(8,128)(2,1)S(1)} %get-tuple-element.66), channel_id=1, source_target_pairs={{0,1},{1,0},{2,3},{3,2},{4,5},{5,4},{6,7},{7,6},{8,9},{9,8},{10,11... | collective-permute-start | bytes 786440 | tf_op jit(solution)/shard_map/ppermute | solution.py:28
  39.1 3.4 %collective-permute-start.22 = (bf16[128,1024]{1,0:T(8,128)(2,1)S(1)}, bf16[128,1024]{1,0:T(8,128)(2,1)S(1)}, u32[]{:S(2)}, u32[]{:S(2)}) collective-permute-start(bf16[128,1024]{1,0:T(8,128)(2,1)S(1)} %get-tuple-element.68), channel_id=1, source_target_pairs={{0,1},{1,0},{2,3},{3,2},{4,5},{5,4},{6,7},{7,6},{8,9},{9,8},{10,11... | collective-permute-start | bytes 786440 | tf_op jit(solution)/shard_map/ppermute | solution.py:28
  39.2 4.6 %collective-permute-start.25 = (bf16[128,1024]{1,0:T(8,128)(2,1)S(1)}, bf16[128,1024]{1,0:T(8,128)(2,1)S(1)}, u32[]{:S(2)}, u32[]{:S(2)}) collective-permute-start(bf16[128,1024]{1,0:T(8,128)(2,1)S(1)} %get-tuple-element.70), channel_id=1, source_target_pairs={{0,1},{1,0},{2,3},{3,2},{4,5},{5,4},{6,7},{7,6},{8,9},{9,8},{10,11... | collective-permute-start | bytes 786440 | tf_op jit(solution)/shard_map/ppermute | solution.py:28
  39.7 5.2 %collective-permute-start.28 = (bf16[128,1024]{1,0:T(8,128)(2,1)S(1)}, bf16[128,1024]{1,0:T(8,128)(2,1)S(1)}, u32[]{:S(2)}, u32[]{:S(2)}) collective-permute-start(bf16[128,1024]{1,0:T(8,128)(2,1)S(1)} %get-tuple-element.72), channel_id=1, source_target_pairs={{0,1},{1,0},{2,3},{3,2},{4,5},{5,4},{6,7},{7,6},{8,9},{9,8},{10,11... | collective-permute-start | bytes 786440 | tf_op jit(solution)/shard_map/ppermute | solution.py:28
  40.2 6.4 %collective-permute-start.17 = (bf16[64,1024]{1,0:T(8,128)(2,1)S(1)}, bf16[64,1024]{1,0:T(8,128)(2,1)S(1)}, u32[]{:S(2)}, u32[]{:S(2)}) collective-permute-start(bf16[64,1024]{1,0:T(8,128)(2,1)S(1)} %slice.64), channel_id=1, source_target_pairs={{0,2},{1,3},{2,0},{3,1},{4,6},{5,7},{6,4},{7,5},{8,10},{9,11},{10,... | collective-permute-start | bytes 393224 | tf_op jit(solution)/shard_map/ppermute | solution.py:28
  41.6 7.9 %collective-permute-start.20 = (bf16[64,1024]{1,0:T(8,128)(2,1)S(1)}, bf16[64,1024]{1,0:T(8,128)(2,1)S(1)}, u32[]{:S(2)}, u32[]{:S(2)}) collective-permute-start(bf16[64,1024]{1,0:T(8,128)(2,1)S(1)} %slice.63), channel_id=1, source_target_pairs={{0,2},{1,3},{2,0},{3,1},{4,6},{5,7},{6,4},{7,5},{8,10},{9,11},{10,... | collective-permute-start | bytes 393224 | tf_op jit(solution)/shard_map/ppermute | solution.py:28
  42.6 9.7 %collective-permute-start.23 = (bf16[64,1024]{1,0:T(8,128)(2,1)S(1)}, bf16[64,1024]{1,0:T(8,128)(2,1)S(1)}, u32[]{:S(2)}, u32[]{:S(2)}) collective-permute-start(bf16[64,1024]{1,0:T(8,128)(2,1)S(1)} %slice.62), channel_id=1, source_target_pairs={{0,2},{1,3},{2,0},{3,1},{4,6},{5,7},{6,4},{7,5},{8,10},{9,11},{10,... | collective-permute-start | bytes 393224 | tf_op jit(solution)/shard_map/ppermute | solution.py:28
  43.9 11.1 %collective-permute-start.26 = (bf16[64,1024]{1,0:T(8,128)(2,1)S(1)}, bf16[64,1024]{1,0:T(8,128)(2,1)S(1)}, u32[]{:S(2)}, u32[]{:S(2)}) collective-permute-start(bf16[64,1024]{1,0:T(8,128)(2,1)S(1)} %slice.61), channel_id=1, source_target_pairs={{0,2},{1,3},{2,0},{3,1},{4,6},{5,7},{6,4},{7,5},{8,10},{9,11},{10,... | collective-permute-start | bytes 393224 | tf_op jit(solution)/shard_map/ppermute | solution.py:28
  45.0 12.1 %collective-permute-start.29 = (bf16[64,1024]{1,0:T(8,128)(2,1)S(1)}, bf16[64,1024]{1,0:T(8,128)(2,1)S(1)}, u32[]{:S(2)}, u32[]{:S(2)}) collective-permute-start(bf16[64,1024]{1,0:T(8,128)(2,1)S(1)} %slice.60), channel_id=1, source_target_pairs={{0,2},{1,3},{2,0},{3,1},{4,6},{5,7},{6,4},{7,5},{8,10},{9,11},{10,... | collective-permute-start | bytes 393224 | tf_op jit(solution)/shard_map/ppermute | solution.py:28
  46.7 12.1 %collective-permute-start.18 = (bf16[64,1024]{1,0:T(8,128)(2,1)S(1)}, bf16[64,1024]{1,0:T(8,128)(2,1)S(1)}, u32[]{:S(2)}, u32[]{:S(2)}) collective-permute-start(bf16[64,1024]{1,0:T(8,128)(2,1)S(1)} %shard_map.77), channel_id=1, source_target_pairs={{0,8},{8,16},{16,24},{24,0},{1,9},{9,17},{17,25},{25,1},{2,10},{10... | collective-permute-start | bytes 393224 | tf_op jit(solution)/shard_map/ppermute | solution.py:23
  49.5 9.3 %collective-permute-start.21 = (bf16[64,1024]{1,0:T(8,128)(2,1)S(1)}, bf16[64,1024]{1,0:T(8,128)(2,1)S(1)}, u32[]{:S(2)}, u32[]{:S(2)}) collective-permute-start(bf16[64,1024]{1,0:T(8,128)(2,1)S(1)} %shard_map.78), channel_id=1, source_target_pairs={{0,8},{8,16},{16,24},{24,0},{1,9},{9,17},{17,25},{25,1},{2,10},{10... | collective-permute-start | bytes 393224 | tf_op jit(solution)/shard_map/ppermute | solution.py:23
  52.3 7.9 %collective-permute-start.24 = (bf16[64,1024]{1,0:T(8,128)(2,1)S(1)}, bf16[64,1024]{1,0:T(8,128)(2,1)S(1)}, u32[]{:S(2)}, u32[]{:S(2)}) collective-permute-start(bf16[64,1024]{1,0:T(8,128)(2,1)S(1)} %shard_map.79), channel_id=1, source_target_pairs={{0,8},{8,16},{16,24},{24,0},{1,9},{9,17},{17,25},{25,1},{2,10},{10... | collective-permute-start | bytes 393224 | tf_op jit(solution)/shard_map/ppermute | solution.py:23
  55.1 7.9 %collective-permute-start.27 = (bf16[64,1024]{1,0:T(8,128)(2,1)S(1)}, bf16[64,1024]{1,0:T(8,128)(2,1)S(1)}, u32[]{:S(2)}, u32[]{:S(2)}) collective-permute-start(bf16[64,1024]{1,0:T(8,128)(2,1)S(1)} %shard_map.80), channel_id=1, source_target_pairs={{0,8},{8,16},{16,24},{24,0},{1,9},{9,17},{17,25},{25,1},{2,10},{10... | collective-permute-start | bytes 393224 | tf_op jit(solution)/shard_map/ppermute | solution.py:23
  57.1 7.6 %collective-permute-start.30 = (bf16[64,1024]{1,0:T(8,128)(2,1)S(1)}, bf16[64,1024]{1,0:T(8,128)(2,1)S(1)}, u32[]{:S(2)}, u32[]{:S(2)}) collective-permute-start(bf16[64,1024]{1,0:T(8,128)(2,1)S(1)} %shard_map.81), channel_id=1, source_target_pairs={{0,8},{8,16},{16,24},{24,0},{1,9},{9,17},{17,25},{25,1},{2,10},{10... | collective-permute-start | bytes 393224 | tf_op jit(solution)/shard_map/ppermute | solution.py:23
  63.0 1.7 %copy-start = (bf16[1,64,5120]{2,1,0:T(8,128)(2,1)}, bf16[1,64,5120]{2,1,0:T(8,128)(2,1)S(1)}, u32[]{:S(2)}) copy-start(bf16[1,64,5120]{2,1,0:T(8,128)(2,1)S(1)} %bitcast_dynamic-update-slice_fusion.1) | copy-start | bytes 1966084

commit v6 on v5

--- a/solution.py
+++ b/solution.py
@@ -12,6 +12,7 @@
 SPAN = 1024
 ROPE_BASE = 500000.0
 NORM_EPS = 1e-06
+MASKED = -1e30
 OUT_CHUNKS = 5
 MIB = 1 << 20
 VMEM_MIB = 16
@@ -131,7 +132,7 @@
                 other = column + (offsets[to // rows + half] - half * rows)
                 k_pos = jnp.where(column >= half * rows, other, k_pos)
             inside = (k_pos >= first) & (k_pos <= q_pos)
-            allowed[at * rows : (at + 1) * rows, to : to + HD] = jnp.where(inside, 1.0, 0.0)
+            allowed[at * rows : (at + 1) * rows, to : to + HD] = jnp.where(inside, 0.0, MASKED)
 
 
 def stacked(pieces):
@@ -243,7 +244,8 @@
     more = jnp.concatenate([more_a[half:, :], more_b[...]], axis=0)
     finish(total + more.astype(jnp.float32), cosine, sine, kv, ready)
     keys = kv.shape[1] // 2
-    allow = jnp.concatenate([allowed[...]] * group, axis=0) > 0.5
+    bias = jnp.concatenate([allowed[...]] * group, axis=0)
+    ones = jnp.ones((kv.shape[0], HD), kv.dtype)
     for head in range(0, keys, HD):
         key = kv[:, head : head + HD]
         value = kv[:, keys + head : keys + head + HD]
@@ -253,36 +255,38 @@
         scores = lax.dot_general(
             query, key, (((1,), (1,)), ((), ())), preferred_element_type=jnp.float32
         )
-        weights = jnp.where(allow, jnp.exp(scores * (1.0 / HD**0.5)), 0.0)
-        weights = weights.astype(jnp.bfloat16)
-        total = jnp.sum(weights.astype(jnp.float32), axis=-1, keepdims=True)
-        mixed = jnp.dot(weights, value, preferred_element_type=jnp.float32) / total
-        mixed = mixed.astype(out.dtype)
+        weights = jnp.exp(scores * (1.0 / HD**0.5) + bias).astype(jnp.bfloat16)
+        value = jnp.concatenate([value, ones], axis=1)
+        mixed = jnp.dot(weights, value, preferred_element_type=jnp.float32)
+        mixed = (mixed[:, :HD] / mixed[:, HD:]).astype(out.dtype)
         for g, c in enumerate(columns):
             out[:, c] = mixed[g * rows : (g + 1) * rows, :]
 
 
-def out_kernel(attended, w, *refs):
+def out_kernel(first, attended, w, *refs):
     stays, leaves = refs[::2], refs[1::2]
     half, wide = stays[0].shape
     rows = half // 2
     block = 2 * HD
     for chunk, (stay, leave) in enumerate(zip(stays, leaves)):
         for at in range(0, wide, block):
-            part = pl.ds(chunk * wide + at, block)
+            part = pl.ds((first + chunk) * wide + at, block)
             total = jnp.dot(attended[...], w[:, part], preferred_element_type=jnp.float32)
             for to, (index, out) in enumerate(((0, stay), (1, leave), (2, stay), (3, leave))):
                 piece = total[index * rows : (index + 1) * rows].astype(out.dtype)
                 out[to // 2 * rows : to // 2 * rows + rows, at : at + block] = piece
 
 
-def project_out(attended, w, chunks):
+def project_out(attended, w, first, chunks):
     rows, depth = attended.shape
-    wide = w.shape[1] // chunks
+    wide = w.shape[1] // OUT_CHUNKS
     pair = [shape(rows // 2, wide, jnp.float32), shape(rows // 2, wide, jnp.bfloat16)]
-    outs = call(out_kernel, pair * chunks, 2 * rows * depth * w.shape[1], 2 * rows * depth)(
-        attended, w
-    )
+    outs = call(
+        functools.partial(out_kernel, first),
+        pair * chunks,
+        2 * rows * depth * wide * chunks,
+        2 * rows * depth,
+    )(attended, w)
     return list(zip(outs[::2], outs[1::2]))
 
 
@@ -400,7 +404,8 @@
 
     w_out = in_vmem(w_out)
     out, first = jnp.zeros((rows, w_out.shape[1]), jnp.bfloat16), 0
-    for stay, leave in project_out(attended, w_out, OUT_CHUNKS):
+    sums = project_out(attended, w_out, 0, 1) + project_out(attended, w_out, 1, OUT_CHUNKS - 1)
+    for stay, leave in sums:
         stay = stay + swap(leave, "tp", 1).astype(jnp.float32)
         arrived = swap(stay[rows:].astype(jnp.bfloat16), "tp", 2)
         part = from_behind(mix(stay[:rows], arrived), "pipe", 1)

time: 65.6 us -> 65.2 us (level)
    pallas_call x1 -> x2, Pallas kernels: 2.2 us -> 2.36 us  [project_out(): call(functools.partial(out_kernel, first), pair * chunks, 2 * rows * dept...]
  transfers between devices with their start and end apart: 31 -> 31, of which waited for: 18 -> 17; matrix products, arithmetic and copies ran while one was open for 1% -> 1% of each run, Pallas kernels for 15% -> 18%
where the time goes in v6:
time: 65.2 us; the launch traced here: 65 us
  starting transfers between devices  26 us (40%)
  waiting for transfers between devices  22.8 us (35%)
  Pallas kernels  14.6 us (22%)
  local copies, waits for them, and re-layouts  0.92 us (1%)
    ppermute x26, starting transfers between devices, swap(): lax.ppermute(value, axis, [(source, source ^ bit) for source in range(cou...  17.9 us
    ppermute x26, waiting for transfers between devices, swap(): lax.ppermute(value, axis, [(source, source ^ bit) for source in range(cou...  17.3 us
    ppermute x5, starting transfers between devices, from_behind(): return lax.ppermute(value, axis, pairs)  8.15 us
    pallas_call x1, Pallas kernels, on_four_by_two(): call(functools.partial(own_kernel, block_rows), [*sums, shape(2 * rows, w...  6.44 us
    ppermute x5, waiting for transfers between devices, from_behind(): return lax.ppermute(value, axis, pairs)  5.52 us
    pallas_call x2, Pallas kernels, project_out(): call(functools.partial(out_kernel, first), pair * chunks, 2 * rows * dept...  2.36 us
  transfers between devices with their start and end apart: 31, of which 17 were waited for; matrix products, arithmetic and copies ran while one was open for 1% of the time, Pallas kernels for 18%

profile of v6, /device:TPU:0, one launch (start us, length us, event | category | flops | bytes accessed | tf_op | source)
XLA Modules:
  0.0 65.0 jit_solution(4449201092911655836)
XLA Ops:
  0.0 1.1 %shard_map.64 = (bf16[64,2560]{1,0:T(8,128)(2,1)S(1)}, bf16[64,2560]{1,0:T(8,128)(2,1)S(1)}) custom-call(bf16[64,5120]{1,0:T(8,128)(2,1)} %bitcast.22), custom_call_target="tpu_custom_call" | custom-call | bytes 1048576 | tf_op jit(solution)/shard_map/pallas_call | solution.py:312
  1.1 0.5 collective-permute-start
  1.6 0.1 collective-permute-start.1
  1.7 2.9 %collective-permute-start.2 = (bf16[64,2560]{1,0:T(8,128)(2,1)S(1)}, bf16[64,2560]{1,0:T(8,128)(2,1)S(1)}, u32[]{:S(2)}, u32[]{:S(2)}) collective-permute-start(bf16[64,2560]{1,0:T(8,128)(2,1)S(1)} %get-tuple-element.40.f0.refs_0_), channel_id=1, source_target_pairs={{0,4},{4,0},{1,5},{5,1},{2,6},{6,2},{3,7},{7,3},{8,12},{12,8},{9,1... | collective-permute-start | bytes 983048 | tf_op jit(solution)/shard_map/ppermute | solution.py:29
  4.6 1.5 %collective-permute-start.3 = (bf16[64,2560]{1,0:T(8,128)(2,1)S(1)}, bf16[64,2560]{1,0:T(8,128)(2,1)S(1)}, u32[]{:S(2)}, u32[]{:S(2)}) collective-permute-start(bf16[64,2560]{1,0:T(8,128)(2,1)S(1)} %get-tuple-element.39.n0), channel_id=1, source_target_pairs={{0,2},{1,3},{2,0},{3,1},{4,6},{5,7},{6,4},{7,5},{8,10},{9,11},{10,... | collective-permute-start | bytes 983048 | tf_op jit(solution)/shard_map/ppermute | solution.py:29
  6.1 6.4 %shard_map.65 = (f32[128,512]{1,0:T(8,128)S(1)}, bf16[128,512]{1,0:T(8,128)(2,1)S(1)}, bf16[128,768]{1,0:T(8,128)(2,1)S(1)}, bf16[2560,256]{1,0:T(8,128)(2,1)S(1...) custom-call(s32[1,8]{1,0:T(1,128)} %lengths.1, ...), custom_call_target="tpu_custom_call" | custom-call | flops 1342177280 | bytes 1310720 | tf_op jit(solution)/shard_map/pallas_call | solution.py:329
  12.6 1.4 %collective-permute-done.3.refs_1_ = bf16[64,2560]{1,0:T(8,128)(2,1)S(1)} collective-permute-done((bf16[64,2560]{1,0:T(8,128)(2,1)S(1)}, bf16[64,2560]{1,0:T(8,128)(2,1)S(1)}, u32[]{:S(2)}, u32[]{:S(2)}) %collective-permute-start.3) | collective-permute-done | bytes 327712 | tf_op jit(solution)/shard_map/ppermute | solution.py:29
  14.1 0.1 collective-permute-start.4
  14.2 0.5 collective-permute-start.7
  14.7 1.5 %collective-permute-start.8 = (bf16[64,2560]{1,0:T(8,128)(2,1)S(1)}, bf16[64,2560]{1,0:T(8,128)(2,1)S(1)}, u32[]{:S(2)}, u32[]{:S(2)}) collective-permute-start(bf16[64,2560]{1,0:T(8,128)(2,1)S(1)} %get-tuple-element.49.f0), channel_id=1, source_target_pairs={{0,2},{1,3},{2,0},{3,1},{4,6},{5,7},{6,4},{7,5},{8,10},{9,11},{10,... | collective-permute-start | bytes 983048 | tf_op jit(solution)/shard_map/ppermute | solution.py:29
  16.2 0.5 collective-permute-start.5
  16.7 0.8 %shard_map.69 = (f32[128,512]{1,0:T(8,128)S(1)}, bf16[192,512]{1,0:T(8,128)(2,1)S(1)}, bf16[64,512]{1,0:T(8,128)(2,1)S(1)}) custom-call(bf16[64,2560]{1,0:T(8,128)(2,1)S(1)} %get-tuple-element.43.n0, bf16[64,2560]{1,0:T(8,128)(2,1)S(1)} %collective-permute-done.4.n1, bf16[64,2560]{1,0:T(8,128)(2,1)S(1)} %get-tuple-element.49.f0, ...), custom_call_target="tpu_custom_call" | custom-call | flops 671088640 | bytes 1310720 | tf_op jit(solution)/shard_map/pallas_call | solution.py:355
  17.6 1.6 %collective-permute-start.9 = (bf16[192,512]{1,0:T(8,128)(2,1)S(1)}, bf16[192,512]{1,0:T(8,128)(2,1)S(1)}, u32[]{:S(2)}, u32[]{:S(2)}) collective-permute-start(bf16[192,512]{1,0:T(8,128)(2,1)S(1)} %get-tuple-element.53.send), channel_id=1, source_target_pairs={{0,4},{4,0},{1,5},{5,1},{2,6},{6,2},{3,7},{7,3},{8,12},{12,8},{9,1... | collective-permute-start | bytes 589832 | tf_op jit(solution)/shard_map/ppermute | solution.py:29
  19.1 3.4 %collective-permute-done.5._.early_a = bf16[128,512]{1,0:T(8,128)(2,1)S(1)} collective-permute-done((bf16[128,512]{1,0:T(8,128)(2,1)S(1)}, bf16[128,512]{1,0:T(8,128)(2,1)S(1)}, u32[]{:S(2)}, u32[]{:S(2)}) %collective-permute-start.5) | collective-permute-done | bytes 131104 | tf_op jit(solution)/shard_map/ppermute | solution.py:29
  22.6 0.7 %shard_map.67.refs_1_.refs_3_.before = f32[128,768]{1,0:T(8,128)S(1)} custom-call(bf16[64,2560]{1,0:T(8,128)(2,1)S(1)} %get-tuple-element.43.n0, bf16[64,2560]{1,0:T(8,128)(2,1)S(1)} %collective-permute-done.4.n1, bf16[128,512]{1,0:T(8,128)(2,1)S(1)} %collective-permute-done.5._.early_a, bf16[2560,768]{1,0:T(8,128)(2,1)S(1)} %get-tuple-element.45.w), custom_call_target="tpu_custom_call" | custom-call | flops 503316480 | bytes 655360 | tf_op jit(solution)/shard_map/pallas_call | solution.py:362
  23.3 0.1 collective-permute-start.6
  23.4 1.6 %collective-permute-done.8.refs_0_.refs_1_.refs_2_ = bf16[64,2560]{1,0:T(8,128)(2,1)S(1)} collective-permute-done((bf16[64,2560]{1,0:T(8,128)(2,1)S(1)}, bf16[64,2560]{1,0:T(8,128)(2,1)S(1)}, u32[]{:S(2)}, u32[]{:S(2)}) %collective-permute-start.8) | collective-permute-done | bytes 327712 | tf_op jit(solution)/shard_map/ppermute | solution.py:29
  25.0 0.6 collective-permute-done.9.refs_4_.early_b.more_a
  25.6 0.1 collective-permute-start.10
  25.7 0.5 collective-permute-start.11
  26.2 0.9 %collective-permute-done.10.refs_0_ = bf16[64,1280]{1,0:T(8,128)(2,1)S(1)} collective-permute-done((bf16[64,1280]{1,0:T(8,128)(2,1)S(1)}, bf16[64,1280]{1,0:T(8,128)(2,1)S(1)}, u32[]{:S(2)}, u32[]{:S(2)}) %collective-permute-start.10) | collective-permute-done | bytes 163872 | tf_op jit(solution)/shard_map/ppermute | solution.py:29
  27.1 0.2 collective-permute-done.11.refs_1_
  27.3 0.5 shard_map.71.refs_3_.far
  27.9 0.6 collective-permute-start.15
  28.5 2.9 %collective-permute-done.6.refs_0_.refs_1_.refs_2_.f0 = bf16[64,2560]{1,0:T(8,128)(2,1)S(1)} collective-permute-done((bf16[64,2560]{1,0:T(8,128)(2,1)S(1)}, bf16[64,2560]{1,0:T(8,128)(2,1)S(1)}, u32[]{:S(2)}, u32[]{:S(2)}) %collective-permute-start.6) | collective-permute-done | bytes 327712 | tf_op jit(solution)/shard_map/ppermute | solution.py:29
  31.4 0.1 collective-permute-start.13
  31.5 0.5 collective-permute-start.14
  32.0 0.1 collective-permute-start.12
  32.1 0.3 shard_map.74.done
  32.4 0.9 %collective-permute-done.12.refs_0_ = bf16[64,768]{1,0:T(8,128)(2,1)S(1)} collective-permute-done((bf16[64,768]{1,0:T(8,128)(2,1)S(1)}, bf16[64,768]{1,0:T(8,128)(2,1)S(1)}, u32[]{:S(2)}, u32[]{:S(2)}) %collective-permute-start.12) | collective-permute-done | bytes 98336 | tf_op jit(solution)/shard_map/ppermute | solution.py:29
  33.3 0.9 %shard_map.73.q_last = bf16[128,768]{1,0:T(8,128)(2,1)S(1)} custom-call(bf16[64,2560]{1,0:T(8,128)(2,1)S(1)} %collective-permute-done.6.refs_0_.refs_1_.refs_2_.f0, bf16[2560,768]{1,0:T(8,128)(2,1)S(1)} %get-tuple-element.46.w, f32[128,768]{1,0:T(8,128)S(1)} %shard_map.67.refs_1_.refs_3_.before, f32[512,128]{1,0:T(8,128)S(1)} %get-tuple-element.47.cosine, ...), custom_call_target="tpu_custom_call" | custom-call | flops 503316480 | bytes 1310720 | tf_op jit(solution)/shard_map/pallas_call | solution.py:386
  34.2 0.8 %collective-permute-done.15.more_b = bf16[192,512]{1,0:T(8,128)(2,1)S(1)} collective-permute-done((bf16[192,512]{1,0:T(8,128)(2,1)S(1)}, bf16[192,512]{1,0:T(8,128)(2,1)S(1)}, u32[]{:S(2)}, u32[]{:S(2)}) %collective-permute-start.15) | collective-permute-done | bytes 196640 | tf_op jit(solution)/shard_map/ppermute | solution.py:29
  35.0 1.2 %shard_map.75.attended = bf16[256,768]{1,0:T(8,128)(2,1)S(1)} custom-call(bf16[128,768]{1,0:T(8,128)(2,1)S(1)} %get-tuple-element.41.q_first, bf16[128,768]{1,0:T(8,128)(2,1)S(1)} %shard_map.73.q_last, bf16[256,512]{1,0:T(8,128)(2,1)S(1)} %shard_map.74.done, f32[128,512]{1,0:T(8,128)S(1)} %get-tuple-element.60.sum_a, ...), custom_call_target="tpu_custom_call" | custom-call | flops 201326592 | bytes 1048576 | tf_op jit(solution)/shard_map/pallas_call | solution.py:397
  36.2 0.6 shard_map.76
  36.8 0.1 collective-permute-start.16
  36.9 1.8 %shard_map.78 = (f32[128,1024]{1,0:T(8,128)S(1)}, bf16[128,1024]{1,0:T(8,128)(2,1)S(1)}, f32[128,1024]{1,0:T(8,128)S(1)}, bf16[128,1024]{1,0:T(8,128)(2,1)S(1)},...) custom-call(bf16[256,768]{1,0:T(8,128)(2,1)S(1)} %shard_map.75.atten, ...), custom_call_target="tpu_custom_call" | custom-call | flops 1610612736 | bytes 393216 | tf_op jit(solution)/shard_map/pallas_call | solution.py:284
  38.7 0.6 collective-permute-start.19
  39.2 0.1 collective-permute-start.22
  39.3 0.4 collective-permute-start.25
  39.7 0.1 collective-permute-start.28
  39.8 0.1 convert_add_fusion.4
  39.9 1.2 %collective-permute-start.17 = (bf16[64,1024]{1,0:T(8,128)(2,1)S(1)}, bf16[64,1024]{1,0:T(8,128)(2,1)S(1)}, u32[]{:S(2)}, u32[]{:S(2)}) collective-permute-start(bf16[64,1024]{1,0:T(8,128)(2,1)S(1)} %slice.64), channel_id=1, source_target_pairs={{0,2},{1,3},{2,0},{3,1},{4,6},{5,7},{6,4},{7,5},{8,10},{9,11},{10,... | collective-permute-start | bytes 393224 | tf_op jit(solution)/shard_map/ppermute | solution.py:29
  41.1 0.1 convert_add_fusion.3
  41.2 0.9 %collective-permute-start.20 = (bf16[64,1024]{1,0:T(8,128)(2,1)S(1)}, bf16[64,1024]{1,0:T(8,128)(2,1)S(1)}, u32[]{:S(2)}, u32[]{:S(2)}) collective-permute-start(bf16[64,1024]{1,0:T(8,128)(2,1)S(1)} %slice.63), channel_id=1, source_target_pairs={{0,2},{1,3},{2,0},{3,1},{4,6},{5,7},{6,4},{7,5},{8,10},{9,11},{10,... | collective-permute-start | bytes 393224 | tf_op jit(solution)/shard_map/ppermute | solution.py:29
  42.2 0.1 convert_add_fusion.2
  42.3 1.2 %collective-permute-start.23 = (bf16[64,1024]{1,0:T(8,128)(2,1)S(1)}, bf16[64,1024]{1,0:T(8,128)(2,1)S(1)}, u32[]{:S(2)}, u32[]{:S(2)}) collective-permute-start(bf16[64,1024]{1,0:T(8,128)(2,1)S(1)} %slice.62), channel_id=1, source_target_pairs={{0,2},{1,3},{2,0},{3,1},{4,6},{5,7},{6,4},{7,5},{8,10},{9,11},{10,... | collective-permute-start | bytes 393224 | tf_op jit(solution)/shard_map/ppermute | solution.py:29
  43.5 0.1 convert_add_fusion.1
  43.6 0.9 %collective-permute-start.26 = (bf16[64,1024]{1,0:T(8,128)(2,1)S(1)}, bf16[64,1024]{1,0:T(8,128)(2,1)S(1)}, u32[]{:S(2)}, u32[]{:S(2)}) collective-permute-start(bf16[64,1024]{1,0:T(8,128)(2,1)S(1)} %slice.61), channel_id=1, source_target_pairs={{0,2},{1,3},{2,0},{3,1},{4,6},{5,7},{6,4},{7,5},{8,10},{9,11},{10,... | collective-permute-start | bytes 393224 | tf_op jit(solution)/shard_map/ppermute | solution.py:29
  44.5 0.1 convert_add_fusion
  44.6 1.2 %collective-permute-start.29 = (bf16[64,1024]{1,0:T(8,128)(2,1)S(1)}, bf16[64,1024]{1,0:T(8,128)(2,1)S(1)}, u32[]{:S(2)}, u32[]{:S(2)}) collective-permute-start(bf16[64,1024]{1,0:T(8,128)(2,1)S(1)} %slice.60), channel_id=1, source_target_pairs={{0,2},{1,3},{2,0},{3,1},{4,6},{5,7},{6,4},{7,5},{8,10},{9,11},{10,... | collective-permute-start | bytes 393224 | tf_op jit(solution)/shard_map/ppermute | solution.py:29
  45.9 0.4 collective-permute-done.17.arrived
  46.3 1.6 %collective-permute-start.18 = (bf16[64,1024]{1,0:T(8,128)(2,1)S(1)}, bf16[64,1024]{1,0:T(8,128)(2,1)S(1)}, u32[]{:S(2)}, u32[]{:S(2)}) collective-permute-start(bf16[64,1024]{1,0:T(8,128)(2,1)S(1)} %shard_map.77), channel_id=1, source_target_pairs={{0,8},{8,16},{16,24},{24,0},{1,9},{9,17},{17,25},{25,1},{2,10},{10... | collective-permute-start | bytes 393224 | tf_op jit(solution)/shard_map/ppermute | solution.py:24
  48.0 1.0 %collective-permute-done.20.arrived = bf16[64,1024]{1,0:T(8,128)(2,1)S(1)} collective-permute-done((bf16[64,1024]{1,0:T(8,128)(2,1)S(1)}, bf16[64,1024]{1,0:T(8,128)(2,1)S(1)}, u32[]{:S(2)}, u32[]{:S(2)}) %collective-permute-start.20) | collective-permute-done | bytes 131104 | tf_op jit(solution)/shard_map/ppermute | solution.py:29
  49.1 1.6 %collective-permute-start.21 = (bf16[64,1024]{1,0:T(8,128)(2,1)S(1)}, bf16[64,1024]{1,0:T(8,128)(2,1)S(1)}, u32[]{:S(2)}, u32[]{:S(2)}) collective-permute-start(bf16[64,1024]{1,0:T(8,128)(2,1)S(1)} %shard_map.79), channel_id=1, source_target_pairs={{0,8},{8,16},{16,24},{24,0},{1,9},{9,17},{17,25},{25,1},{2,10},{10... | collective-permute-start | bytes 393224 | tf_op jit(solution)/shard_map/ppermute | solution.py:24
  50.7 1.1 %collective-permute-done.23.arrived = bf16[64,1024]{1,0:T(8,128)(2,1)S(1)} collective-permute-done((bf16[64,1024]{1,0:T(8,128)(2,1)S(1)}, bf16[64,1024]{1,0:T(8,128)(2,1)S(1)}, u32[]{:S(2)}, u32[]{:S(2)}) %collective-permute-start.23) | collective-permute-done | bytes 131104 | tf_op jit(solution)/shard_map/ppermute | solution.py:29
  51.9 1.6 %collective-permute-start.24 = (bf16[64,1024]{1,0:T(8,128)(2,1)S(1)}, bf16[64,1024]{1,0:T(8,128)(2,1)S(1)}, u32[]{:S(2)}, u32[]{:S(2)}) collective-permute-start(bf16[64,1024]{1,0:T(8,128)(2,1)S(1)} %shard_map.80), channel_id=1, source_target_pairs={{0,8},{8,16},{16,24},{24,0},{1,9},{9,17},{17,25},{25,1},{2,10},{10... | collective-permute-start | bytes 393224 | tf_op jit(solution)/shard_map/ppermute | solution.py:24
  53.5 1.1 %collective-permute-done.26.arrived = bf16[64,1024]{1,0:T(8,128)(2,1)S(1)} collective-permute-done((bf16[64,1024]{1,0:T(8,128)(2,1)S(1)}, bf16[64,1024]{1,0:T(8,128)(2,1)S(1)}, u32[]{:S(2)}, u32[]{:S(2)}) %collective-permute-start.26) | collective-permute-done | bytes 131104 | tf_op jit(solution)/shard_map/ppermute | solution.py:29
  54.7 1.6 %collective-permute-start.27 = (bf16[64,1024]{1,0:T(8,128)(2,1)S(1)}, bf16[64,1024]{1,0:T(8,128)(2,1)S(1)}, u32[]{:S(2)}, u32[]{:S(2)}) collective-permute-start(bf16[64,1024]{1,0:T(8,128)(2,1)S(1)} %shard_map.81), channel_id=1, source_target_pairs={{0,8},{8,16},{16,24},{24,0},{1,9},{9,17},{17,25},{25,1},{2,10},{10... | collective-permute-start | bytes 393224 | tf_op jit(solution)/shard_map/ppermute | solution.py:24
  56.3 0.7 %collective-permute-done.29.arrived = bf16[64,1024]{1,0:T(8,128)(2,1)S(1)} collective-permute-done((bf16[64,1024]{1,0:T(8,128)(2,1)S(1)}, bf16[64,1024]{1,0:T(8,128)(2,1)S(1)}, u32[]{:S(2)}, u32[]{:S(2)}) %collective-permute-start.29) | collective-permute-done | bytes 131104 | tf_op jit(solution)/shard_map/ppermute | solution.py:29
  57.1 1.6 %collective-permute-start.30 = (bf16[64,1024]{1,0:T(8,128)(2,1)S(1)}, bf16[64,1024]{1,0:T(8,128)(2,1)S(1)}, u32[]{:S(2)}, u32[]{:S(2)}) collective-permute-start(bf16[64,1024]{1,0:T(8,128)(2,1)S(1)} %shard_map.82), channel_id=1, source_target_pairs={{0,8},{8,16},{16,24},{24,0},{1,9},{9,17},{17,25},{25,1},{2,10},{10... | collective-permute-start | bytes 393224 | tf_op jit(solution)/shard_map/ppermute | solution.py:24
  58.8 0.2 collective-permute-done.24
  59.0 2.8 %collective-permute-done.27 = bf16[64,1024]{1,0:T(8,128)(2,1)S(1)} collective-permute-done((bf16[64,1024]{1,0:T(8,128)(2,1)S(1)}, bf16[64,1024]{1,0:T(8,128)(2,1)S(1)}, u32[]{:S(2)}, u32[]{:S(2)}) %collective-permute-start.27) | collective-permute-done | bytes 131104 | tf_op jit(solution)/shard_map/ppermute | solution.py:24
  61.8 2.5 %collective-permute-done.30 = bf16[64,1024]{1,0:T(8,128)(2,1)S(1)} collective-permute-done((bf16[64,1024]{1,0:T(8,128)(2,1)S(1)}, bf16[64,1024]{1,0:T(8,128)(2,1)S(1)}, u32[]{:S(2)}, u32[]{:S(2)}) %collective-permute-start.30) | collective-permute-done | bytes 131104 | tf_op jit(solution)/shard_map/ppermute | solution.py:24
  64.3 0.7 %bitcast_dynamic-update-slice_fusion = bf16[1,64,5120]{2,1,0:T(8,128)(2,1)} fusion(bf16[1,64,5120]{2,1,0:T(8,128)(2,1)} %copy-done, bf16[64,1024]{1,0:T(8,128)(2,1)S(1)} %collective-permute-done.30), kind=kLoop, calls=%fused_computation.11 | loop fusion | bytes 262144 | tf_op jit(solution)/shard_map/dynamic_update_slice | solution.py:412
  (44 shorter events, 0.6 us)
Async XLA Ops:
  1.1 5.0 %collective-permute-start = (bf16[64,2560]{1,0:T(8,128)(2,1)S(1)}, bf16[64,2560]{1,0:T(8,128)(2,1)S(1)}, u32[]{:S(2)}, u32[]{:S(2)}) collective-permute-start(bf16[64,2560]{1,0:T(8,128)(2,1)S(1)} %get-tuple-element.39.n0), channel_id=1, source_target_pairs={{0,1},{1,0},{2,3},{3,2},{4,5},{5,4},{6,7},{7,6},{8,9},{9,8},{10,11... | collective-permute-start | bytes 983048 | tf_op jit(solution)/shard_map/ppermute | solution.py:29
  1.6 4.5 %collective-permute-start.1 = (bf16[64,2560]{1,0:T(8,128)(2,1)S(1)}, bf16[64,2560]{1,0:T(8,128)(2,1)S(1)}, u32[]{:S(2)}, u32[]{:S(2)}) collective-permute-start(bf16[64,2560]{1,0:T(8,128)(2,1)S(1)} %get-tuple-element.40.f0.refs_0_), channel_id=1, source_target_pairs={{0,1},{1,0},{2,3},{3,2},{4,5},{5,4},{6,7},{7,6},{8,9},{9,8},{10,11... | collective-permute-start | bytes 983048 | tf_op jit(solution)/shard_map/ppermute | solution.py:29
  1.7 10.9 %collective-permute-start.2 = (bf16[64,2560]{1,0:T(8,128)(2,1)S(1)}, bf16[64,2560]{1,0:T(8,128)(2,1)S(1)}, u32[]{:S(2)}, u32[]{:S(2)}) collective-permute-start(bf16[64,2560]{1,0:T(8,128)(2,1)S(1)} %get-tuple-element.40.f0.refs_0_), channel_id=1, source_target_pairs={{0,4},{4,0},{1,5},{5,1},{2,6},{6,2},{3,7},{7,3},{8,12},{12,8},{9,1... | collective-permute-start | bytes 983048 | tf_op jit(solution)/shard_map/ppermute | solution.py:29
  4.6 9.4 %collective-permute-start.3 = (bf16[64,2560]{1,0:T(8,128)(2,1)S(1)}, bf16[64,2560]{1,0:T(8,128)(2,1)S(1)}, u32[]{:S(2)}, u32[]{:S(2)}) collective-permute-start(bf16[64,2560]{1,0:T(8,128)(2,1)S(1)} %get-tuple-element.39.n0), channel_id=1, source_target_pairs={{0,2},{1,3},{2,0},{3,1},{4,6},{5,7},{6,4},{7,5},{8,10},{9,11},{10,... | collective-permute-start | bytes 983048 | tf_op jit(solution)/shard_map/ppermute | solution.py:29
  14.1 2.6 %collective-permute-start.4 = (bf16[64,2560]{1,0:T(8,128)(2,1)S(1)}, bf16[64,2560]{1,0:T(8,128)(2,1)S(1)}, u32[]{:S(2)}, u32[]{:S(2)}) collective-permute-start(bf16[64,2560]{1,0:T(8,128)(2,1)S(1)} %get-tuple-element.43.n0), channel_id=1, source_target_pairs={{0,1},{1,0},{2,3},{3,2},{4,5},{5,4},{6,7},{7,6},{8,9},{9,8},{10,11... | collective-permute-start | bytes 983048 | tf_op jit(solution)/shard_map/ppermute | solution.py:29
  14.2 2.6 %collective-permute-start.7 = (bf16[64,2560]{1,0:T(8,128)(2,1)S(1)}, bf16[64,2560]{1,0:T(8,128)(2,1)S(1)}, u32[]{:S(2)}, u32[]{:S(2)}) collective-permute-start(bf16[64,2560]{1,0:T(8,128)(2,1)S(1)} %get-tuple-element.49.f0), channel_id=1, source_target_pairs={{0,1},{1,0},{2,3},{3,2},{4,5},{5,4},{6,7},{7,6},{8,9},{9,8},{10,11... | collective-permute-start | bytes 983048 | tf_op jit(solution)/shard_map/ppermute | solution.py:29
  14.7 10.3 %collective-permute-start.8 = (bf16[64,2560]{1,0:T(8,128)(2,1)S(1)}, bf16[64,2560]{1,0:T(8,128)(2,1)S(1)}, u32[]{:S(2)}, u32[]{:S(2)}) collective-permute-start(bf16[64,2560]{1,0:T(8,128)(2,1)S(1)} %get-tuple-element.49.f0), channel_id=1, source_target_pairs={{0,2},{1,3},{2,0},{3,1},{4,6},{5,7},{6,4},{7,5},{8,10},{9,11},{10,... | collective-permute-start | bytes 983048 | tf_op jit(solution)/shard_map/ppermute | solution.py:29
  16.2 6.4 %collective-permute-start.5 = (bf16[128,512]{1,0:T(8,128)(2,1)S(1)}, bf16[128,512]{1,0:T(8,128)(2,1)S(1)}, u32[]{:S(2)}, u32[]{:S(2)}) collective-permute-start(bf16[128,512]{1,0:T(8,128)(2,1)S(1)} %get-tuple-element.44), channel_id=1, source_target_pairs={{0,4},{4,0},{1,5},{5,1},{2,6},{6,2},{3,7},{7,3},{8,12},{12,8},{9,1... | collective-permute-start | bytes 393224 | tf_op jit(solution)/shard_map/ppermute | solution.py:29
  17.6 8.0 %collective-permute-start.9 = (bf16[192,512]{1,0:T(8,128)(2,1)S(1)}, bf16[192,512]{1,0:T(8,128)(2,1)S(1)}, u32[]{:S(2)}, u32[]{:S(2)}) collective-permute-start(bf16[192,512]{1,0:T(8,128)(2,1)S(1)} %get-tuple-element.53.send), channel_id=1, source_target_pairs={{0,4},{4,0},{1,5},{5,1},{2,6},{6,2},{3,7},{7,3},{8,12},{12,8},{9,1... | collective-permute-start | bytes 589832 | tf_op jit(solution)/shard_map/ppermute | solution.py:29
  23.3 8.1 %collective-permute-start.6 = (bf16[64,2560]{1,0:T(8,128)(2,1)S(1)}, bf16[64,2560]{1,0:T(8,128)(2,1)S(1)}, u32[]{:S(2)}, u32[]{:S(2)}) collective-permute-start(bf16[64,2560]{1,0:T(8,128)(2,1)S(1)} %shard_map.68), channel_id=1, source_target_pairs={{0,2},{1,3},{2,0},{3,1},{4,6},{5,7},{6,4},{7,5},{8,10},{9,11},{10,... | collective-permute-start | bytes 983048 | tf_op jit(solution)/shard_map/ppermute | solution.py:29
  25.6 1.5 %collective-permute-start.10 = (bf16[64,1280]{1,0:T(8,128)(2,1)S(1)}, bf16[64,1280]{1,0:T(8,128)(2,1)S(1)}, u32[]{:S(2)}, u32[]{:S(2)}) collective-permute-start(bf16[64,1280]{1,0:T(8,128)(2,1)S(1)} %get-tuple-element.55), channel_id=1, source_target_pairs={{0,1},{1,0},{2,3},{3,2},{4,5},{5,4},{6,7},{7,6},{8,9},{9,8},{10,11... | collective-permute-start | bytes 491528 | tf_op jit(solution)/shard_map/ppermute | solution.py:29
  25.7 1.6 %collective-permute-start.11 = (bf16[64,1280]{1,0:T(8,128)(2,1)S(1)}, bf16[64,1280]{1,0:T(8,128)(2,1)S(1)}, u32[]{:S(2)}, u32[]{:S(2)}) collective-permute-start(bf16[64,1280]{1,0:T(8,128)(2,1)S(1)} %get-tuple-element.56), channel_id=1, source_target_pairs={{0,1},{1,0},{2,3},{3,2},{4,5},{5,4},{6,7},{7,6},{8,9},{9,8},{10,11... | collective-permute-start | bytes 491528 | tf_op jit(solution)/shard_map/ppermute | solution.py:29
  27.3 8.8 %slice-start = ((s8[7864320]{0:T(1024)(128)(4,1)}), s8[4194304]{0:T(1024)(128)(4,1)S(1)}, s32[]{:S(2)}) async-start(s8[7864320]{0:T(1024)(128)(4,1)} %bitcast.15), calls=%async_computation | async-start | bytes 8388608
  27.9 7.1 %collective-permute-start.15 = (bf16[192,512]{1,0:T(8,128)(2,1)S(1)}, bf16[192,512]{1,0:T(8,128)(2,1)S(1)}, u32[]{:S(2)}, u32[]{:S(2)}) collective-permute-start(bf16[192,512]{1,0:T(8,128)(2,1)S(1)} %shard_map.71.refs_3_.far), channel_id=1, source_target_pairs={{0,4},{4,0},{1,5},{5,1},{2,6},{6,2},{3,7},{7,3},{8,12},{12,8},{9,1... | collective-permute-start | bytes 589832 | tf_op jit(solution)/shard_map/ppermute | solution.py:29
  31.4 1.9 %collective-permute-start.13 = (bf16[64,896]{1,0:T(8,128)(2,1)S(1)}, bf16[64,896]{1,0:T(8,128)(2,1)S(1)}, u32[]{:S(2)}, u32[]{:S(2)}) collective-permute-start(bf16[64,896]{1,0:T(8,128)(2,1)S(1)} %get-tuple-element.58), channel_id=1, source_target_pairs={{0,1},{1,0},{2,3},{3,2},{4,5},{5,4},{6,7},{7,6},{8,9},{9,8},{10,11... | collective-permute-start | bytes 344072 | tf_op jit(solution)/shard_map/ppermute | solution.py:29
  31.5 1.8 %collective-permute-start.14 = (bf16[64,896]{1,0:T(8,128)(2,1)S(1)}, bf16[64,896]{1,0:T(8,128)(2,1)S(1)}, u32[]{:S(2)}, u32[]{:S(2)}) collective-permute-start(bf16[64,896]{1,0:T(8,128)(2,1)S(1)} %get-tuple-element.59), channel_id=1, source_target_pairs={{0,1},{1,0},{2,3},{3,2},{4,5},{5,4},{6,7},{7,6},{8,9},{9,8},{10,11... | collective-permute-start | bytes 344072 | tf_op jit(solution)/shard_map/ppermute | solution.py:29
  32.0 1.3 %collective-permute-start.12 = (bf16[64,768]{1,0:T(8,128)(2,1)S(1)}, bf16[64,768]{1,0:T(8,128)(2,1)S(1)}, u32[]{:S(2)}, u32[]{:S(2)}) collective-permute-start(bf16[64,768]{1,0:T(8,128)(2,1)S(1)} %get-tuple-element.57), channel_id=1, source_target_pairs={{0,1},{1,0},{2,3},{3,2},{4,5},{5,4},{6,7},{7,6},{8,9},{9,8},{10,11... | collective-permute-start | bytes 294920 | tf_op jit(solution)/shard_map/ppermute | solution.py:29
  33.3 2.9 %slice-start.1 = ((s8[7864320]{0:T(1024)(128)(4,1)}), s8[3670016]{0:T(1024)(128)(4,1)S(1)}, s32[]{:S(2)}) async-start(s8[7864320]{0:T(1024)(128)(4,1)} %bitcast.15), calls=%async_computation.1 | async-start | bytes 7340032
  36.8 3.0 %collective-permute-start.16 = (bf16[128,1024]{1,0:T(8,128)(2,1)S(1)}, bf16[128,1024]{1,0:T(8,128)(2,1)S(1)}, u32[]{:S(2)}, u32[]{:S(2)}) collective-permute-start(bf16[128,1024]{1,0:T(8,128)(2,1)S(1)} %get-tuple-element.64), channel_id=1, source_target_pairs={{0,1},{1,0},{2,3},{3,2},{4,5},{5,4},{6,7},{7,6},{8,9},{9,8},{10,11... | collective-permute-start | bytes 786440 | tf_op jit(solution)/shard_map/ppermute | solution.py:29
  38.7 2.5 %collective-permute-start.19 = (bf16[128,1024]{1,0:T(8,128)(2,1)S(1)}, bf16[128,1024]{1,0:T(8,128)(2,1)S(1)}, u32[]{:S(2)}, u32[]{:S(2)}) collective-permute-start(bf16[128,1024]{1,0:T(8,128)(2,1)S(1)} %get-tuple-element.66), channel_id=1, source_target_pairs={{0,1},{1,0},{2,3},{3,2},{4,5},{5,4},{6,7},{7,6},{8,9},{9,8},{10,11... | collective-permute-start | bytes 786440 | tf_op jit(solution)/shard_map/ppermute | solution.py:29
  39.2 2.9 %collective-permute-start.22 = (bf16[128,1024]{1,0:T(8,128)(2,1)S(1)}, bf16[128,1024]{1,0:T(8,128)(2,1)S(1)}, u32[]{:S(2)}, u32[]{:S(2)}) collective-permute-start(bf16[128,1024]{1,0:T(8,128)(2,1)S(1)} %get-tuple-element.68), channel_id=1, source_target_pairs={{0,1},{1,0},{2,3},{3,2},{4,5},{5,4},{6,7},{7,6},{8,9},{9,8},{10,11... | collective-permute-start | bytes 786440 | tf_op jit(solution)/shard_map/ppermute | solution.py:29
  39.3 4.2 %collective-permute-start.25 = (bf16[128,1024]{1,0:T(8,128)(2,1)S(1)}, bf16[128,1024]{1,0:T(8,128)(2,1)S(1)}, u32[]{:S(2)}, u32[]{:S(2)}) collective-permute-start(bf16[128,1024]{1,0:T(8,128)(2,1)S(1)} %get-tuple-element.70), channel_id=1, source_target_pairs={{0,1},{1,0},{2,3},{3,2},{4,5},{5,4},{6,7},{7,6},{8,9},{9,8},{10,11... | collective-permute-start | bytes 786440 | tf_op jit(solution)/shard_map/ppermute | solution.py:29
  39.7 4.8 %collective-permute-start.28 = (bf16[128,1024]{1,0:T(8,128)(2,1)S(1)}, bf16[128,1024]{1,0:T(8,128)(2,1)S(1)}, u32[]{:S(2)}, u32[]{:S(2)}) collective-permute-start(bf16[128,1024]{1,0:T(8,128)(2,1)S(1)} %get-tuple-element.72), channel_id=1, source_target_pairs={{0,1},{1,0},{2,3},{3,2},{4,5},{5,4},{6,7},{7,6},{8,9},{9,8},{10,11... | collective-permute-start | bytes 786440 | tf_op jit(solution)/shard_map/ppermute | solution.py:29
  39.9 6.4 %collective-permute-start.17 = (bf16[64,1024]{1,0:T(8,128)(2,1)S(1)}, bf16[64,1024]{1,0:T(8,128)(2,1)S(1)}, u32[]{:S(2)}, u32[]{:S(2)}) collective-permute-start(bf16[64,1024]{1,0:T(8,128)(2,1)S(1)} %slice.64), channel_id=1, source_target_pairs={{0,2},{1,3},{2,0},{3,1},{4,6},{5,7},{6,4},{7,5},{8,10},{9,11},{10,... | collective-permute-start | bytes 393224 | tf_op jit(solution)/shard_map/ppermute | solution.py:29
  41.2 7.8 %collective-permute-start.20 = (bf16[64,1024]{1,0:T(8,128)(2,1)S(1)}, bf16[64,1024]{1,0:T(8,128)(2,1)S(1)}, u32[]{:S(2)}, u32[]{:S(2)}) collective-permute-start(bf16[64,1024]{1,0:T(8,128)(2,1)S(1)} %slice.63), channel_id=1, source_target_pairs={{0,2},{1,3},{2,0},{3,1},{4,6},{5,7},{6,4},{7,5},{8,10},{9,11},{10,... | collective-permute-start | bytes 393224 | tf_op jit(solution)/shard_map/ppermute | solution.py:29
  42.3 9.6 %collective-permute-start.23 = (bf16[64,1024]{1,0:T(8,128)(2,1)S(1)}, bf16[64,1024]{1,0:T(8,128)(2,1)S(1)}, u32[]{:S(2)}, u32[]{:S(2)}) collective-permute-start(bf16[64,1024]{1,0:T(8,128)(2,1)S(1)} %slice.62), channel_id=1, source_target_pairs={{0,2},{1,3},{2,0},{3,1},{4,6},{5,7},{6,4},{7,5},{8,10},{9,11},{10,... | collective-permute-start | bytes 393224 | tf_op jit(solution)/shard_map/ppermute | solution.py:29
  43.6 11.1 %collective-permute-start.26 = (bf16[64,1024]{1,0:T(8,128)(2,1)S(1)}, bf16[64,1024]{1,0:T(8,128)(2,1)S(1)}, u32[]{:S(2)}, u32[]{:S(2)}) collective-permute-start(bf16[64,1024]{1,0:T(8,128)(2,1)S(1)} %slice.61), channel_id=1, source_target_pairs={{0,2},{1,3},{2,0},{3,1},{4,6},{5,7},{6,4},{7,5},{8,10},{9,11},{10,... | collective-permute-start | bytes 393224 | tf_op jit(solution)/shard_map/ppermute | solution.py:29
  44.6 12.4 %collective-permute-start.29 = (bf16[64,1024]{1,0:T(8,128)(2,1)S(1)}, bf16[64,1024]{1,0:T(8,128)(2,1)S(1)}, u32[]{:S(2)}, u32[]{:S(2)}) collective-permute-start(bf16[64,1024]{1,0:T(8,128)(2,1)S(1)} %slice.60), channel_id=1, source_target_pairs={{0,2},{1,3},{2,0},{3,1},{4,6},{5,7},{6,4},{7,5},{8,10},{9,11},{10,... | collective-permute-start | bytes 393224 | tf_op jit(solution)/shard_map/ppermute | solution.py:29
  46.3 12.4 %collective-permute-start.18 = (bf16[64,1024]{1,0:T(8,128)(2,1)S(1)}, bf16[64,1024]{1,0:T(8,128)(2,1)S(1)}, u32[]{:S(2)}, u32[]{:S(2)}) collective-permute-start(bf16[64,1024]{1,0:T(8,128)(2,1)S(1)} %shard_map.77), channel_id=1, source_target_pairs={{0,8},{8,16},{16,24},{24,0},{1,9},{9,17},{17,25},{25,1},{2,10},{10... | collective-permute-start | bytes 393224 | tf_op jit(solution)/shard_map/ppermute | solution.py:24
  49.1 9.7 %collective-permute-start.21 = (bf16[64,1024]{1,0:T(8,128)(2,1)S(1)}, bf16[64,1024]{1,0:T(8,128)(2,1)S(1)}, u32[]{:S(2)}, u32[]{:S(2)}) collective-permute-start(bf16[64,1024]{1,0:T(8,128)(2,1)S(1)} %shard_map.79), channel_id=1, source_target_pairs={{0,8},{8,16},{16,24},{24,0},{1,9},{9,17},{17,25},{25,1},{2,10},{10... | collective-permute-start | bytes 393224 | tf_op jit(solution)/shard_map/ppermute | solution.py:24
  51.9 7.1 %collective-permute-start.24 = (bf16[64,1024]{1,0:T(8,128)(2,1)S(1)}, bf16[64,1024]{1,0:T(8,128)(2,1)S(1)}, u32[]{:S(2)}, u32[]{:S(2)}) collective-permute-start(bf16[64,1024]{1,0:T(8,128)(2,1)S(1)} %shard_map.80), channel_id=1, source_target_pairs={{0,8},{8,16},{16,24},{24,0},{1,9},{9,17},{17,25},{25,1},{2,10},{10... | collective-permute-start | bytes 393224 | tf_op jit(solution)/shard_map/ppermute | solution.py:24
  54.7 7.1 %collective-permute-start.27 = (bf16[64,1024]{1,0:T(8,128)(2,1)S(1)}, bf16[64,1024]{1,0:T(8,128)(2,1)S(1)}, u32[]{:S(2)}, u32[]{:S(2)}) collective-permute-start(bf16[64,1024]{1,0:T(8,128)(2,1)S(1)} %shard_map.81), channel_id=1, source_target_pairs={{0,8},{8,16},{16,24},{24,0},{1,9},{9,17},{17,25},{25,1},{2,10},{10... | collective-permute-start | bytes 393224 | tf_op jit(solution)/shard_map/ppermute | solution.py:24
  57.1 7.3 %collective-permute-start.30 = (bf16[64,1024]{1,0:T(8,128)(2,1)S(1)}, bf16[64,1024]{1,0:T(8,128)(2,1)S(1)}, u32[]{:S(2)}, u32[]{:S(2)}) collective-permute-start(bf16[64,1024]{1,0:T(8,128)(2,1)S(1)} %shard_map.82), channel_id=1, source_target_pairs={{0,8},{8,16},{16,24},{24,0},{1,9},{9,17},{17,25},{25,1},{2,10},{10... | collective-permute-start | bytes 393224 | tf_op jit(solution)/shard_map/ppermute | solution.py:24
  61.8 2.5 %copy-start = (bf16[1,64,5120]{2,1,0:T(8,128)(2,1)}, bf16[1,64,5120]{2,1,0:T(8,128)(2,1)S(1)}, u32[]{:S(2)}) copy-start(bf16[1,64,5120]{2,1,0:T(8,128)(2,1)S(1)} %bitcast_dynamic-update-slice_fusion.1) | copy-start | bytes 1966084

commit v7 on v6

--- a/solution.py
+++ b/solution.py
@@ -149,7 +149,7 @@
         out[:, to] = total.astype(out.dtype)
 
 
-def own_kernel(block_rows, lengths, n0, n1, f0, f1, w_key, w_value, w, *refs):
+def own_kernel(block_rows, lengths, n0, f0, other, w_key, w_value, w, *refs):
     own_sum, own_send, query, key, value, w_near, w_far, cosine, sine, allowed, sems = refs
     piece, depth = n0.shape
     ctx = lax.axis_index("ctx")
@@ -160,7 +160,9 @@
     for copy in copies:
         copy.start()
     fill_tables(piece, block_rows, lengths, cosine, sine, allowed)
-    near, far = stacked((n0, n1)), stacked((f0, f1))
+    at = pl.multiple_of(ctx * depth, depth)
+    near = jnp.concatenate([n0[...], other[:, pl.ds(at, depth)]], axis=0)
+    far = jnp.concatenate([f0[...], other[:, pl.ds(depth - at, depth)]], axis=0)
     wide = key.shape[1]
     for index, weight in enumerate((key, value)):
         copies[index].wait()
@@ -319,8 +321,7 @@
     )(in_hbm(own))
     far_a = swap(x_far, "ctx", 1)
     near_b = swap(x_near, "tp", 2)
-    x_near_s = swap(x_near, "tp", 1)
-    x_far_s = swap(x_far, "tp", 1)
+    own_s = swap(own, "tp", 1)
 
     wide = w_query.shape[1]
     kv_wide = 2 * w_key.shape[1]
@@ -338,11 +339,11 @@
         ],
         kv_flops + 8 * rows * half * wide,
         8 * rows * half,
-        in_specs=[smem] + [vmem] * 4 + [anywhere] * 3,
+        in_specs=[smem] + [vmem] * 3 + [anywhere] * 3,
         scratch_shapes=[pltpu.SemaphoreType.DMA((4,))],
     )(
         in_hbm(doc_lengths),
-        *(x_near, x_near_s, x_far, x_far_s),
+        *(x_near, x_far, own_s),
         *(in_hbm(w_key), in_hbm(w_value), in_hbm(w_query)),
     )
     key, value, w_near, w_far = in_vmem(key), in_vmem(value), in_vmem(w_near), in_vmem(w_far)

time: 65.2 us -> 65.1 us (level)
    ppermute x26 -> x25, starting transfers between devices: 17.9 us -> 17.4 us  [swap(): lax.ppermute(value, axis, [(source, source ^ bit) for source in range(cou...]
    ppermute x26 -> x25, waiting for transfers between devices: 17.3 us -> 17.7 us  [swap(): lax.ppermute(value, axis, [(source, source ^ bit) for source in range(cou...]
  transfers between devices with their start and end apart: 31 -> 30, of which waited for: 17 -> 18; matrix products, arithmetic and copies ran while one was open for 1% -> 1% of each run, Pallas kernels for 18% -> 20%
where the time goes in v7:
time: 65.1 us; the launch traced here: 64.9 us
  starting transfers between devices  25.5 us (39%)
  waiting for transfers between devices  23.3 us (36%)
  Pallas kernels  14.6 us (22%)
  local copies, waits for them, and re-layouts  0.92 us (1%)
    ppermute x25, waiting for transfers between devices, swap(): lax.ppermute(value, axis, [(source, source ^ bit) for source in range(cou...  17.7 us
    ppermute x25, starting transfers between devices, swap(): lax.ppermute(value, axis, [(source, source ^ bit) for source in range(cou...  17.4 us
    ppermute x5, starting transfers between devices, from_behind(): return lax.ppermute(value, axis, pairs)  8.15 us
    pallas_call x1, Pallas kernels, on_four_by_two(): call(functools.partial(own_kernel, block_rows), [*sums, shape(2 * rows, w...  6.43 us
    ppermute x5, waiting for transfers between devices, from_behind(): return lax.ppermute(value, axis, pairs)  5.52 us
    pallas_call x2, Pallas kernels, project_out(): call(functools.partial(out_kernel, first), pair * chunks, 2 * rows * dept...  2.36 us
  transfers between devices with their start and end apart: 30, of which 18 were waited for; matrix products, arithmetic and copies ran while one was open for 1% of the time, Pallas kernels for 20%

profile of v7, /device:TPU:0, one launch (start us, length us, event | category | flops | bytes accessed | tf_op | source)
XLA Modules:
  0.0 64.9 jit_solution(18112060864198735384)
XLA Ops:
  0.0 0.5 collective-permute-start
  0.5 1.1 %shard_map.64 = (bf16[64,2560]{1,0:T(8,128)(2,1)S(1)}, bf16[64,2560]{1,0:T(8,128)(2,1)S(1)}) custom-call(bf16[64,5120]{1,0:T(8,128)(2,1)} %bitcast.23), custom_call_target="tpu_custom_call" | custom-call | bytes 1048576 | tf_op jit(solution)/shard_map/pallas_call | solution.py:314
  1.5 2.6 %collective-permute-start.1 = (bf16[64,2560]{1,0:T(8,128)(2,1)S(1)}, bf16[64,2560]{1,0:T(8,128)(2,1)S(1)}, u32[]{:S(2)}, u32[]{:S(2)}) collective-permute-start(bf16[64,2560]{1,0:T(8,128)(2,1)S(1)} %get-tuple-element.40.f0.refs_0_), channel_id=1, source_target_pairs={{0,4},{4,0},{1,5},{5,1},{2,6},{6,2},{3,7},{7,3},{8,12},{12,8},{9,1... | collective-permute-start | bytes 983048 | tf_op jit(solution)/shard_map/ppermute | solution.py:29
  4.1 1.5 %collective-permute-start.2 = (bf16[64,2560]{1,0:T(8,128)(2,1)S(1)}, bf16[64,2560]{1,0:T(8,128)(2,1)S(1)}, u32[]{:S(2)}, u32[]{:S(2)}) collective-permute-start(bf16[64,2560]{1,0:T(8,128)(2,1)S(1)} %get-tuple-element.39.n0), channel_id=1, source_target_pairs={{0,2},{1,3},{2,0},{3,1},{4,6},{5,7},{6,4},{7,5},{8,10},{9,11},{10,... | collective-permute-start | bytes 983048 | tf_op jit(solution)/shard_map/ppermute | solution.py:29
  5.6 6.4 %shard_map.65 = (f32[128,512]{1,0:T(8,128)S(1)}, bf16[128,512]{1,0:T(8,128)(2,1)S(1)}, bf16[128,768]{1,0:T(8,128)(2,1)S(1)}, bf16[2560,256]{1,0:T(8,128)(2,1)S(1...) custom-call(s32[1,8]{1,0:T(1,128)} %lengths.1, ...), custom_call_target="tpu_custom_call" | custom-call | flops 1342177280 | bytes 1310720 | tf_op jit(solution)/shard_map/pallas_call | solution.py:330
  12.1 0.4 collective-permute-done.1.refs_0_
  12.5 1.5 %collective-permute-done.2.refs_1_ = bf16[64,2560]{1,0:T(8,128)(2,1)S(1)} collective-permute-done((bf16[64,2560]{1,0:T(8,128)(2,1)S(1)}, bf16[64,2560]{1,0:T(8,128)(2,1)S(1)}, u32[]{:S(2)}, u32[]{:S(2)}) %collective-permute-start.2) | collective-permute-done | bytes 327712 | tf_op jit(solution)/shard_map/ppermute | solution.py:29
  14.0 0.1 collective-permute-start.3
  14.1 0.5 collective-permute-start.6
  14.6 1.5 %collective-permute-start.7 = (bf16[64,2560]{1,0:T(8,128)(2,1)S(1)}, bf16[64,2560]{1,0:T(8,128)(2,1)S(1)}, u32[]{:S(2)}, u32[]{:S(2)}) collective-permute-start(bf16[64,2560]{1,0:T(8,128)(2,1)S(1)} %get-tuple-element.49.f0), channel_id=1, source_target_pairs={{0,2},{1,3},{2,0},{3,1},{4,6},{5,7},{6,4},{7,5},{8,10},{9,11},{10,... | collective-permute-start | bytes 983048 | tf_op jit(solution)/shard_map/ppermute | solution.py:29
  16.1 0.5 collective-permute-start.4
  16.6 0.8 %shard_map.69 = (f32[128,512]{1,0:T(8,128)S(1)}, bf16[192,512]{1,0:T(8,128)(2,1)S(1)}, bf16[64,512]{1,0:T(8,128)(2,1)S(1)}) custom-call(bf16[64,2560]{1,0:T(8,128)(2,1)S(1)} %get-tuple-element.43.n0, bf16[64,2560]{1,0:T(8,128)(2,1)S(1)} %collective-permute-done.3.n1, bf16[64,2560]{1,0:T(8,128)(2,1)S(1)} %get-tuple-element.49.f0, ...), custom_call_target="tpu_custom_call" | custom-call | flops 671088640 | bytes 1310720 | tf_op jit(solution)/shard_map/pallas_call | solution.py:356
  17.5 1.6 %collective-permute-start.8 = (bf16[192,512]{1,0:T(8,128)(2,1)S(1)}, bf16[192,512]{1,0:T(8,128)(2,1)S(1)}, u32[]{:S(2)}, u32[]{:S(2)}) collective-permute-start(bf16[192,512]{1,0:T(8,128)(2,1)S(1)} %get-tuple-element.53.send), channel_id=1, source_target_pairs={{0,4},{4,0},{1,5},{5,1},{2,6},{6,2},{3,7},{7,3},{8,12},{12,8},{9,1... | collective-permute-start | bytes 589832 | tf_op jit(solution)/shard_map/ppermute | solution.py:29
  19.0 3.4 %collective-permute-done.4._.early_a = bf16[128,512]{1,0:T(8,128)(2,1)S(1)} collective-permute-done((bf16[128,512]{1,0:T(8,128)(2,1)S(1)}, bf16[128,512]{1,0:T(8,128)(2,1)S(1)}, u32[]{:S(2)}, u32[]{:S(2)}) %collective-permute-start.4) | collective-permute-done | bytes 131104 | tf_op jit(solution)/shard_map/ppermute | solution.py:29
  22.5 0.7 %shard_map.67.refs_1_.refs_3_.before = f32[128,768]{1,0:T(8,128)S(1)} custom-call(bf16[64,2560]{1,0:T(8,128)(2,1)S(1)} %get-tuple-element.43.n0, bf16[64,2560]{1,0:T(8,128)(2,1)S(1)} %collective-permute-done.3.n1, bf16[128,512]{1,0:T(8,128)(2,1)S(1)} %collective-permute-done.4._.early_a, bf16[2560,768]{1,0:T(8,128)(2,1)S(1)} %get-tuple-element.45.w), custom_call_target="tpu_custom_call" | custom-call | flops 503316480 | bytes 655360 | tf_op jit(solution)/shard_map/pallas_call | solution.py:363
  23.2 0.1 collective-permute-start.5
  23.3 1.6 %collective-permute-done.7.refs_0_.refs_1_.refs_2_ = bf16[64,2560]{1,0:T(8,128)(2,1)S(1)} collective-permute-done((bf16[64,2560]{1,0:T(8,128)(2,1)S(1)}, bf16[64,2560]{1,0:T(8,128)(2,1)S(1)}, u32[]{:S(2)}, u32[]{:S(2)}) %collective-permute-start.7) | collective-permute-done | bytes 327712 | tf_op jit(solution)/shard_map/ppermute | solution.py:29
  24.9 0.6 collective-permute-done.8.refs_4_.early_b.more_a
  25.6 0.1 collective-permute-start.9
  25.6 0.5 collective-permute-start.10
  26.1 0.9 %collective-permute-done.9.refs_0_ = bf16[64,1280]{1,0:T(8,128)(2,1)S(1)} collective-permute-done((bf16[64,1280]{1,0:T(8,128)(2,1)S(1)}, bf16[64,1280]{1,0:T(8,128)(2,1)S(1)}, u32[]{:S(2)}, u32[]{:S(2)}) %collective-permute-start.9) | collective-permute-done | bytes 163872 | tf_op jit(solution)/shard_map/ppermute | solution.py:29
  27.0 0.2 collective-permute-done.10.refs_1_
  27.3 0.5 shard_map.71.refs_3_.far
  27.8 0.6 collective-permute-start.14
  28.4 2.9 %collective-permute-done.5.refs_0_.refs_1_.refs_2_.f0 = bf16[64,2560]{1,0:T(8,128)(2,1)S(1)} collective-permute-done((bf16[64,2560]{1,0:T(8,128)(2,1)S(1)}, bf16[64,2560]{1,0:T(8,128)(2,1)S(1)}, u32[]{:S(2)}, u32[]{:S(2)}) %collective-permute-start.5) | collective-permute-done | bytes 327712 | tf_op jit(solution)/shard_map/ppermute | solution.py:29
  31.3 0.1 collective-permute-start.12
  31.4 0.5 collective-permute-start.13
  31.9 0.1 collective-permute-start.11
  32.0 0.3 shard_map.74.done
  32.3 0.9 %collective-permute-done.11.refs_0_ = bf16[64,768]{1,0:T(8,128)(2,1)S(1)} collective-permute-done((bf16[64,768]{1,0:T(8,128)(2,1)S(1)}, bf16[64,768]{1,0:T(8,128)(2,1)S(1)}, u32[]{:S(2)}, u32[]{:S(2)}) %collective-permute-start.11) | collective-permute-done | bytes 98336 | tf_op jit(solution)/shard_map/ppermute | solution.py:29
  33.2 0.9 %shard_map.73.q_last = bf16[128,768]{1,0:T(8,128)(2,1)S(1)} custom-call(bf16[64,2560]{1,0:T(8,128)(2,1)S(1)} %collective-permute-done.5.refs_0_.refs_1_.refs_2_.f0, bf16[2560,768]{1,0:T(8,128)(2,1)S(1)} %get-tuple-element.46.w, f32[128,768]{1,0:T(8,128)S(1)} %shard_map.67.refs_1_.refs_3_.before, f32[512,128]{1,0:T(8,128)S(1)} %get-tuple-element.47.cosine, ...), custom_call_target="tpu_custom_call" | custom-call | flops 503316480 | bytes 1310720 | tf_op jit(solution)/shard_map/pallas_call | solution.py:387
  34.1 0.8 %collective-permute-done.14.more_b = bf16[192,512]{1,0:T(8,128)(2,1)S(1)} collective-permute-done((bf16[192,512]{1,0:T(8,128)(2,1)S(1)}, bf16[192,512]{1,0:T(8,128)(2,1)S(1)}, u32[]{:S(2)}, u32[]{:S(2)}) %collective-permute-start.14) | collective-permute-done | bytes 196640 | tf_op jit(solution)/shard_map/ppermute | solution.py:29
  34.9 1.2 %shard_map.75.attended = bf16[256,768]{1,0:T(8,128)(2,1)S(1)} custom-call(bf16[128,768]{1,0:T(8,128)(2,1)S(1)} %get-tuple-element.41.q_first, bf16[128,768]{1,0:T(8,128)(2,1)S(1)} %shard_map.73.q_last, bf16[256,512]{1,0:T(8,128)(2,1)S(1)} %shard_map.74.done, f32[128,512]{1,0:T(8,128)S(1)} %get-tuple-element.60.sum_a, ...), custom_call_target="tpu_custom_call" | custom-call | flops 201326592 | bytes 1048576 | tf_op jit(solution)/shard_map/pallas_call | solution.py:398
  36.1 0.6 shard_map.76
  36.7 0.1 collective-permute-start.15
  36.8 1.8 %shard_map.78 = (f32[128,1024]{1,0:T(8,128)S(1)}, bf16[128,1024]{1,0:T(8,128)(2,1)S(1)}, f32[128,1024]{1,0:T(8,128)S(1)}, bf16[128,1024]{1,0:T(8,128)(2,1)S(1)},...) custom-call(bf16[256,768]{1,0:T(8,128)(2,1)S(1)} %shard_map.75.atten, ...), custom_call_target="tpu_custom_call" | custom-call | flops 1610612736 | bytes 393216 | tf_op jit(solution)/shard_map/pallas_call | solution.py:286
  38.6 0.6 collective-permute-start.18
  39.1 0.1 collective-permute-start.21
  39.2 0.4 collective-permute-start.24
  39.6 0.1 collective-permute-start.27
  39.7 0.1 convert_add_fusion.4
  39.8 1.2 %collective-permute-start.16 = (bf16[64,1024]{1,0:T(8,128)(2,1)S(1)}, bf16[64,1024]{1,0:T(8,128)(2,1)S(1)}, u32[]{:S(2)}, u32[]{:S(2)}) collective-permute-start(bf16[64,1024]{1,0:T(8,128)(2,1)S(1)} %slice.64), channel_id=1, source_target_pairs={{0,2},{1,3},{2,0},{3,1},{4,6},{5,7},{6,4},{7,5},{8,10},{9,11},{10,... | collective-permute-start | bytes 393224 | tf_op jit(solution)/shard_map/ppermute | solution.py:29
  41.0 0.1 convert_add_fusion.3
  41.1 0.9 %collective-permute-start.19 = (bf16[64,1024]{1,0:T(8,128)(2,1)S(1)}, bf16[64,1024]{1,0:T(8,128)(2,1)S(1)}, u32[]{:S(2)}, u32[]{:S(2)}) collective-permute-start(bf16[64,1024]{1,0:T(8,128)(2,1)S(1)} %slice.63), channel_id=1, source_target_pairs={{0,2},{1,3},{2,0},{3,1},{4,6},{5,7},{6,4},{7,5},{8,10},{9,11},{10,... | collective-permute-start | bytes 393224 | tf_op jit(solution)/shard_map/ppermute | solution.py:29
  42.1 0.1 convert_add_fusion.2
  42.2 1.2 %collective-permute-start.22 = (bf16[64,1024]{1,0:T(8,128)(2,1)S(1)}, bf16[64,1024]{1,0:T(8,128)(2,1)S(1)}, u32[]{:S(2)}, u32[]{:S(2)}) collective-permute-start(bf16[64,1024]{1,0:T(8,128)(2,1)S(1)} %slice.62), channel_id=1, source_target_pairs={{0,2},{1,3},{2,0},{3,1},{4,6},{5,7},{6,4},{7,5},{8,10},{9,11},{10,... | collective-permute-start | bytes 393224 | tf_op jit(solution)/shard_map/ppermute | solution.py:29
  43.4 0.1 convert_add_fusion.1
  43.5 0.9 %collective-permute-start.25 = (bf16[64,1024]{1,0:T(8,128)(2,1)S(1)}, bf16[64,1024]{1,0:T(8,128)(2,1)S(1)}, u32[]{:S(2)}, u32[]{:S(2)}) collective-permute-start(bf16[64,1024]{1,0:T(8,128)(2,1)S(1)} %slice.61), channel_id=1, source_target_pairs={{0,2},{1,3},{2,0},{3,1},{4,6},{5,7},{6,4},{7,5},{8,10},{9,11},{10,... | collective-permute-start | bytes 393224 | tf_op jit(solution)/shard_map/ppermute | solution.py:29
  44.4 0.1 convert_add_fusion
  44.6 1.2 %collective-permute-start.28 = (bf16[64,1024]{1,0:T(8,128)(2,1)S(1)}, bf16[64,1024]{1,0:T(8,128)(2,1)S(1)}, u32[]{:S(2)}, u32[]{:S(2)}) collective-permute-start(bf16[64,1024]{1,0:T(8,128)(2,1)S(1)} %slice.60), channel_id=1, source_target_pairs={{0,2},{1,3},{2,0},{3,1},{4,6},{5,7},{6,4},{7,5},{8,10},{9,11},{10,... | collective-permute-start | bytes 393224 | tf_op jit(solution)/shard_map/ppermute | solution.py:29
  45.8 0.4 collective-permute-done.16.arrived
  46.2 1.6 %collective-permute-start.17 = (bf16[64,1024]{1,0:T(8,128)(2,1)S(1)}, bf16[64,1024]{1,0:T(8,128)(2,1)S(1)}, u32[]{:S(2)}, u32[]{:S(2)}) collective-permute-start(bf16[64,1024]{1,0:T(8,128)(2,1)S(1)} %shard_map.77), channel_id=1, source_target_pairs={{0,8},{8,16},{16,24},{24,0},{1,9},{9,17},{17,25},{25,1},{2,10},{10... | collective-permute-start | bytes 393224 | tf_op jit(solution)/shard_map/ppermute | solution.py:24
  47.9 1.0 %collective-permute-done.19.arrived = bf16[64,1024]{1,0:T(8,128)(2,1)S(1)} collective-permute-done((bf16[64,1024]{1,0:T(8,128)(2,1)S(1)}, bf16[64,1024]{1,0:T(8,128)(2,1)S(1)}, u32[]{:S(2)}, u32[]{:S(2)}) %collective-permute-start.19) | collective-permute-done | bytes 131104 | tf_op jit(solution)/shard_map/ppermute | solution.py:29
  49.0 1.6 %collective-permute-start.20 = (bf16[64,1024]{1,0:T(8,128)(2,1)S(1)}, bf16[64,1024]{1,0:T(8,128)(2,1)S(1)}, u32[]{:S(2)}, u32[]{:S(2)}) collective-permute-start(bf16[64,1024]{1,0:T(8,128)(2,1)S(1)} %shard_map.79), channel_id=1, source_target_pairs={{0,8},{8,16},{16,24},{24,0},{1,9},{9,17},{17,25},{25,1},{2,10},{10... | collective-permute-start | bytes 393224 | tf_op jit(solution)/shard_map/ppermute | solution.py:24
  50.6 1.1 %collective-permute-done.22.arrived = bf16[64,1024]{1,0:T(8,128)(2,1)S(1)} collective-permute-done((bf16[64,1024]{1,0:T(8,128)(2,1)S(1)}, bf16[64,1024]{1,0:T(8,128)(2,1)S(1)}, u32[]{:S(2)}, u32[]{:S(2)}) %collective-permute-start.22) | collective-permute-done | bytes 131104 | tf_op jit(solution)/shard_map/ppermute | solution.py:29
  51.8 1.6 %collective-permute-start.23 = (bf16[64,1024]{1,0:T(8,128)(2,1)S(1)}, bf16[64,1024]{1,0:T(8,128)(2,1)S(1)}, u32[]{:S(2)}, u32[]{:S(2)}) collective-permute-start(bf16[64,1024]{1,0:T(8,128)(2,1)S(1)} %shard_map.80), channel_id=1, source_target_pairs={{0,8},{8,16},{16,24},{24,0},{1,9},{9,17},{17,25},{25,1},{2,10},{10... | collective-permute-start | bytes 393224 | tf_op jit(solution)/shard_map/ppermute | solution.py:24
  53.5 1.1 %collective-permute-done.25.arrived = bf16[64,1024]{1,0:T(8,128)(2,1)S(1)} collective-permute-done((bf16[64,1024]{1,0:T(8,128)(2,1)S(1)}, bf16[64,1024]{1,0:T(8,128)(2,1)S(1)}, u32[]{:S(2)}, u32[]{:S(2)}) %collective-permute-start.25) | collective-permute-done | bytes 131104 | tf_op jit(solution)/shard_map/ppermute | solution.py:29
  54.6 1.6 %collective-permute-start.26 = (bf16[64,1024]{1,0:T(8,128)(2,1)S(1)}, bf16[64,1024]{1,0:T(8,128)(2,1)S(1)}, u32[]{:S(2)}, u32[]{:S(2)}) collective-permute-start(bf16[64,1024]{1,0:T(8,128)(2,1)S(1)} %shard_map.81), channel_id=1, source_target_pairs={{0,8},{8,16},{16,24},{24,0},{1,9},{9,17},{17,25},{25,1},{2,10},{10... | collective-permute-start | bytes 393224 | tf_op jit(solution)/shard_map/ppermute | solution.py:24
  56.3 0.7 %collective-permute-done.28.arrived = bf16[64,1024]{1,0:T(8,128)(2,1)S(1)} collective-permute-done((bf16[64,1024]{1,0:T(8,128)(2,1)S(1)}, bf16[64,1024]{1,0:T(8,128)(2,1)S(1)}, u32[]{:S(2)}, u32[]{:S(2)}) %collective-permute-start.28) | collective-permute-done | bytes 131104 | tf_op jit(solution)/shard_map/ppermute | solution.py:29
  57.0 1.6 %collective-permute-start.29 = (bf16[64,1024]{1,0:T(8,128)(2,1)S(1)}, bf16[64,1024]{1,0:T(8,128)(2,1)S(1)}, u32[]{:S(2)}, u32[]{:S(2)}) collective-permute-start(bf16[64,1024]{1,0:T(8,128)(2,1)S(1)} %shard_map.82), channel_id=1, source_target_pairs={{0,8},{8,16},{16,24},{24,0},{1,9},{9,17},{17,25},{25,1},{2,10},{10... | collective-permute-start | bytes 393224 | tf_op jit(solution)/shard_map/ppermute | solution.py:24
  58.7 0.2 collective-permute-done.23
  58.9 2.8 %collective-permute-done.26 = bf16[64,1024]{1,0:T(8,128)(2,1)S(1)} collective-permute-done((bf16[64,1024]{1,0:T(8,128)(2,1)S(1)}, bf16[64,1024]{1,0:T(8,128)(2,1)S(1)}, u32[]{:S(2)}, u32[]{:S(2)}) %collective-permute-start.26) | collective-permute-done | bytes 131104 | tf_op jit(solution)/shard_map/ppermute | solution.py:24
  61.8 2.5 %collective-permute-done.29 = bf16[64,1024]{1,0:T(8,128)(2,1)S(1)} collective-permute-done((bf16[64,1024]{1,0:T(8,128)(2,1)S(1)}, bf16[64,1024]{1,0:T(8,128)(2,1)S(1)}, u32[]{:S(2)}, u32[]{:S(2)}) %collective-permute-start.29) | collective-permute-done | bytes 131104 | tf_op jit(solution)/shard_map/ppermute | solution.py:24
  64.3 0.7 %bitcast_dynamic-update-slice_fusion = bf16[1,64,5120]{2,1,0:T(8,128)(2,1)} fusion(bf16[1,64,5120]{2,1,0:T(8,128)(2,1)} %copy-done, bf16[64,1024]{1,0:T(8,128)(2,1)S(1)} %collective-permute-done.29), kind=kLoop, calls=%fused_computation.11 | loop fusion | bytes 262144 | tf_op jit(solution)/shard_map/dynamic_update_slice | solution.py:413
  (42 shorter events, 0.6 us)
Async XLA Ops:
  0.0 5.6 %collective-permute-start = (bf16[64,5120]{1,0:T(8,128)(2,1)}, bf16[64,5120]{1,0:T(8,128)(2,1)S(1)}, u32[]{:S(2)}, u32[]{:S(2)}) collective-permute-start(bf16[64,5120]{1,0:T(8,128)(2,1)} %bitcast.22), channel_id=1, source_target_pairs={{0,1},{1,0},{2,3},{3,2},{4,5},{5,4},{6,7},{7,6},{8,9},{9,8},{10,11... | collective-permute-start | bytes 1966088 | tf_op jit(solution)/shard_map/ppermute | solution.py:29
  1.5 10.9 %collective-permute-start.1 = (bf16[64,2560]{1,0:T(8,128)(2,1)S(1)}, bf16[64,2560]{1,0:T(8,128)(2,1)S(1)}, u32[]{:S(2)}, u32[]{:S(2)}) collective-permute-start(bf16[64,2560]{1,0:T(8,128)(2,1)S(1)} %get-tuple-element.40.f0.refs_0_), channel_id=1, source_target_pairs={{0,4},{4,0},{1,5},{5,1},{2,6},{6,2},{3,7},{7,3},{8,12},{12,8},{9,1... | collective-permute-start | bytes 983048 | tf_op jit(solution)/shard_map/ppermute | solution.py:29
  4.1 9.8 %collective-permute-start.2 = (bf16[64,2560]{1,0:T(8,128)(2,1)S(1)}, bf16[64,2560]{1,0:T(8,128)(2,1)S(1)}, u32[]{:S(2)}, u32[]{:S(2)}) collective-permute-start(bf16[64,2560]{1,0:T(8,128)(2,1)S(1)} %get-tuple-element.39.n0), channel_id=1, source_target_pairs={{0,2},{1,3},{2,0},{3,1},{4,6},{5,7},{6,4},{7,5},{8,10},{9,11},{10,... | collective-permute-start | bytes 983048 | tf_op jit(solution)/shard_map/ppermute | solution.py:29
  14.0 2.6 %collective-permute-start.3 = (bf16[64,2560]{1,0:T(8,128)(2,1)S(1)}, bf16[64,2560]{1,0:T(8,128)(2,1)S(1)}, u32[]{:S(2)}, u32[]{:S(2)}) collective-permute-start(bf16[64,2560]{1,0:T(8,128)(2,1)S(1)} %get-tuple-element.43.n0), channel_id=1, source_target_pairs={{0,1},{1,0},{2,3},{3,2},{4,5},{5,4},{6,7},{7,6},{8,9},{9,8},{10,11... | collective-permute-start | bytes 983048 | tf_op jit(solution)/shard_map/ppermute | solution.py:29
  14.1 2.6 %collective-permute-start.6 = (bf16[64,2560]{1,0:T(8,128)(2,1)S(1)}, bf16[64,2560]{1,0:T(8,128)(2,1)S(1)}, u32[]{:S(2)}, u32[]{:S(2)}) collective-permute-start(bf16[64,2560]{1,0:T(8,128)(2,1)S(1)} %get-tuple-element.49.f0), channel_id=1, source_target_pairs={{0,1},{1,0},{2,3},{3,2},{4,5},{5,4},{6,7},{7,6},{8,9},{9,8},{10,11... | collective-permute-start | bytes 983048 | tf_op jit(solution)/shard_map/ppermute | solution.py:29
  14.6 10.3 %collective-permute-start.7 = (bf16[64,2560]{1,0:T(8,128)(2,1)S(1)}, bf16[64,2560]{1,0:T(8,128)(2,1)S(1)}, u32[]{:S(2)}, u32[]{:S(2)}) collective-permute-start(bf16[64,2560]{1,0:T(8,128)(2,1)S(1)} %get-tuple-element.49.f0), channel_id=1, source_target_pairs={{0,2},{1,3},{2,0},{3,1},{4,6},{5,7},{6,4},{7,5},{8,10},{9,11},{10,... | collective-permute-start | bytes 983048 | tf_op jit(solution)/shard_map/ppermute | solution.py:29
  16.1 6.4 %collective-permute-start.4 = (bf16[128,512]{1,0:T(8,128)(2,1)S(1)}, bf16[128,512]{1,0:T(8,128)(2,1)S(1)}, u32[]{:S(2)}, u32[]{:S(2)}) collective-permute-start(bf16[128,512]{1,0:T(8,128)(2,1)S(1)} %get-tuple-element.44), channel_id=1, source_target_pairs={{0,4},{4,0},{1,5},{5,1},{2,6},{6,2},{3,7},{7,3},{8,12},{12,8},{9,1... | collective-permute-start | bytes 393224 | tf_op jit(solution)/shard_map/ppermute | solution.py:29
  17.5 8.0 %collective-permute-start.8 = (bf16[192,512]{1,0:T(8,128)(2,1)S(1)}, bf16[192,512]{1,0:T(8,128)(2,1)S(1)}, u32[]{:S(2)}, u32[]{:S(2)}) collective-permute-start(bf16[192,512]{1,0:T(8,128)(2,1)S(1)} %get-tuple-element.53.send), channel_id=1, source_target_pairs={{0,4},{4,0},{1,5},{5,1},{2,6},{6,2},{3,7},{7,3},{8,12},{12,8},{9,1... | collective-permute-start | bytes 589832 | tf_op jit(solution)/shard_map/ppermute | solution.py:29
  23.2 8.1 %collective-permute-start.5 = (bf16[64,2560]{1,0:T(8,128)(2,1)S(1)}, bf16[64,2560]{1,0:T(8,128)(2,1)S(1)}, u32[]{:S(2)}, u32[]{:S(2)}) collective-permute-start(bf16[64,2560]{1,0:T(8,128)(2,1)S(1)} %shard_map.68), channel_id=1, source_target_pairs={{0,2},{1,3},{2,0},{3,1},{4,6},{5,7},{6,4},{7,5},{8,10},{9,11},{10,... | collective-permute-start | bytes 983048 | tf_op jit(solution)/shard_map/ppermute | solution.py:29
  25.6 1.5 %collective-permute-start.9 = (bf16[64,1280]{1,0:T(8,128)(2,1)S(1)}, bf16[64,1280]{1,0:T(8,128)(2,1)S(1)}, u32[]{:S(2)}, u32[]{:S(2)}) collective-permute-start(bf16[64,1280]{1,0:T(8,128)(2,1)S(1)} %get-tuple-element.55), channel_id=1, source_target_pairs={{0,1},{1,0},{2,3},{3,2},{4,5},{5,4},{6,7},{7,6},{8,9},{9,8},{10,11... | collective-permute-start | bytes 491528 | tf_op jit(solution)/shard_map/ppermute | solution.py:29
  25.6 1.6 %collective-permute-start.10 = (bf16[64,1280]{1,0:T(8,128)(2,1)S(1)}, bf16[64,1280]{1,0:T(8,128)(2,1)S(1)}, u32[]{:S(2)}, u32[]{:S(2)}) collective-permute-start(bf16[64,1280]{1,0:T(8,128)(2,1)S(1)} %get-tuple-element.56), channel_id=1, source_target_pairs={{0,1},{1,0},{2,3},{3,2},{4,5},{5,4},{6,7},{7,6},{8,9},{9,8},{10,11... | collective-permute-start | bytes 491528 | tf_op jit(solution)/shard_map/ppermute | solution.py:29
  27.3 8.8 %slice-start = ((s8[7864320]{0:T(1024)(128)(4,1)}), s8[4194304]{0:T(1024)(128)(4,1)S(1)}, s32[]{:S(2)}) async-start(s8[7864320]{0:T(1024)(128)(4,1)} %bitcast.15), calls=%async_computation | async-start | bytes 8388608
  27.8 7.1 %collective-permute-start.14 = (bf16[192,512]{1,0:T(8,128)(2,1)S(1)}, bf16[192,512]{1,0:T(8,128)(2,1)S(1)}, u32[]{:S(2)}, u32[]{:S(2)}) collective-permute-start(bf16[192,512]{1,0:T(8,128)(2,1)S(1)} %shard_map.71.refs_3_.far), channel_id=1, source_target_pairs={{0,4},{4,0},{1,5},{5,1},{2,6},{6,2},{3,7},{7,3},{8,12},{12,8},{9,1... | collective-permute-start | bytes 589832 | tf_op jit(solution)/shard_map/ppermute | solution.py:29
  31.3 1.9 %collective-permute-start.12 = (bf16[64,896]{1,0:T(8,128)(2,1)S(1)}, bf16[64,896]{1,0:T(8,128)(2,1)S(1)}, u32[]{:S(2)}, u32[]{:S(2)}) collective-permute-start(bf16[64,896]{1,0:T(8,128)(2,1)S(1)} %get-tuple-element.58), channel_id=1, source_target_pairs={{0,1},{1,0},{2,3},{3,2},{4,5},{5,4},{6,7},{7,6},{8,9},{9,8},{10,11... | collective-permute-start | bytes 344072 | tf_op jit(solution)/shard_map/ppermute | solution.py:29
  31.4 1.8 %collective-permute-start.13 = (bf16[64,896]{1,0:T(8,128)(2,1)S(1)}, bf16[64,896]{1,0:T(8,128)(2,1)S(1)}, u32[]{:S(2)}, u32[]{:S(2)}) collective-permute-start(bf16[64,896]{1,0:T(8,128)(2,1)S(1)} %get-tuple-element.59), channel_id=1, source_target_pairs={{0,1},{1,0},{2,3},{3,2},{4,5},{5,4},{6,7},{7,6},{8,9},{9,8},{10,11... | collective-permute-start | bytes 344072 | tf_op jit(solution)/shard_map/ppermute | solution.py:29
  31.9 1.3 %collective-permute-start.11 = (bf16[64,768]{1,0:T(8,128)(2,1)S(1)}, bf16[64,768]{1,0:T(8,128)(2,1)S(1)}, u32[]{:S(2)}, u32[]{:S(2)}) collective-permute-start(bf16[64,768]{1,0:T(8,128)(2,1)S(1)} %get-tuple-element.57), channel_id=1, source_target_pairs={{0,1},{1,0},{2,3},{3,2},{4,5},{5,4},{6,7},{7,6},{8,9},{9,8},{10,11... | collective-permute-start | bytes 294920 | tf_op jit(solution)/shard_map/ppermute | solution.py:29
  33.2 2.9 %slice-start.1 = ((s8[7864320]{0:T(1024)(128)(4,1)}), s8[3670016]{0:T(1024)(128)(4,1)S(1)}, s32[]{:S(2)}) async-start(s8[7864320]{0:T(1024)(128)(4,1)} %bitcast.15), calls=%async_computation.1 | async-start | bytes 7340032
  36.7 3.0 %collective-permute-start.15 = (bf16[128,1024]{1,0:T(8,128)(2,1)S(1)}, bf16[128,1024]{1,0:T(8,128)(2,1)S(1)}, u32[]{:S(2)}, u32[]{:S(2)}) collective-permute-start(bf16[128,1024]{1,0:T(8,128)(2,1)S(1)} %get-tuple-element.64), channel_id=1, source_target_pairs={{0,1},{1,0},{2,3},{3,2},{4,5},{5,4},{6,7},{7,6},{8,9},{9,8},{10,11... | collective-permute-start | bytes 786440 | tf_op jit(solution)/shard_map/ppermute | solution.py:29
  38.6 2.5 %collective-permute-start.18 = (bf16[128,1024]{1,0:T(8,128)(2,1)S(1)}, bf16[128,1024]{1,0:T(8,128)(2,1)S(1)}, u32[]{:S(2)}, u32[]{:S(2)}) collective-permute-start(bf16[128,1024]{1,0:T(8,128)(2,1)S(1)} %get-tuple-element.66), channel_id=1, source_target_pairs={{0,1},{1,0},{2,3},{3,2},{4,5},{5,4},{6,7},{7,6},{8,9},{9,8},{10,11... | collective-permute-start | bytes 786440 | tf_op jit(solution)/shard_map/ppermute | solution.py:29
  39.1 2.9 %collective-permute-start.21 = (bf16[128,1024]{1,0:T(8,128)(2,1)S(1)}, bf16[128,1024]{1,0:T(8,128)(2,1)S(1)}, u32[]{:S(2)}, u32[]{:S(2)}) collective-permute-start(bf16[128,1024]{1,0:T(8,128)(2,1)S(1)} %get-tuple-element.68), channel_id=1, source_target_pairs={{0,1},{1,0},{2,3},{3,2},{4,5},{5,4},{6,7},{7,6},{8,9},{9,8},{10,11... | collective-permute-start | bytes 786440 | tf_op jit(solution)/shard_map/ppermute | solution.py:29
  39.2 4.2 %collective-permute-start.24 = (bf16[128,1024]{1,0:T(8,128)(2,1)S(1)}, bf16[128,1024]{1,0:T(8,128)(2,1)S(1)}, u32[]{:S(2)}, u32[]{:S(2)}) collective-permute-start(bf16[128,1024]{1,0:T(8,128)(2,1)S(1)} %get-tuple-element.70), channel_id=1, source_target_pairs={{0,1},{1,0},{2,3},{3,2},{4,5},{5,4},{6,7},{7,6},{8,9},{9,8},{10,11... | collective-permute-start | bytes 786440 | tf_op jit(solution)/shard_map/ppermute | solution.py:29
  39.6 4.8 %collective-permute-start.27 = (bf16[128,1024]{1,0:T(8,128)(2,1)S(1)}, bf16[128,1024]{1,0:T(8,128)(2,1)S(1)}, u32[]{:S(2)}, u32[]{:S(2)}) collective-permute-start(bf16[128,1024]{1,0:T(8,128)(2,1)S(1)} %get-tuple-element.72), channel_id=1, source_target_pairs={{0,1},{1,0},{2,3},{3,2},{4,5},{5,4},{6,7},{7,6},{8,9},{9,8},{10,11... | collective-permute-start | bytes 786440 | tf_op jit(solution)/shard_map/ppermute | solution.py:29
  39.8 6.4 %collective-permute-start.16 = (bf16[64,1024]{1,0:T(8,128)(2,1)S(1)}, bf16[64,1024]{1,0:T(8,128)(2,1)S(1)}, u32[]{:S(2)}, u32[]{:S(2)}) collective-permute-start(bf16[64,1024]{1,0:T(8,128)(2,1)S(1)} %slice.64), channel_id=1, source_target_pairs={{0,2},{1,3},{2,0},{3,1},{4,6},{5,7},{6,4},{7,5},{8,10},{9,11},{10,... | collective-permute-start | bytes 393224 | tf_op jit(solution)/shard_map/ppermute | solution.py:29
  41.1 7.8 %collective-permute-start.19 = (bf16[64,1024]{1,0:T(8,128)(2,1)S(1)}, bf16[64,1024]{1,0:T(8,128)(2,1)S(1)}, u32[]{:S(2)}, u32[]{:S(2)}) collective-permute-start(bf16[64,1024]{1,0:T(8,128)(2,1)S(1)} %slice.63), channel_id=1, source_target_pairs={{0,2},{1,3},{2,0},{3,1},{4,6},{5,7},{6,4},{7,5},{8,10},{9,11},{10,... | collective-permute-start | bytes 393224 | tf_op jit(solution)/shard_map/ppermute | solution.py:29
  42.2 9.6 %collective-permute-start.22 = (bf16[64,1024]{1,0:T(8,128)(2,1)S(1)}, bf16[64,1024]{1,0:T(8,128)(2,1)S(1)}, u32[]{:S(2)}, u32[]{:S(2)}) collective-permute-start(bf16[64,1024]{1,0:T(8,128)(2,1)S(1)} %slice.62), channel_id=1, source_target_pairs={{0,2},{1,3},{2,0},{3,1},{4,6},{5,7},{6,4},{7,5},{8,10},{9,11},{10,... | collective-permute-start | bytes 393224 | tf_op jit(solution)/shard_map/ppermute | solution.py:29
  43.5 11.1 %collective-permute-start.25 = (bf16[64,1024]{1,0:T(8,128)(2,1)S(1)}, bf16[64,1024]{1,0:T(8,128)(2,1)S(1)}, u32[]{:S(2)}, u32[]{:S(2)}) collective-permute-start(bf16[64,1024]{1,0:T(8,128)(2,1)S(1)} %slice.61), channel_id=1, source_target_pairs={{0,2},{1,3},{2,0},{3,1},{4,6},{5,7},{6,4},{7,5},{8,10},{9,11},{10,... | collective-permute-start | bytes 393224 | tf_op jit(solution)/shard_map/ppermute | solution.py:29
  44.6 12.4 %collective-permute-start.28 = (bf16[64,1024]{1,0:T(8,128)(2,1)S(1)}, bf16[64,1024]{1,0:T(8,128)(2,1)S(1)}, u32[]{:S(2)}, u32[]{:S(2)}) collective-permute-start(bf16[64,1024]{1,0:T(8,128)(2,1)S(1)} %slice.60), channel_id=1, source_target_pairs={{0,2},{1,3},{2,0},{3,1},{4,6},{5,7},{6,4},{7,5},{8,10},{9,11},{10,... | collective-permute-start | bytes 393224 | tf_op jit(solution)/shard_map/ppermute | solution.py:29
  46.2 12.4 %collective-permute-start.17 = (bf16[64,1024]{1,0:T(8,128)(2,1)S(1)}, bf16[64,1024]{1,0:T(8,128)(2,1)S(1)}, u32[]{:S(2)}, u32[]{:S(2)}) collective-permute-start(bf16[64,1024]{1,0:T(8,128)(2,1)S(1)} %shard_map.77), channel_id=1, source_target_pairs={{0,8},{8,16},{16,24},{24,0},{1,9},{9,17},{17,25},{25,1},{2,10},{10... | collective-permute-start | bytes 393224 | tf_op jit(solution)/shard_map/ppermute | solution.py:24
  49.0 9.7 %collective-permute-start.20 = (bf16[64,1024]{1,0:T(8,128)(2,1)S(1)}, bf16[64,1024]{1,0:T(8,128)(2,1)S(1)}, u32[]{:S(2)}, u32[]{:S(2)}) collective-permute-start(bf16[64,1024]{1,0:T(8,128)(2,1)S(1)} %shard_map.79), channel_id=1, source_target_pairs={{0,8},{8,16},{16,24},{24,0},{1,9},{9,17},{17,25},{25,1},{2,10},{10... | collective-permute-start | bytes 393224 | tf_op jit(solution)/shard_map/ppermute | solution.py:24
  51.8 7.1 %collective-permute-start.23 = (bf16[64,1024]{1,0:T(8,128)(2,1)S(1)}, bf16[64,1024]{1,0:T(8,128)(2,1)S(1)}, u32[]{:S(2)}, u32[]{:S(2)}) collective-permute-start(bf16[64,1024]{1,0:T(8,128)(2,1)S(1)} %shard_map.80), channel_id=1, source_target_pairs={{0,8},{8,16},{16,24},{24,0},{1,9},{9,17},{17,25},{25,1},{2,10},{10... | collective-permute-start | bytes 393224 | tf_op jit(solution)/shard_map/ppermute | solution.py:24
  54.6 7.1 %collective-permute-start.26 = (bf16[64,1024]{1,0:T(8,128)(2,1)S(1)}, bf16[64,1024]{1,0:T(8,128)(2,1)S(1)}, u32[]{:S(2)}, u32[]{:S(2)}) collective-permute-start(bf16[64,1024]{1,0:T(8,128)(2,1)S(1)} %shard_map.81), channel_id=1, source_target_pairs={{0,8},{8,16},{16,24},{24,0},{1,9},{9,17},{17,25},{25,1},{2,10},{10... | collective-permute-start | bytes 393224 | tf_op jit(solution)/shard_map/ppermute | solution.py:24
  57.0 7.3 %collective-permute-start.29 = (bf16[64,1024]{1,0:T(8,128)(2,1)S(1)}, bf16[64,1024]{1,0:T(8,128)(2,1)S(1)}, u32[]{:S(2)}, u32[]{:S(2)}) collective-permute-start(bf16[64,1024]{1,0:T(8,128)(2,1)S(1)} %shard_map.82), channel_id=1, source_target_pairs={{0,8},{8,16},{16,24},{24,0},{1,9},{9,17},{17,25},{25,1},{2,10},{10... | collective-permute-start | bytes 393224 | tf_op jit(solution)/shard_map/ppermute | solution.py:24
  61.7 2.5 %copy-start = (bf16[1,64,5120]{2,1,0:T(8,128)(2,1)}, bf16[1,64,5120]{2,1,0:T(8,128)(2,1)S(1)}, u32[]{:S(2)}) copy-start(bf16[1,64,5120]{2,1,0:T(8,128)(2,1)S(1)} %bitcast_dynamic-update-slice_fusion.1) | copy-start | bytes 1966084
